TPU v7x, 512 devices: a whole 4x8x8 slice. The times are simulated.
512 devices in a mesh: sample: 32 (over x_lo, y, core), head: 16 (over z, x_hi).
Axes of the slice: x: 4 (x_hi: 2, x_lo: 2; x = x_hi * 2 + x_lo), y: 8, z: 8, core: 2. Of those that a mesh axis runs over, the one named last changes fastest.
Arguments:
- q_nope: bfloat16 [4096, 8192], P('sample', 'head'), may hold values from -6 to 6
- q_rope: bfloat16 [4096, 4096], P('sample', 'head'), may hold values from -12 to 12
- resp_latent: bfloat16 [4096, 512], P('sample'), may hold values from -6 to 6
- resp_rope_t: bfloat16 [64, 4096], P(None, 'sample'), may hold values from -6 to 6
- prompt_latent: bfloat16 [512, 512], P('sample'), may hold values from -6 to 6
- prompt_rope_t: bfloat16 [64, 512], P(None, 'sample'), may hold values from -4 to 4
- w_key_up: bfloat16 [512, 8192], P(None, 'head'), may hold values from -0.5 to 0.5
- w_value_up: bfloat16 [512, 8192], P(None, 'head'), may hold values from -0.25 to 0.25
- grad_out: bfloat16 [4096, 8192], P('sample', 'head'), may hold values from -6 to 6
- lengths: int32 [32], P('sample'), may hold values from 1 to 128, as said below
Outputs:
- d_q_nope: bfloat16 [4096, 8192], P('sample', 'head')
- d_q_rope: bfloat16 [4096, 4096], P('sample', 'head')
- d_key_up: float32 [512, 8192], P('sample', 'head')
- d_value_up: float32 [512, 8192], P('sample', 'head')
- d_prompt_latent: float32 [512, 512], P('sample')
- d_prompt_rope_t: float32 [64, 512], P(None, 'sample')
- d_resp_latent: float32 [4096, 512], P('sample')
- d_resp_rope_t: float32 [64, 4096], P(None, 'sample')
Inputs may be any that keep to these rules, and one draw needn't show every extreme that they name: `lengths`: some rollout has length exactly 128.
All inputs are finite; a program needn't handle non-finite values.
Results may differ from a plain program's by a relative error of at most 0.03.
Values may be sent and summed in bfloat16 or wider, within the bound.
No kernel may reach another device: no remote copies, remote signals or barrier semaphores. Data moves between devices by JAX's collectives and lax.ppermute only.
A program may use at most 64 MiB of HBM per device.

v0:
```python
import jax
import jax.numpy as jnp
from jax import lax
from jax.sharding import PartitionSpec as P

DR = 64
DN = 128
DV = 128


def local_grads(
    query_nope, query_rope, keys_latent, keys_rope, length, grad_rows, w_key_up, w_value_up
):
    wide = jnp.float32
    token_rows = query_nope.shape[0]
    head_count = w_key_up.shape[1] // DN
    latent_dim = w_key_up.shape[0]
    prompt_rows = keys_latent.shape[0] - token_rows
    softmax_scale = (DN + DR) ** (-0.5)
    position = jnp.arange(token_rows, dtype=jnp.int32)
    key_index = jnp.arange(keys_latent.shape[0], dtype=jnp.int32) - prompt_rows
    allowed = (key_index[None, :] < 0) | (key_index[None, :] <= position[:, None]) & (
        key_index[None, :] < length
    )
    live = position < length
    masked_grad = jnp.where(live[:, None], grad_rows, jnp.zeros_like(grad_rows))
    nope_heads = query_nope.reshape(token_rows, head_count, DN)
    rope_heads = query_rope.reshape(token_rows, head_count, DR)
    grad_heads = masked_grad.reshape(token_rows, head_count, DV)
    key_up = w_key_up.reshape(latent_dim, head_count, DN)
    value_up = w_value_up.reshape(latent_dim, head_count, DV)
    q_latent = jnp.einsum("thn,chn->htc", nope_heads, key_up, preferred_element_type=wide).astype(
        jnp.bfloat16
    )
    scores = jnp.einsum("htc,kc->htk", q_latent, keys_latent, preferred_element_type=wide)
    scores = scores + jnp.einsum("thr,rk->htk", rope_heads, keys_rope, preferred_element_type=wide)
    scores = jnp.where(allowed[None], softmax_scale * scores, jnp.float32(-1e30))
    highest = jnp.max(scores, axis=-1, keepdims=True)
    exponent = jnp.exp(scores - highest)
    attention = exponent / jnp.sum(exponent, axis=-1, keepdims=True)
    attention_b = attention.astype(jnp.bfloat16)
    out_latent = jnp.einsum(
        "htk,kc->htc", attention_b, keys_latent, preferred_element_type=wide
    ).astype(jnp.bfloat16)
    d_out_latent = jnp.einsum(
        "thv,chv->htc", grad_heads, value_up, preferred_element_type=wide
    ).astype(jnp.bfloat16)
    d_attention = jnp.einsum("htc,kc->htk", d_out_latent, keys_latent, preferred_element_type=wide)
    row_delta = jnp.sum(attention * d_attention, axis=-1, keepdims=True)
    d_scores = (softmax_scale * attention * (d_attention - row_delta)).astype(jnp.bfloat16)
    d_q_latent = jnp.einsum(
        "htk,kc->htc", d_scores, keys_latent, preferred_element_type=wide
    ).astype(jnp.bfloat16)
    d_q_rope = (
        jnp.einsum("htk,rk->thr", d_scores, keys_rope, preferred_element_type=wide)
        .astype(jnp.bfloat16)
        .reshape(token_rows, head_count * DR)
    )
    d_q_nope = (
        jnp.einsum("htc,chn->thn", d_q_latent, key_up, preferred_element_type=wide)
        .astype(jnp.bfloat16)
        .reshape(token_rows, head_count * DN)
    )
    key_latent_grad = jnp.einsum("htk,htc->kc", d_scores, q_latent, preferred_element_type=wide)
    key_latent_grad = key_latent_grad + jnp.einsum(
        "htk,htc->kc", attention_b, d_out_latent, preferred_element_type=wide
    )
    key_rope_grad = jnp.einsum("htk,thr->rk", d_scores, rope_heads, preferred_element_type=wide)
    factors = (d_q_latent, nope_heads, out_latent, grad_heads)
    return (d_q_nope, d_q_rope, key_latent_grad, key_rope_grad, factors)


def weight_terms(factors, count):
    d_q_latent, nope_heads, out_latent, grad_heads = factors
    head_count = nope_heads.shape[1]
    key_part = jnp.einsum(
        "htc,thn->chn", d_q_latent, nope_heads, preferred_element_type=jnp.float32
    ).reshape(count, head_count * DN)
    value_part = jnp.einsum(
        "htc,thv->chv", out_latent, grad_heads, preferred_element_type=jnp.float32
    ).reshape(count, head_count * DV)
    return jnp.concatenate([key_part, value_part], axis=1)


def body(
    q_nope,
    q_rope,
    resp_latent,
    resp_rope_t,
    prompt_latent,
    prompt_rope_t,
    w_key_up,
    w_value_up,
    grad_out,
    lengths,
):
    all_latent, all_rope = (
        lax.all_gather(prompt_latent, "sample", axis=0, tiled=True),
        lax.all_gather(prompt_rope_t, "sample", axis=1, tiled=True),
    )
    prompt_rows = all_latent.shape[0]
    page_rows = prompt_latent.shape[0]
    latent_dim = w_key_up.shape[0]
    key_width = w_key_up.shape[1]
    keys_latent = jnp.concatenate([all_latent, resp_latent], axis=0)
    keys_rope = jnp.concatenate([all_rope, resp_rope_t], axis=1)
    d_q_nope, d_q_rope, key_latent_grad, key_rope_grad, factors = local_grads(
        q_nope, q_rope, keys_latent, keys_rope, lengths[0], grad_out, w_key_up, w_value_up
    )
    weight_sum = lax.psum_scatter(
        weight_terms(factors, latent_dim).astype(jnp.bfloat16),
        "sample",
        scatter_dimension=0,
        tiled=True,
    ).astype(jnp.float32)
    d_key_up = weight_sum[:, :key_width]
    d_value_up = weight_sum[:, key_width:]
    prompt_lat_part = key_latent_grad[:prompt_rows]
    prompt_rope_part = key_rope_grad[:, :prompt_rows]
    resp_lat_part = key_latent_grad[prompt_rows:]
    resp_rope_part = key_rope_grad[:, prompt_rows:]
    prompt_lat_sum, prompt_rope_sum = lax.psum(
        (prompt_lat_part, prompt_rope_part), ("sample", "head")
    )
    owner_start = lax.axis_index("sample") * page_rows
    d_prompt_latent = lax.dynamic_slice_in_dim(prompt_lat_sum, owner_start, page_rows, 0)
    d_prompt_rope_t = lax.dynamic_slice_in_dim(prompt_rope_sum, owner_start, page_rows, 1)
    d_resp_latent, d_resp_rope_t = (
        lax.psum(resp_lat_part.astype(jnp.bfloat16), "head").astype(jnp.float32),
        lax.psum(resp_rope_part.astype(jnp.bfloat16), "head").astype(jnp.float32),
    )
    return (
        d_q_nope,
        d_q_rope,
        d_key_up,
        d_value_up,
        d_prompt_latent,
        d_prompt_rope_t,
        d_resp_latent,
        d_resp_rope_t,
    )


def solution(mesh):
    return jax.shard_map(
        body,
        mesh=mesh,
        in_specs=(
            P("sample", "head"),
            P("sample", "head"),
            P("sample", None),
            P(None, "sample"),
            P("sample", None),
            P(None, "sample"),
            P(None, "head"),
            P(None, "head"),
            P("sample", "head"),
            P("sample"),
        ),
        out_specs=(
            P("sample", "head"),
            P("sample", "head"),
            P("sample", "head"),
            P("sample", "head"),
            P("sample", None),
            P(None, "sample"),
            P("sample", None),
            P(None, "sample"),
        ),
        check_vma=False,
    )
```

profile of v0, /device:TPU:16, one launch (start us, length us, event | category | flops | bytes accessed | tf_op | source)
XLA Modules:
  0.0 547.2 jit_solution(6527101862433534105)
XLA Ops:
  8.8 1.6 copy.56
  10.4 1.0 broadcast_select_fusion
  12.2 1.0 copy.73
  13.2 33.2 %all_gather.7 = bf16[64,512]{0,1:T(8,128)(2,1)S(1)} all-gather(bf16[64,16]{0,1:T(8,128)(2,1)} %param.15), channel_id=1, replica_groups=mesh['sample'=32,'head'=16] {'sample'}, dimensions={1}, use_global_device_ids=true | all-gather | bytes 67584 | tf_op jit(solution)/shard_map/all_gather | solution.py:99
  47.1 34.0 %all_gather.6 = bf16[512,512]{1,0:T(8,128)(2,1)S(1)} all-gather(bf16[16,512]{1,0:T(8,128)(2,1)} %param.14), channel_id=1, replica_groups=mesh['sample'=32,'head'=16] {'sample'}, dimensions={0}, use_global_device_ids=true | all-gather | bytes 540672 | tf_op jit(solution)/shard_map/all_gather | solution.py:98
  83.0 1.9 fusion.21
  84.9 1.1 convolution_convert_fusion.4
  86.1 3.4 convolution_bitcast_fusion
  89.5 2.2 multiply_reduce_fusion
  92.1 1.0 copy-done.6
  93.6 1.1 copy-done.2
  95.4 2.3 slice.28
  97.7 1.1 convolution_bitcast_fusion.3
  100.2 3.0 convolution_convert_fusion.1
  103.3 2.0 copy.64
  105.3 1.5 convolution_convert_fusion.3
  107.1 1.0 copy.63
  108.1 2.2 pad_maximum_fusion
  113.2 80.3 %psum.31 = bf16[64,128]{1,0:T(8,128)(2,1)S(1)} all-reduce(bf16[64,128]{1,0:T(8,128)(2,1)S(1)} %slice.35), channel_id=1, replica_groups=mesh['sample'=32,'head'=16] {'head'}, use_global_device_ids=true, to_apply=%region_7.8 | all-reduce | flops 8192 | bytes 32768 | tf_op jit(solution)/shard_map/psum | solution.py:130
  194.2 63.9 %all-reduce.4.cloned.1.call-done = bf16[128,512]{1,0:T(8,128)(2,1)} async-done(((bf16[128,512]{1,0:T(8,128)(2,1)}), bf16[128,512]{1,0:T(8,128)(2,1)}) %all-reduce.4.cloned.1.call-update) | async-done | bytes 131088 | tf_op jit(solution)/shard_map/psum | solution.py:129
  258.1 1.6 convert_element_type.53
  259.8 275.8 %all-reduce.6.cloned.1.call-done = (f32[512,512]{1,0:T(8,128)}, f32[64,512]{1,0:T(8,128)}) async-done(((f32[512,512]{1,0:T(8,128)}, f32[64,512]{1,0:T(8,128)}), (f32[512,512]{1,0:T(8,128)}, f32[64,512]{1,0:T(8,128)})) %all-reduce.6.cloned.1.call-update) | async-done | bytes 1179664 | tf_op jit(solution)/shard_map/psum | solution.py:122
  537.0 1.4 constant_dynamic-slice_fusion.1
  538.4 1.4 fusion.20
  (66 shorter events, 11.6 us)
Async XLA Ops:
  8.0 76.9 %copy-start = (bf16[512,512]{1,0:T(8,128)(2,1)S(1)}, bf16[512,512]{1,0:T(8,128)(2,1)}, u32[]{:S(2)}) copy-start(bf16[512,512]{1,0:T(8,128)(2,1)} %param.17) | copy-start | bytes 1572868
  8.0 73.1 %copy-start.14 = (bf16[512,512]{1,0:T(8,128)(2,1)S(1)}, bf16[512,512]{1,0:T(8,128)(2,1)}, u32[]{:S(2)}) copy-start(bf16[512,512]{1,0:T(8,128)(2,1)} %param.16) | copy-start | bytes 1572868
  8.0 250.1 %all-reduce.4.cloned.1.call-start = ((), (), s32[]{:S(2)}) async-start(), calls=%async_computation.2 | async-start | bytes 262144 | tf_op jit(solution)/shard_map/psum | solution.py:129
  13.2 68.5 %copy-start.7 = (bf16[128,512]{0,1:T(8,128)(2,1)}, bf16[128,512]{0,1:T(8,128)(2,1)S(1)}, u32[]{:S(2)}) copy-start(bf16[128,512]{0,1:T(8,128)(2,1)S(1)} %copy.73) | copy-start | bytes 393220
  47.1 34.7 %copy-start.15 = (bf16[128,512]{1,0:T(8,128)(2,1)S(1)}, bf16[128,512]{1,0:T(8,128)(2,1)}, u32[]{:S(2)}) copy-start(bf16[128,512]{1,0:T(8,128)(2,1)} %param.12) | copy-start | bytes 393220
  81.1 8.4 %copy-start.3 = (bf16[512,512]{1,0:T(8,128)(2,1)}, bf16[512,512]{1,0:T(8,128)(2,1)S(1)}, u32[]{:S(2)}) copy-start(bf16[512,512]{1,0:T(8,128)(2,1)S(1)} %all_gather.6) | copy-start | bytes 1572868
  81.7 0.8 copy-start.10
  81.7 0.9 copy-start.12
  81.7 0.9 copy-start.17
  83.0 1.9 copy-start.13
  86.1 3.4 copy-start.16
  89.5 2.2 copy-start.1
  89.5 2.3 copy-start.18
  91.8 1.3 copy-start.6
  93.6 1.1 copy-start.2
  95.4 440.2 %all-reduce.6.cloned.1.call-start = ((), (), s32[]{:S(2)}) async-start(), calls=%async_computation.3 | async-start | bytes 2359296 | tf_op jit(solution)/shard_map/psum | solution.py:122
  97.7 2.5 copy-start.4
  98.8 0.7 copy-start.9
  100.2 438.2 %reduce-scatter.2.cloned.1.call-start = ((), (), s32[]{:S(2)}) async-start(), calls=%async_computation.1 | async-start | bytes 1081344 | tf_op jit(solution)/shard_map/reduce_scatter | solution.py:110
  105.3 1.5 copy-start.8
  106.8 1.3 copy-start.5
  110.3 1.9 copy-start.11
Sparse Core Ops, SparseCore 0:
  95.5 162.5 all-reduce.3
  263.4 272.1 all-reduce.5
Sparse Core Ops, SparseCore 1:
  110.4 113.8 reduce-scatter.1
where the time goes:
time: 549 us; the launch traced here: 547 us
  waiting for transfers between devices  340 us (62%)
  blocking collectives  148 us (27%)
  local copies, waits for them, and re-layouts  20.3 us (4%)
  between operations  16.5 us (3%)
  matrix products  15.2 us (3%)
  other arithmetic  7.71 us (1%)
    psum x1, waiting for transfers between devices, body(): lax.psum((prompt_lat_part, prompt_rope_part), ('sample', 'head'))  276 us
    psum x1, blocking collectives, body(): lax.psum(resp_rope_part.astype(jnp.bfloat16), 'head').astype(jnp.float32)  80.3 us
    psum x1, waiting for transfers between devices, body(): lax.psum(resp_lat_part.astype(jnp.bfloat16), 'head').astype(jnp.float32)  63.9 us
    all_gather x1, blocking collectives, body(): lax.all_gather(prompt_latent, 'sample', axis=0, tiled=True)  34 us
    all_gather x1, blocking collectives, body(): lax.all_gather(prompt_rope_t, 'sample', axis=1, tiled=True)  33.2 us
  transfers between devices with their start and end apart: 3, of which 2 were waited for; matrix products, arithmetic and copies ran while one was open for 4% of the time, Pallas kernels for 0%

commit v1 on v0

v1 whole, which is shorter than its diff:
```python
import jax
import jax.numpy as jnp
from jax import lax
from jax.experimental import pallas as pl
from jax.experimental.pallas import tpu as pltpu
from jax.sharding import Mesh, PartitionSpec as P

DC = 512
DR = 64
DN = 128
DV = 128
RESP = 128
PAGE = 16
LOCAL = 4
ROWS = LOCAL * RESP
EXT = 640
CHIPS = 16
HALF = CHIPS * PAGE
KEYS = 2 * HALF + RESP
WIDE = 2 * LOCAL * DN + EXT
SCALE = (DN + DR) ** (-0.5)
F32 = jnp.float32
BF16 = jnp.bfloat16
SAMPLE = ("xl", "y", "c")
HEAD = ("z", "xh")
PARAMS = pltpu.CompilerParams(vmem_limit_bytes=40 * 1024 * 1024)


def dot(a, b, ca, cb):
    return lax.dot_general(a, b, (((ca,), (cb,)), ((), ())), preferred_element_type=F32)


def columns(part, width):
    return slice(part * width, (part + 1) * width)


def with_rope(latent, rope_t):
    rope = jnp.transpose(rope_t.astype(F32))
    pad = jnp.zeros((latent.shape[0], EXT - DC - DR), F32)
    return jnp.concatenate([latent.astype(F32), rope, pad], axis=1).astype(BF16)


def pages_kernel(latent, rope_t, out):
    page = with_rope(latent[...], rope_t[...])
    for k in range(CHIPS):
        out[k] = page


def main_kernel(
    where,
    q_nope,
    q_rope,
    grad,
    w_key,
    w_value,
    own,
    other,
    resp_latent,
    resp_rope_t,
    d_q_nope,
    d_q_rope,
    send_resp,
    keep,
    send,
    keys,
    query,
    d_out,
    weight,
    prompt,
):
    length = where[0]
    core = where[1]
    keys[0:HALF, :] = own[...].reshape(HALF, EXT)
    keys[HALF : 2 * HALF, :] = other[...].reshape(HALF, EXT)
    keys[2 * HALF : KEYS, :] = with_rope(resp_latent[...], resp_rope_t[...])
    live = lax.broadcasted_iota(jnp.int32, (RESP, LOCAL * DV), 0) < length
    masked = jnp.where(live, grad[...].astype(F32), 0.0).astype(BF16)
    rope_pad = jnp.zeros((RESP, EXT - DC - DR), BF16)
    for h in range(LOCAL):
        rows = columns(h, RESP)
        query[rows, 0:DC] = dot(q_nope[:, columns(h, DN)], w_key[:, columns(h, DN)], 1, 1).astype(
            BF16
        )
        query[rows, DC:EXT] = jnp.concatenate([q_rope[:, columns(h, DR)], rope_pad], axis=1)
        d_out[rows, :] = dot(masked[:, columns(h, DV)], w_value[:, columns(h, DV)], 1, 1).astype(
            BF16
        )
    key_rows = keys[...]
    key_latent = keys[:, 0:DC]
    scores = dot(key_rows, query[...], 1, 1) * SCALE
    token = lax.broadcasted_iota(jnp.int32, (RESP, ROWS), 1) % RESP
    key_at = lax.broadcasted_iota(jnp.int32, (RESP, ROWS), 0)
    allowed = (key_at <= token) & (key_at < length)
    scores = jnp.concatenate(
        [scores[0 : 2 * HALF], jnp.where(allowed, scores[2 * HALF : KEYS], -1e30)], axis=0
    )
    highest = jnp.max(scores, axis=0, keepdims=True)
    exponent = jnp.exp(scores - highest)
    attention = exponent * (1.0 / jnp.sum(exponent, axis=0, keepdims=True))
    attention_b = attention.astype(BF16)
    d_attention = dot(key_latent, d_out[...], 1, 1)
    row_delta = jnp.sum(attention * d_attention, axis=0, keepdims=True)
    d_scores = (SCALE * attention * (d_attention - row_delta)).astype(BF16)
    key_grad = dot(d_scores, query[...], 1, 0)
    key_grad_v = dot(attention_b, d_out[...], 1, 0)
    prompt[:, 0:DC] = (key_grad[:, 0:DC] + key_grad_v).astype(BF16)
    prompt[:, DC:EXT] = key_grad[:, DC:EXT].astype(BF16)
    for g in range(CHIPS):
        at = 2 * HALF + g * 8
        send_resp[g, :, 0:DC] = (key_grad[at : at + 8, 0:DC] + key_grad_v[at : at + 8]).astype(
            BF16
        )
        send_resp[g, :, DC:EXT] = key_grad[at : at + 8, DC:EXT].astype(BF16)
    d_query = dot(key_rows, d_scores, 0, 0).astype(BF16)
    out_latent = dot(key_latent, attention_b, 0, 0).astype(BF16)
    for h in range(LOCAL):
        d_q = d_query[0:DC, columns(h, RESP)]
        d_q_nope[:, columns(h, DN)] = dot(d_q, w_key[:, columns(h, DN)], 0, 0).astype(BF16)
        weight[:, columns(h, DN)] = dot(d_q, q_nope[:, columns(h, DN)], 1, 0).astype(BF16)
        weight[:, columns(LOCAL + h, DN)] = dot(
            out_latent[:, columns(h, RESP)], masked[:, columns(h, DV)], 1, 0
        ).astype(BF16)
    d_rope = jnp.concatenate(
        [
            jnp.transpose(d_query[DC : DC + DR, columns(h, RESP)].astype(F32)) for h in range(LOCAL)
        ],
        axis=1,
    )
    d_q_rope[...] = d_rope.astype(BF16)
    width = 2 * LOCAL * DN
    for k in range(CHIPS):
        mine = pl.ds(pl.multiple_of((2 * k + core) * PAGE, PAGE), PAGE)
        theirs = pl.ds(pl.multiple_of((2 * k + 1 - core) * PAGE, PAGE), PAGE)
        keep[k, :, 0:width] = weight[mine, :]
        send[k, :, 0:width] = weight[theirs, :]
        keep[k, :, width:WIDE] = prompt[k * PAGE : (k + 1) * PAGE, :]
        send[k, :, width:WIDE] = prompt[HALF + k * PAGE : HALF + (k + 1) * PAGE, :]


def middle_kernel(sample_parts, head_parts, d_key_up, d_value_up, out):
    total = sample_parts[0].astype(F32)
    for k in range(1, CHIPS):
        total = total + sample_parts[k].astype(F32)
    d_key_up[...] = total[:, 0 : LOCAL * DN]
    d_value_up[...] = total[:, LOCAL * DN : 2 * LOCAL * DN]
    page = total[:, 2 * LOCAL * DN : WIDE]
    rows = head_parts[0].astype(F32)
    for g in range(1, CHIPS):
        rows = rows + head_parts[g].astype(F32)
    line = jnp.concatenate([rows, page[0:8], page[8:16]], axis=1).astype(BF16)
    for g in range(CHIPS):
        out[g] = line


def last_kernel(parts, d_prompt, d_prompt_rope_t, d_resp, d_resp_rope_t):
    total = parts[0, :, EXT : 3 * EXT].astype(F32)
    for g in range(1, CHIPS):
        total = total + parts[g, :, EXT : 3 * EXT].astype(F32)
    page = jnp.concatenate([total[:, 0:EXT], total[:, EXT : 2 * EXT]], axis=0)
    d_prompt[...] = page[:, 0:DC]
    d_prompt_rope_t[...] = jnp.transpose(page[:, DC:EXT])[0:DR]
    rows = jnp.concatenate([parts[g, :, 0:EXT].astype(F32) for g in range(CHIPS)], axis=0)
    d_resp[...] = rows[:, 0:DC]
    d_resp_rope_t[...] = jnp.transpose(rows[:, DC:EXT])[0:DR]


def call(kernel, outs, *args, scratch=(), scalars=0):
    vmem = pl.BlockSpec(memory_space=pltpu.VMEM)
    smem = pl.BlockSpec(memory_space=pltpu.SMEM)
    return pl.pallas_call(
        kernel,
        out_shape=[jax.ShapeDtypeStruct(shape, kind) for shape, kind in outs],
        in_specs=[smem] * scalars + [vmem] * (len(args) - scalars),
        out_specs=[vmem] * len(outs),
        scratch_shapes=list(scratch),
        compiler_params=PARAMS,
    )(*args)


def spread(parts, axes):
    return lax.all_to_all(parts, axes, 0, 0, tiled=True)


def body(
    q_nope,
    q_rope,
    resp_latent,
    resp_rope_t,
    prompt_latent,
    prompt_rope_t,
    w_key_up,
    w_value_up,
    grad_out,
    lengths,
):
    swap = [(0, 1), (1, 0)]
    (pages,) = call(pages_kernel, [((CHIPS, PAGE, EXT), BF16)], prompt_latent, prompt_rope_t)
    own = spread(pages, ("xl", "y"))
    other = lax.ppermute(own, "c", swap)
    where = jnp.stack([lengths[0], lax.axis_index("c").astype(jnp.int32)])
    d_q_nope, d_q_rope, send_resp, keep, send = call(
        main_kernel,
        [
            ((RESP, LOCAL * DN), BF16),
            ((RESP, LOCAL * DR), BF16),
            ((CHIPS, 8, EXT), BF16),
            ((CHIPS, PAGE, WIDE), BF16),
            ((CHIPS, PAGE, WIDE), BF16),
        ],
        where,
        q_nope,
        q_rope,
        grad_out,
        w_key_up,
        w_value_up,
        own,
        other,
        resp_latent,
        resp_rope_t,
        scalars=1,
        scratch=[
            pltpu.VMEM((KEYS, EXT), BF16),
            pltpu.VMEM((ROWS, EXT), BF16),
            pltpu.VMEM((ROWS, DC), BF16),
            pltpu.VMEM((DC, 2 * LOCAL * DN), BF16),
            pltpu.VMEM((KEYS, EXT), BF16),
        ],
    )
    chip_sum = keep + lax.ppermute(send, "c", swap)
    head_parts = spread(send_resp, HEAD)
    sample_parts = spread(chip_sum, ("xl", "y"))
    d_key_up, d_value_up, line = call(
        middle_kernel,
        [
            ((PAGE, LOCAL * DN), F32),
            ((PAGE, LOCAL * DV), F32),
            ((CHIPS, 8, 3 * EXT), BF16),
        ],
        sample_parts,
        head_parts,
    )
    lines = spread(line, HEAD)
    d_prompt, d_prompt_rope_t, d_resp, d_resp_rope_t = call(
        last_kernel,
        [
            ((PAGE, DC), F32),
            ((DR, PAGE), F32),
            ((RESP, DC), F32),
            ((DR, RESP), F32),
        ],
        lines,
    )
    return (
        d_q_nope,
        d_q_rope,
        d_key_up,
        d_value_up,
        d_prompt,
        d_prompt_rope_t,
        d_resp,
        d_resp_rope_t,
    )


def solution(mesh):
    fine = Mesh(mesh.devices.reshape(2, 8, 2, 8, 2), SAMPLE + HEAD)
    return jax.shard_map(
        body,
        mesh=fine,
        in_specs=(
            P(SAMPLE, HEAD),
            P(SAMPLE, HEAD),
            P(SAMPLE, None),
            P(None, SAMPLE),
            P(SAMPLE, None),
            P(None, SAMPLE),
            P(None, HEAD),
            P(None, HEAD),
            P(SAMPLE, HEAD),
            P(SAMPLE),
        ),
        out_specs=(
            P(SAMPLE, HEAD),
            P(SAMPLE, HEAD),
            P(SAMPLE, HEAD),
            P(SAMPLE, HEAD),
            P(SAMPLE, None),
            P(None, SAMPLE),
            P(SAMPLE, None),
            P(None, SAMPLE),
        ),
        check_vma=False,
    )
```

time: 549 us -> 110 us (0.20)
  the two profiles are of different devices: /device:TPU:16 before, /device:TPU:8 now
where the time goes in v1:
time: 110 us
  blocking collectives  65.2 us (59%)
  starting transfers between devices  16.6 us (15%)
  waiting for transfers between devices  10.8 us (10%)
  local copies, waits for them, and re-layouts  7.43 us (7%)
  Pallas kernels  6.77 us (6%)
  other arithmetic  1.43 us (1%)
  between operations  1.36 us (1%)
    all_to_all x3, blocking collectives, spread(): return lax.all_to_all(parts, axes, 0, 0, tiled=True)  65.2 us
    all_to_all x1, starting transfers between devices, spread(): return lax.all_to_all(parts, axes, 0, 0, tiled=True)  12.6 us
    all_to_all x1, waiting for transfers between devices, spread(): return lax.all_to_all(parts, axes, 0, 0, tiled=True)  9.9 us
    unnamed x20, local copies, waits for them, and re-layouts  7.43 us
    pallas_call x4, Pallas kernels, call(): pl.pallas_call(kernel, out_shape=[jax.ShapeDtypeStruct(shape, kind) for s...  6.77 us
  transfers between devices with their start and end apart: 3, of which 2 were waited for; matrix products, arithmetic and copies ran while one was open for 1% of the time, Pallas kernels for 0%

profile of v1, /device:TPU:8, one launch (start us, length us, event | category | flops | bytes accessed | tf_op | source)
XLA Modules:
  0.0 109.5 jit_solution(9155145238404477277)
XLA Ops:
  0.7 0.9 copy.18.rope_t
  1.5 0.7 copy-done.7
  2.2 0.1 shard_map.161
  2.3 19.4 %all_to_all.20.own = bf16[16,16,640]{2,1,0:T(8,128)(2,1)S(1)} all-to-all(bf16[16,16,640]{2,1,0:T(8,128)(2,1)S(1)} %shard_map.161), channel_id=1, replica_groups=mesh['xl'=2,'y'=8,'c'=2,'z'=8,'xh'=2] {'xl','y'}, dimensions={0} | all-to-all | bytes 655360 | tf_op jit(solution)/shard_map/all_to_all | solution.py:181
  21.8 1.9 %collective-permute-start = (bf16[16,16,640]{2,1,0:T(8,128)(2,1)S(1)}, bf16[16,16,640]{2,1,0:T(8,128)(2,1)S(1)}, u32[]{:S(2)}, u32[]{:S(2)}) collective-permute-start(bf16[16,16,640]{2,1,0:T(8,128)(2,1)S(1)} %all_to_all.20.own), channel_id=1, source_target_pairs={{0,16},{16,0},{1,17},{17,1},{2,18},{18,2},{3,19},{19,3},{4,20},{20... | collective-permute-start | bytes 983048 | tf_op jit(solution)/shard_map/ppermute | solution.py:199
  24.3 0.1 pad_add_fusion.where
  24.4 0.9 collective-permute-done.other
  25.3 0.9 copy-done.2
  26.2 0.9 copy-done.3
  27.1 0.9 copy-done.4
  28.0 0.8 copy-done.5
  28.8 0.7 copy-done.6
  29.6 5.2 %shard_map.162 = (bf16[128,512]{1,0:T(8,128)(2,1)}, bf16[128,256]{1,0:T(8,128)(2,1)}, bf16[16,8,640]{2,1,0:T(8,128)(2,1)}, bf16[16,16,1664]{2,1,0:T(8,128)(2,1)S(1)}, bf16[16,16,1664]{2,1,0:T(8,128)(2,1)S(1)}) custom-call(s32[2]{0:T(128)S(1)} %pad_add_fusion.where, bf16[128,512]{1,0:T(8,128)(2,1)S(1)} %copy-done.2, bf16[128,256]{1,0:T(8,128)(2,1)S(1)} %copy-done.5, ...), custom_call_target="tpu_custom_call" | custom-call | tf_op jit(solution)/shard_map/pallas_call | solution.py:170
  34.8 2.0 %collective-permute-start.1 = (bf16[16,16,1664]{2,1,0:T(8,128)(2,1)S(1)}, bf16[16,16,1664]{2,1,0:T(8,128)(2,1)S(1)}, u32[]{:S(2)}, u32[]{:S(2)}) collective-permute-start(bf16[16,16,1664]{2,1,0:T(8,128)(2,1)S(1)} %get-tuple-element.23), channel_id=1, source_target_pairs={{0,16},{16,0},{1,17},{17,1},{2,18},{18,2},{3,19},{19,3},{4,20},{20... | collective-permute-start | bytes 2555912 | tf_op jit(solution)/shard_map/ppermute | solution.py:229
  36.8 12.6 %all-to-all-start.2 = ((bf16[16,8,640]{2,1,0:T(8,128)(2,1)}), bf16[16,8,640]{2,1,0:T(8,128)(2,1)S(1)}, u32[]{:S(2)}, u32[]{:S(2)}) async-start(bf16[16,8,640]{2,1,0:T(8,128)(2,1)} %get-tuple-element.24), calls=%async_computation.2 | async-start | bytes 327680 | tf_op jit(solution)/shard_map/all_to_all | solution.py:181
  49.5 0.0 collective-permute-done.1
  49.5 0.9 copy-done.8
  50.4 1.4 %add.3 = bf16[16,16,1664]{2,1,0:T(8,128)(2,1)S(1)} add(bf16[16,16,1664]{2,1,0:T(8,128)(2,1)S(1)} %get-tuple-element.22, bf16[16,16,1664]{2,1,0:T(8,128)(2,1)} %copy-done.8) | non-fusion elementwise | flops 425984 | bytes 2555904 | tf_op jit(solution)/shard_map/add | solution.py:229
  51.8 9.9 %all-to-all-done.2.head_parts = bf16[16,8,640]{2,1,0:T(8,128)(2,1)S(1)} async-done(((bf16[16,8,640]{2,1,0:T(8,128)(2,1)}), bf16[16,8,640]{2,1,0:T(8,128)(2,1)S(1)}, u32[]{:S(2)}, u32[]{:S(2)}) %all-to-all-start.2) | async-done | bytes 163872 | tf_op jit(solution)/shard_map/all_to_all | solution.py:181
  61.7 25.9 %all_to_all.21.sample_parts = bf16[16,16,1664]{2,1,0:T(8,128)(2,1)S(1)} all-to-all(bf16[16,16,1664]{2,1,0:T(8,128)(2,1)S(1)} %add.3), channel_id=1, replica_groups=mesh['xl'=2,'y'=8,'c'=2,'z'=8,'xh'=2] {'xl','y'}, dimensions={0} | all-to-all | bytes 1703936 | tf_op jit(solution)/shard_map/all_to_all | solution.py:181
  87.6 0.7 shard_map.163
  88.3 19.8 %all_to_all.22.parts = bf16[16,8,1920]{2,1,0:T(8,128)(2,1)S(1)} all-to-all(bf16[16,8,1920]{2,1,0:T(8,128)(2,1)S(1)} %get-tuple-element.27), channel_id=1, replica_groups=mesh['xl'=2,'y'=8,'c'=2,'z'=8,'xh'=2] {'z','xh'}, dimensions={0} | all-to-all | bytes 983040 | tf_op jit(solution)/shard_map/all_to_all | solution.py:181
  108.1 0.8 shard_map.164
  108.8 0.7 copy.19
  (11 shorter events, 0.0 us)
Async XLA Ops:
  0.6 24.7 %copy-start.1 = (bf16[512,512]{1,0:T(8,128)(2,1)S(1)}, bf16[512,512]{1,0:T(8,128)(2,1)}, u32[]{:S(2)}) copy-start(bf16[512,512]{1,0:T(8,128)(2,1)} %w_value.1) | copy-start | bytes 1572868
  0.6 24.6 %copy-start = (bf16[512,512]{1,0:T(8,128)(2,1)S(1)}, bf16[512,512]{1,0:T(8,128)(2,1)}, u32[]{:S(2)}) copy-start(bf16[512,512]{1,0:T(8,128)(2,1)} %w_key.1) | copy-start | bytes 1572868
  1.5 0.7 copy-start.7
  21.8 3.5 %collective-permute-start = (bf16[16,16,640]{2,1,0:T(8,128)(2,1)S(1)}, bf16[16,16,640]{2,1,0:T(8,128)(2,1)S(1)}, u32[]{:S(2)}, u32[]{:S(2)}) collective-permute-start(bf16[16,16,640]{2,1,0:T(8,128)(2,1)S(1)} %all_to_all.20.own), channel_id=1, source_target_pairs={{0,16},{16,0},{1,17},{17,1},{2,18},{18,2},{3,19},{19,3},{4,20},{20... | collective-permute-start | bytes 983048 | tf_op jit(solution)/shard_map/ppermute | solution.py:199
  25.3 0.9 copy-start.2
  26.2 0.9 copy-start.3
  27.1 0.9 copy-start.4
  28.0 0.8 copy-start.5
  28.8 0.7 copy-start.6
  34.8 14.7 %collective-permute-start.1 = (bf16[16,16,1664]{2,1,0:T(8,128)(2,1)S(1)}, bf16[16,16,1664]{2,1,0:T(8,128)(2,1)S(1)}, u32[]{:S(2)}, u32[]{:S(2)}) collective-permute-start(bf16[16,16,1664]{2,1,0:T(8,128)(2,1)S(1)} %get-tuple-element.23), channel_id=1, source_target_pairs={{0,16},{16,0},{1,17},{17,1},{2,18},{18,2},{3,19},{19,3},{4,20},{20... | collective-permute-start | bytes 2555912 | tf_op jit(solution)/shard_map/ppermute | solution.py:229
  36.8 24.8 %all-to-all-start.2 = ((bf16[16,8,640]{2,1,0:T(8,128)(2,1)}), bf16[16,8,640]{2,1,0:T(8,128)(2,1)S(1)}, u32[]{:S(2)}, u32[]{:S(2)}) async-start(bf16[16,8,640]{2,1,0:T(8,128)(2,1)} %get-tuple-element.24), calls=%async_computation.2 | async-start | bytes 327680 | tf_op jit(solution)/shard_map/all_to_all | solution.py:181
  49.5 0.9 copy-start.8

commit v2 on v1

v2 whole, which is shorter than its diff:
```python
import functools

import jax
import jax.numpy as jnp
from jax import lax
from jax.experimental import pallas as pl
from jax.experimental.pallas import tpu as pltpu
from jax.sharding import Mesh, PartitionSpec as P

DC = 512
DR = 64
DN = 128
DV = 128
RESP = 128
PAGE = 16
LOCAL = 4
ROWS = LOCAL * RESP
EXT = 640
CHIPS = 16
HALF = CHIPS * PAGE
KEYS = 2 * HALF + RESP
WIDE = 2 * LOCAL * DN + EXT
OWNERS = [4 * (b & 1) + 2 * (b >> 1 & 1) + (b >> 2 & 1) for b in range(RESP // PAGE)]
SCALE = (DN + DR) ** (-0.5)
F32 = jnp.float32
BF16 = jnp.bfloat16
SAMPLE = ("xl", "y", "c")
HEAD = ("z", "xh")
PARAMS = pltpu.CompilerParams(vmem_limit_bytes=40 * 1024 * 1024)


def dot(a, b, ca, cb):
    return lax.dot_general(a, b, (((ca,), (cb,)), ((), ())), preferred_element_type=F32)


def columns(part, width):
    return slice(part * width, (part + 1) * width)


def with_rope(latent, rope):
    pad = jnp.zeros((latent.shape[0], EXT - DC - DR), BF16)
    return jnp.concatenate([latent, rope, pad], axis=1)


def pages_kernel(latent_far, rope_far, out, latent, rope, done):
    first = pltpu.make_async_copy(latent_far, latent, done.at[0])
    second = pltpu.make_async_copy(rope_far, rope, done.at[1])
    first.start()
    second.start()
    first.wait()
    second.wait()
    page = with_rope(latent[...], rope[...])
    for k in range(CHIPS):
        out[k] = page


def query_kernel(
    where,
    q_nope,
    q_rope,
    grad,
    w_key,
    w_value,
    resp_latent,
    resp_rope_t,
    query,
    d_out,
    masked_out,
    resp_keys,
):
    length = where[0]
    rope = jnp.transpose(resp_rope_t[...].astype(F32)).astype(BF16)
    resp_keys[...] = with_rope(resp_latent[...], rope)
    live = lax.broadcasted_iota(jnp.int32, (RESP, LOCAL * DV), 0) < length
    masked = jnp.where(live, grad[...].astype(F32), 0.0).astype(BF16)
    masked_out[...] = masked
    for h in range(LOCAL):
        rows = columns(h, RESP)
        latent = dot(q_nope[:, columns(h, DN)], w_key[:, columns(h, DN)], 1, 1)
        query[rows, :] = with_rope(latent.astype(BF16), q_rope[:, columns(h, DR)])
        d_out[rows, :] = dot(masked[:, columns(h, DV)], w_value[:, columns(h, DV)], 1, 1).astype(
            BF16
        )


def attention_kernel(
    where,
    query,
    d_out,
    own,
    other,
    resp_keys,
    keep_resp,
    send_resp,
    attention_out,
    d_scores_out,
    keys,
):
    length = where[0]
    keys[0:HALF, :] = own[...].reshape(HALF, EXT)
    keys[HALF : 2 * HALF, :] = other[...].reshape(HALF, EXT)
    keys[2 * HALF : KEYS, :] = resp_keys[...]
    scores = dot(keys[...], query[...], 1, 1) * SCALE
    token = lax.broadcasted_iota(jnp.int32, (RESP, ROWS), 1) % RESP
    key_at = lax.broadcasted_iota(jnp.int32, (RESP, ROWS), 0)
    allowed = (key_at <= token) & (key_at < length)
    scores = jnp.concatenate(
        [scores[0 : 2 * HALF], jnp.where(allowed, scores[2 * HALF : KEYS], -1e30)], axis=0
    )
    highest = jnp.max(scores, axis=0, keepdims=True)
    exponent = jnp.exp(scores - highest)
    attention = exponent * (1.0 / jnp.sum(exponent, axis=0, keepdims=True))
    attention_b = attention.astype(BF16)
    attention_out[...] = attention_b
    d_attention = dot(keys[:, 0:DC], d_out[...], 1, 1)
    row_delta = jnp.sum(attention * d_attention, axis=0, keepdims=True)
    d_scores = (SCALE * attention * (d_attention - row_delta)).astype(BF16)
    d_scores_out[...] = d_scores
    own_grad = dot(d_scores[2 * HALF : KEYS], query[...], 1, 0)
    own_grad_v = dot(attention_b[2 * HALF : KEYS], d_out[...], 1, 0)
    resp = jnp.concatenate([own_grad[:, 0:DC] + own_grad_v, own_grad[:, DC:EXT]], axis=1)
    blocks = resp.astype(BF16).reshape(RESP // PAGE, PAGE, EXT)
    place = where[2]
    for g in range(RESP // PAGE // 2):
        low, high = blocks[g], blocks[RESP // PAGE // 2 + g]
        keep_resp[g] = jnp.where(place == 0, low, high)
        send_resp[g] = jnp.where(place == 0, high, low)


def grads_kernel(
    where,
    q_nope,
    masked,
    query,
    d_out,
    keys,
    attention,
    d_scores,
    d_query_out,
    keep,
    send,
    weight,
    prompt,
):
    core = where[1]
    prompt_scores = d_scores[0 : 2 * HALF, :]
    key_grad = dot(prompt_scores, query[...], 1, 0)
    key_grad_v = dot(attention[0 : 2 * HALF, :], d_out[...], 1, 0)
    prompt[:, 0:DC] = (key_grad[:, 0:DC] + key_grad_v).astype(BF16)
    prompt[:, DC:EXT] = key_grad[:, DC:EXT].astype(BF16)
    d_query = dot(keys[...], d_scores[...], 0, 0).astype(BF16)
    d_query_out[...] = d_query
    out_latent = dot(keys[:, 0:DC], attention[...], 0, 0).astype(BF16)
    for h in range(LOCAL):
        d_q = d_query[0:DC, columns(h, RESP)]
        weight[:, columns(h, DN)] = dot(d_q, q_nope[:, columns(h, DN)], 1, 0).astype(BF16)
        weight[:, columns(LOCAL + h, DN)] = dot(
            out_latent[:, columns(h, RESP)], masked[:, columns(h, DV)], 1, 0
        ).astype(BF16)
    width = 2 * LOCAL * DN
    for k in range(CHIPS):
        mine = pl.ds(pl.multiple_of((2 * k + core) * PAGE, PAGE), PAGE)
        theirs = pl.ds(pl.multiple_of((2 * k + 1 - core) * PAGE, PAGE), PAGE)
        keep[k, :, 0:width] = weight[mine, :]
        send[k, :, 0:width] = weight[theirs, :]
        keep[k, :, width:WIDE] = prompt[k * PAGE : (k + 1) * PAGE, :]
        send[k, :, width:WIDE] = prompt[HALF + k * PAGE : HALF + (k + 1) * PAGE, :]


def query_grad_kernel(d_query, w_key, d_q_nope, d_q_rope):
    for h in range(LOCAL):
        d_q = d_query[0:DC, columns(h, RESP)]
        d_q_nope[:, columns(h, DN)] = dot(d_q, w_key[:, columns(h, DN)], 0, 0).astype(BF16)
    d_rope = jnp.concatenate(
        [
            jnp.transpose(d_query[DC : DC + DR, columns(h, RESP)].astype(F32)) for h in range(LOCAL)
        ],
        axis=1,
    )
    d_q_rope[...] = d_rope.astype(BF16)


def halve_kernel(bit, where, kept, received, keep, send):
    half = keep.shape[0]
    place = where[bit]
    mine = pl.ds(place * half, half)
    theirs = pl.ds((1 - place) * half, half)
    keep[...] = (kept[mine].astype(F32) + received[mine].astype(F32)).astype(BF16)
    send[...] = (kept[theirs].astype(F32) + received[theirs].astype(F32)).astype(BF16)


def middle_kernel(sample_parts, kept, received, d_key_up, d_value_up, out):
    total = sample_parts[0].astype(F32)
    for k in range(1, CHIPS):
        total = total + sample_parts[k].astype(F32)
    d_key_up[...] = total[:, 0 : LOCAL * DN]
    d_value_up[...] = total[:, LOCAL * DN : 2 * LOCAL * DN]
    page = total[:, 2 * LOCAL * DN : WIDE]
    rows = kept[0].astype(F32) + received[0].astype(F32)
    line = jnp.concatenate([rows, page], axis=1).astype(BF16)
    for g in range(CHIPS):
        out[g] = line


def last_kernel(parts, d_prompt, d_prompt_rope, d_resp, d_resp_rope_t):
    page = parts[0, :, EXT : 2 * EXT].astype(F32)
    for g in range(1, CHIPS):
        page = page + parts[g, :, EXT : 2 * EXT].astype(F32)
    d_prompt[...] = page[:, 0:DC]
    d_prompt_rope[...] = page[:, DC : DC + DR]
    rows = jnp.concatenate(
        [parts[g, :, 0:EXT].astype(F32) + parts[g + 8, :, 0:EXT].astype(F32) for g in OWNERS],
        axis=0,
    )
    d_resp[...] = rows[:, 0:DC]
    d_resp_rope_t[...] = jnp.transpose(rows[:, DC:EXT])[0:DR]


def call(kernel, outs, *args, scratch=(), scalars=0, flops=0, far=False):
    vmem = pl.BlockSpec(memory_space=pltpu.VMEM)
    smem = pl.BlockSpec(memory_space=pltpu.SMEM)
    return pl.pallas_call(
        kernel,
        out_shape=[jax.ShapeDtypeStruct(shape, kind) for shape, kind in outs],
        in_specs=[smem] * scalars + [pl.BlockSpec(memory_space=pl.ANY) if far else vmem] * (len(args) - scalars),
        out_specs=[vmem] * len(outs),
        scratch_shapes=list(scratch),
        compiler_params=PARAMS,
        cost_estimate=pl.CostEstimate(flops=flops, bytes_accessed=0, transcendentals=0),
    )(*args)


def spread(parts, axes):
    return lax.all_to_all(parts, axes, 0, 0, tiled=True)


def body(
    q_nope,
    q_rope,
    resp_latent,
    resp_rope_t,
    prompt_latent,
    prompt_rope_t,
    w_key_up,
    w_value_up,
    grad_out,
    lengths,
):
    swap = [(0, 1), (1, 0)]
    (pages,) = call(
        pages_kernel,
        [((CHIPS, PAGE, EXT), BF16)],
        prompt_latent,
        jnp.transpose(prompt_rope_t),
        far=True,
        scratch=[
            pltpu.VMEM((PAGE, DC), BF16),
            pltpu.VMEM((PAGE, DR), BF16),
            pltpu.SemaphoreType.DMA((2,)),
        ],
    )
    own = spread(pages, ("xl", "y"))
    z = lax.axis_index("z")
    where = jnp.stack(
        [lengths[0], lax.axis_index("c"), lax.axis_index("xh"), z & 1, z >> 1 & 1]
    )
    query, d_out, masked, resp_keys = call(
        query_kernel,
        [
            ((ROWS, EXT), BF16),
            ((ROWS, DC), BF16),
            ((RESP, LOCAL * DV), BF16),
            ((RESP, EXT), BF16),
        ],
        where,
        q_nope,
        q_rope,
        grad_out,
        w_key_up,
        w_value_up,
        resp_latent,
        resp_rope_t,
        scalars=1,
        flops=4_000_000_000,
    )
    own, query = lax.optimization_barrier((own, query))
    other = lax.ppermute(own, "c", swap)
    keep_resp, send_resp, attention, d_scores, keys = call(
        attention_kernel,
        [
            ((RESP // PAGE // 2, PAGE, EXT), BF16),
            ((RESP // PAGE // 2, PAGE, EXT), BF16),
            ((KEYS, ROWS), BF16),
            ((KEYS, ROWS), BF16),
            ((KEYS, EXT), BF16),
        ],
        where,
        query,
        d_out,
        own,
        other,
        resp_keys,
        scalars=1,
        flops=4_000_000_000,
    )
    got_resp = lax.ppermute(send_resp, "xh", swap)
    d_query, keep, send = call(
        grads_kernel,
        [
            ((EXT, ROWS), BF16),
            ((CHIPS, PAGE, WIDE), BF16),
            ((CHIPS, PAGE, WIDE), BF16),
        ],
        where,
        q_nope,
        masked,
        query,
        d_out,
        keys,
        attention,
        d_scores,
        scalars=1,
        flops=4_000_000_000,
        scratch=[
            pltpu.VMEM((DC, 2 * LOCAL * DN), BF16),
            pltpu.VMEM((2 * HALF, EXT), BF16),
        ],
    )
    chip_sum = keep + lax.ppermute(send, "c", swap)
    sample_parts = spread(chip_sum, ("xl", "y"))
    d_q_nope, d_q_rope = call(
        query_grad_kernel,
        [((RESP, LOCAL * DN), BF16), ((RESP, LOCAL * DR), BF16)],
        d_query,
        w_key_up,
        flops=1_000_000_000,
    )
    for bit in range(2):
        half = keep_resp.shape[0] // 2
        keep_resp, send_resp = call(
            functools.partial(halve_kernel, 3 + bit),
            [((half, PAGE, EXT), BF16)] * 2,
            where,
            keep_resp,
            got_resp,
            scalars=1,
        )
        got_resp = lax.ppermute(send_resp, "z", [(i, i ^ (1 << bit)) for i in range(8)])
    d_key_up, d_value_up, line = call(
        middle_kernel,
        [
            ((PAGE, LOCAL * DN), F32),
            ((PAGE, LOCAL * DV), F32),
            ((CHIPS, PAGE, 2 * EXT), BF16),
        ],
        sample_parts,
        keep_resp,
        got_resp,
    )
    lines = spread(line, HEAD)
    d_prompt, d_prompt_rope, d_resp, d_resp_rope_t = call(
        last_kernel,
        [
            ((PAGE, DC), F32),
            ((PAGE, DR), F32),
            ((RESP, DC), F32),
            ((DR, RESP), F32),
        ],
        lines,
    )
    return (
        d_q_nope,
        d_q_rope,
        d_key_up,
        d_value_up,
        d_prompt,
        jnp.transpose(d_prompt_rope),
        d_resp,
        d_resp_rope_t,
    )


def solution(mesh):
    fine = Mesh(mesh.devices.reshape(2, 8, 2, 8, 2), SAMPLE + HEAD)
    return jax.shard_map(
        body,
        mesh=fine,
        in_specs=(
            P(SAMPLE, HEAD),
            P(SAMPLE, HEAD),
            P(SAMPLE, None),
            P(None, SAMPLE),
            P(SAMPLE, None),
            P(None, SAMPLE),
            P(None, HEAD),
            P(None, HEAD),
            P(SAMPLE, HEAD),
            P(SAMPLE),
        ),
        out_specs=(
            P(SAMPLE, HEAD),
            P(SAMPLE, HEAD),
            P(SAMPLE, HEAD),
            P(SAMPLE, HEAD),
            P(SAMPLE, None),
            P(None, SAMPLE),
            P(SAMPLE, None),
            P(None, SAMPLE),
        ),
        check_vma=False,
    )
```

time: 110 us -> 99.9 us (0.908)
  the two profiles are of different devices: /device:TPU:8 before, /device:TPU:24 now
where the time goes in v2:
time: 99.9 us; the launch traced here: 99.2 us
  starting transfers between devices  44.4 us (44%)
  waiting for transfers between devices  38.8 us (39%)
  Pallas kernels  10.9 us (11%)
  local copies, waits for them, and re-layouts  2.55 us (3%)
  between operations  1.48 us (1%)
  other arithmetic  1.12 us (1%)
    all_to_all x3, starting transfers between devices, spread(): return lax.all_to_all(parts, axes, 0, 0, tiled=True)  25.5 us
    all_to_all x3, waiting for transfers between devices, spread(): return lax.all_to_all(parts, axes, 0, 0, tiled=True)  25.1 us
    pallas_call x9, Pallas kernels, call(): pl.pallas_call(kernel, out_shape=[jax.ShapeDtypeStruct(shape, kind) for s...  10.9 us
    ppermute x2, starting transfers between devices, body(): lax.ppermute(send_resp, 'z', [(i, i ^ 1 << bit) for i in range(8)])  10.4 us
    ppermute x1, waiting for transfers between devices, body(): got_resp = lax.ppermute(send_resp, 'xh', swap)  6.13 us
    ppermute x1, starting transfers between devices, body(): got_resp = lax.ppermute(send_resp, 'xh', swap)  4.63 us
    ppermute x2, waiting for transfers between devices, body(): lax.ppermute(send_resp, 'z', [(i, i ^ 1 << bit) for i in range(8)])  3.71 us
    unnamed x20, local copies, waits for them, and re-layouts  2.47 us
  transfers between devices with their start and end apart: 8, of which 7 were waited for; matrix products, arithmetic and copies ran while one was open for 0% of the time, Pallas kernels for 3%

profile of v2, /device:TPU:24, one launch (start us, length us, event | category | flops | bytes accessed | tf_op | source)
XLA Modules:
  0.0 99.2 jit_solution(11504067784205567558)
XLA Ops:
  2.0 0.8 shard_map.162
  2.9 9.1 %all-to-all-start = ((bf16[16,16,640]{2,1,0:T(8,128)(2,1)}), bf16[16,16,640]{2,1,0:T(8,128)(2,1)S(1)}, u32[]{:S(2)}, u32[]{:S(2)}) async-start(bf16[16,16,640]{2,1,0:T(8,128)(2,1)} %shard_map.162), calls=%async_computation | async-start | bytes 655360 | tf_op jit(solution)/shard_map/all_to_all | solution.py:234
  12.8 1.0 %copy-done.3 = bf16[512,512]{1,0:T(8,128)(2,1)S(1)} copy-done((bf16[512,512]{1,0:T(8,128)(2,1)S(1)}, bf16[512,512]{1,0:T(8,128)(2,1)}, u32[]{:S(2)}) %copy-start.3) | copy-done | bytes 524312
  13.8 1.0 shard_map.161
  14.8 6.5 %all-to-all-done.own = bf16[16,16,640]{2,1,0:T(8,128)(2,1)S(1)} async-done(((bf16[16,16,640]{2,1,0:T(8,128)(2,1)}), bf16[16,16,640]{2,1,0:T(8,128)(2,1)S(1)}, u32[]{:S(2)}, u32[]{:S(2)}) %all-to-all-start) | async-done | bytes 327712 | tf_op jit(solution)/shard_map/all_to_all | solution.py:234
  21.3 1.9 %collective-permute-start = (bf16[16,16,640]{2,1,0:T(8,128)(2,1)S(1)}, bf16[16,16,640]{2,1,0:T(8,128)(2,1)S(1)}, u32[]{:S(2)}, u32[]{:S(2)}) collective-permute-start(bf16[16,16,640]{2,1,0:T(8,128)(2,1)S(1)} %all-to-all-done.own), channel_id=1, source_target_pairs={{0,16},{16,0},{1,17},{17,1},{2,18},{18,2},{3,19},{19,3},{4,20},{20... | collective-permute-start | bytes 983048 | tf_op jit(solution)/shard_map/ppermute | solution.py:287
  23.3 1.6 %collective-permute-done.other = bf16[16,16,640]{2,1,0:T(8,128)(2,1)S(1)} collective-permute-done((bf16[16,16,640]{2,1,0:T(8,128)(2,1)S(1)}, bf16[16,16,640]{2,1,0:T(8,128)(2,1)S(1)}, u32[]{:S(2)}, u32[]{:S(2)}) %collective-permute-start) | collective-permute-done | bytes 327712 | tf_op jit(solution)/shard_map/ppermute | solution.py:287
  24.9 2.4 %shard_map.163 = (bf16[4,16,640]{2,1,0:T(8,128)(2,1)S(1)}, bf16[4,16,640]{2,1,0:T(8,128)(2,1)S(1)}, bf16[640,512]{1,0:T(8,128)(2,1)S(1)}, bf16[640,512]{1,0:T(8,128)(2,1)S(1)}, bf16[640,640]{1,0:T(8,128)(2,1)S(1)}) custom-call(s32[5]{0:T(128)S(1)} %stack.19.where, bf16[512,640]{1,0:T(8,128)(2,1)S(1)} %get-tuple-element.37.query, ...), custom_call_target="tpu_custom_call" | custom-call | flops 4000000000 | tf_op jit(solution)/shard_map/pallas_call | solution.py:222
  27.3 2.8 %shard_map.164 = (bf16[640,512]{1,0:T(8,128)(2,1)S(1)}, bf16[16,16,1664]{2,1,0:T(8,128)(2,1)S(1)}, bf16[16,16,1664]{2,1,0:T(8,128)(2,1)S(1)}) custom-call(s32[5]{0:T(128)S(1)} %stack.19.where, bf16[128,512]{1,0:T(8,128)(2,1)S(1)} %copy-done.7, bf16[128,512]{1,0:T(8,128)(2,1)S(1)} %get-tuple-element.35.masked, bf16[512,640]{1,0:T(8,128)(2,1)S(1)} %get-tuple-element.37.query, ...), custom_call_target="tpu_custom_call" | custom-call | flops 4000000000 | tf_op jit(solution)/shard_map/pallas_call | solution.py:222
  30.1 2.0 %collective-permute-start.1 = (bf16[16,16,1664]{2,1,0:T(8,128)(2,1)S(1)}, bf16[16,16,1664]{2,1,0:T(8,128)(2,1)S(1)}, u32[]{:S(2)}, u32[]{:S(2)}) collective-permute-start(bf16[16,16,1664]{2,1,0:T(8,128)(2,1)S(1)} %get-tuple-element.48), channel_id=1, source_target_pairs={{0,16},{16,0},{1,17},{17,1},{2,18},{18,2},{3,19},{19,3},{4,20},{20... | collective-permute-start | bytes 2555912 | tf_op jit(solution)/shard_map/ppermute | solution.py:329
  32.1 2.2 %collective-permute-done.1 = bf16[16,16,1664]{2,1,0:T(8,128)(2,1)S(1)} collective-permute-done((bf16[16,16,1664]{2,1,0:T(8,128)(2,1)S(1)}, bf16[16,16,1664]{2,1,0:T(8,128)(2,1)S(1)}, u32[]{:S(2)}, u32[]{:S(2)}) %collective-permute-start.1) | collective-permute-done | bytes 852000 | tf_op jit(solution)/shard_map/ppermute | solution.py:329
  34.3 1.1 %add.3 = bf16[16,16,1664]{2,1,0:T(8,128)(2,1)} add(bf16[16,16,1664]{2,1,0:T(8,128)(2,1)S(1)} %get-tuple-element.47, bf16[16,16,1664]{2,1,0:T(8,128)(2,1)S(1)} %collective-permute-done.1) | non-fusion elementwise | flops 425984 | bytes 2555904 | tf_op jit(solution)/shard_map/add | solution.py:329
  35.5 6.0 %all-to-all-start.1 = ((bf16[16,16,1664]{2,1,0:T(8,128)(2,1)}), bf16[16,16,1664]{2,1,0:T(8,128)(2,1)S(1)}, u32[]{:S(2)}, u32[]{:S(2)}) async-start(bf16[16,16,1664]{2,1,0:T(8,128)(2,1)} %add.3), calls=%async_computation.1 | async-start | bytes 1703936 | tf_op jit(solution)/shard_map/all_to_all | solution.py:234
  41.4 4.6 %collective-permute-start.2 = (bf16[4,16,640]{2,1,0:T(8,128)(2,1)S(1)}, bf16[4,16,640]{2,1,0:T(8,128)(2,1)S(1)}, u32[]{:S(2)}, u32[]{:S(2)}) collective-permute-start(bf16[4,16,640]{2,1,0:T(8,128)(2,1)S(1)} %get-tuple-element.50), channel_id=1, source_target_pairs={{0,1},{1,0},{2,3},{3,2},{4,5},{5,4},{6,7},{7,6},{8,9},{9,8},{10,11... | collective-permute-start | bytes 245768 | tf_op jit(solution)/shard_map/ppermute | solution.py:306
  46.1 6.1 %collective-permute-done.2.received = bf16[4,16,640]{2,1,0:T(8,128)(2,1)S(1)} collective-permute-done((bf16[4,16,640]{2,1,0:T(8,128)(2,1)S(1)}, bf16[4,16,640]{2,1,0:T(8,128)(2,1)S(1)}, u32[]{:S(2)}, u32[]{:S(2)}) %collective-permute-start.2) | collective-permute-done | bytes 81952 | tf_op jit(solution)/shard_map/ppermute | solution.py:306
  52.8 4.3 %collective-permute-start.3 = (bf16[2,16,640]{2,1,0:T(8,128)(2,1)S(1)}, bf16[2,16,640]{2,1,0:T(8,128)(2,1)S(1)}, u32[]{:S(2)}, u32[]{:S(2)}) collective-permute-start(bf16[2,16,640]{2,1,0:T(8,128)(2,1)S(1)} %get-tuple-element.52), channel_id=1, source_target_pairs={{0,2},{2,0},{4,6},{6,4},{8,10},{10,8},{12,14},{14,12},{1,3},{3,1},... | collective-permute-start | bytes 122888 | tf_op jit(solution)/shard_map/ppermute | solution.py:348
  57.1 2.0 %collective-permute-done.3.received = bf16[2,16,640]{2,1,0:T(8,128)(2,1)S(1)} collective-permute-done((bf16[2,16,640]{2,1,0:T(8,128)(2,1)S(1)}, bf16[2,16,640]{2,1,0:T(8,128)(2,1)S(1)}, u32[]{:S(2)}, u32[]{:S(2)}) %collective-permute-start.3) | collective-permute-done | bytes 40992 | tf_op jit(solution)/shard_map/ppermute | solution.py:348
  59.6 6.1 %collective-permute-start.4 = (bf16[1,16,640]{2,1,0:T(8,128)(2,1)S(1)}, bf16[1,16,640]{2,1,0:T(8,128)(2,1)S(1)}, u32[]{:S(2)}, u32[]{:S(2)}) collective-permute-start(bf16[1,16,640]{2,1,0:T(8,128)(2,1)S(1)} %get-tuple-element.54), channel_id=1, source_target_pairs={{0,4},{2,6},{4,0},{6,2},{8,12},{10,14},{12,8},{14,10},{1,5},{3,7},... | collective-permute-start | bytes 61448 | tf_op jit(solution)/shard_map/ppermute | solution.py:348
  65.7 1.7 %collective-permute-done.4.received = bf16[1,16,640]{2,1,0:T(8,128)(2,1)S(1)} collective-permute-done((bf16[1,16,640]{2,1,0:T(8,128)(2,1)S(1)}, bf16[1,16,640]{2,1,0:T(8,128)(2,1)S(1)}, u32[]{:S(2)}, u32[]{:S(2)}) %collective-permute-start.4) | collective-permute-done | bytes 20512 | tf_op jit(solution)/shard_map/ppermute | solution.py:348
  67.5 1.0 shard_map.168
  68.4 10.4 %all-to-all-start.2 = ((bf16[16,16,1280]{2,1,0:T(8,128)(2,1)}), bf16[16,16,1280]{2,1,0:T(8,128)(2,1)S(1)}, u32[]{:S(2)}, u32[]{:S(2)}) async-start(bf16[16,16,1280]{2,1,0:T(8,128)(2,1)} %get-tuple-element.57), calls=%async_computation.2 | async-start | bytes 1310720 | tf_op jit(solution)/shard_map/all_to_all | solution.py:234
  78.8 1.0 %shard_map.165 = (bf16[128,512]{1,0:T(8,128)(2,1)}, bf16[128,256]{1,0:T(8,128)(2,1)}) custom-call(bf16[640,512]{1,0:T(8,128)(2,1)S(1)} %get-tuple-element.44.d_query, bf16[512,512]{1,0:T(8,128)(2,1)S(1)} %copy-done.4), custom_call_target="tpu_custom_call" | custom-call | flops 1000000000 | tf_op jit(solution)/shard_map/pallas_call | solution.py:222
  79.9 18.6 %all-to-all-done.2.parts = bf16[16,16,1280]{2,1,0:T(8,128)(2,1)S(1)} async-done(((bf16[16,16,1280]{2,1,0:T(8,128)(2,1)}), bf16[16,16,1280]{2,1,0:T(8,128)(2,1)S(1)}, u32[]{:S(2)}, u32[]{:S(2)}) %all-to-all-start.2) | async-done | bytes 655392 | tf_op jit(solution)/shard_map/all_to_all | solution.py:234
  98.4 0.8 shard_map.169
  (23 shorter events, 2.7 us)
Async XLA Ops:
  0.6 0.7 copy-start
  1.4 0.7 copy-start.1
  2.0 10.7 %copy-start.2 = (bf16[512,512]{1,0:T(8,128)(2,1)S(1)}, bf16[512,512]{1,0:T(8,128)(2,1)}, u32[]{:S(2)}) copy-start(bf16[512,512]{1,0:T(8,128)(2,1)} %w_value.1) | copy-start | bytes 1572868
  2.8 9.9 %copy-start.5 = (bf16[128,512]{1,0:T(8,128)(2,1)S(1)}, bf16[128,512]{1,0:T(8,128)(2,1)}, u32[]{:S(2)}) copy-start(bf16[128,512]{1,0:T(8,128)(2,1)} %grad.1) | copy-start | bytes 393220
  2.8 9.9 %copy-start.6 = (bf16[128,512]{1,0:T(8,128)(2,1)S(1)}, bf16[128,512]{1,0:T(8,128)(2,1)}, u32[]{:S(2)}) copy-start(bf16[128,512]{1,0:T(8,128)(2,1)} %resp_latent.1) | copy-start | bytes 393220
  2.9 9.9 %copy-start.7 = (bf16[128,512]{1,0:T(8,128)(2,1)S(1)}, bf16[128,512]{1,0:T(8,128)(2,1)}, u32[]{:S(2)}) copy-start(bf16[128,512]{1,0:T(8,128)(2,1)} %q_nope.3) | copy-start | bytes 393220
  2.9 9.9 %copy-start.8 = (bf16[128,256]{1,0:T(8,128)(2,1)S(1)}, bf16[128,256]{1,0:T(8,128)(2,1)}, u32[]{:S(2)}) copy-start(bf16[128,256]{1,0:T(8,128)(2,1)} %q_rope.1) | copy-start | bytes 196612
  2.9 18.5 %all-to-all-start = ((bf16[16,16,640]{2,1,0:T(8,128)(2,1)}), bf16[16,16,640]{2,1,0:T(8,128)(2,1)S(1)}, u32[]{:S(2)}, u32[]{:S(2)}) async-start(bf16[16,16,640]{2,1,0:T(8,128)(2,1)} %shard_map.162), calls=%async_computation | async-start | bytes 655360 | tf_op jit(solution)/shard_map/all_to_all | solution.py:234
  12.0 0.8 copy-start.9
  12.8 1.0 %copy-start.3 = (bf16[512,512]{1,0:T(8,128)(2,1)S(1)}, bf16[512,512]{1,0:T(8,128)(2,1)}, u32[]{:S(2)}) copy-start(bf16[512,512]{1,0:T(8,128)(2,1)} %w_key.3) | copy-start | bytes 1572868
  21.3 3.5 %collective-permute-start = (bf16[16,16,640]{2,1,0:T(8,128)(2,1)S(1)}, bf16[16,16,640]{2,1,0:T(8,128)(2,1)S(1)}, u32[]{:S(2)}, u32[]{:S(2)}) collective-permute-start(bf16[16,16,640]{2,1,0:T(8,128)(2,1)S(1)} %all-to-all-done.own), channel_id=1, source_target_pairs={{0,16},{16,0},{1,17},{17,1},{2,18},{18,2},{3,19},{19,3},{4,20},{20... | collective-permute-start | bytes 983048 | tf_op jit(solution)/shard_map/ppermute | solution.py:287
  30.1 4.3 %collective-permute-start.1 = (bf16[16,16,1664]{2,1,0:T(8,128)(2,1)S(1)}, bf16[16,16,1664]{2,1,0:T(8,128)(2,1)S(1)}, u32[]{:S(2)}, u32[]{:S(2)}) collective-permute-start(bf16[16,16,1664]{2,1,0:T(8,128)(2,1)S(1)} %get-tuple-element.48), channel_id=1, source_target_pairs={{0,16},{16,0},{1,17},{17,1},{2,18},{18,2},{3,19},{19,3},{4,20},{20... | collective-permute-start | bytes 2555912 | tf_op jit(solution)/shard_map/ppermute | solution.py:329
  35.5 32.0 %all-to-all-start.1 = ((bf16[16,16,1664]{2,1,0:T(8,128)(2,1)}), bf16[16,16,1664]{2,1,0:T(8,128)(2,1)S(1)}, u32[]{:S(2)}, u32[]{:S(2)}) async-start(bf16[16,16,1664]{2,1,0:T(8,128)(2,1)} %add.3), calls=%async_computation.1 | async-start | bytes 1703936 | tf_op jit(solution)/shard_map/all_to_all | solution.py:234
  41.4 10.8 %collective-permute-start.2 = (bf16[4,16,640]{2,1,0:T(8,128)(2,1)S(1)}, bf16[4,16,640]{2,1,0:T(8,128)(2,1)S(1)}, u32[]{:S(2)}, u32[]{:S(2)}) collective-permute-start(bf16[4,16,640]{2,1,0:T(8,128)(2,1)S(1)} %get-tuple-element.50), channel_id=1, source_target_pairs={{0,1},{1,0},{2,3},{3,2},{4,5},{5,4},{6,7},{7,6},{8,9},{9,8},{10,11... | collective-permute-start | bytes 245768 | tf_op jit(solution)/shard_map/ppermute | solution.py:306
  52.8 6.3 %collective-permute-start.3 = (bf16[2,16,640]{2,1,0:T(8,128)(2,1)S(1)}, bf16[2,16,640]{2,1,0:T(8,128)(2,1)S(1)}, u32[]{:S(2)}, u32[]{:S(2)}) collective-permute-start(bf16[2,16,640]{2,1,0:T(8,128)(2,1)S(1)} %get-tuple-element.52), channel_id=1, source_target_pairs={{0,2},{2,0},{4,6},{6,4},{8,10},{10,8},{12,14},{14,12},{1,3},{3,1},... | collective-permute-start | bytes 122888 | tf_op jit(solution)/shard_map/ppermute | solution.py:348
  59.6 7.8 %collective-permute-start.4 = (bf16[1,16,640]{2,1,0:T(8,128)(2,1)S(1)}, bf16[1,16,640]{2,1,0:T(8,128)(2,1)S(1)}, u32[]{:S(2)}, u32[]{:S(2)}) collective-permute-start(bf16[1,16,640]{2,1,0:T(8,128)(2,1)S(1)} %get-tuple-element.54), channel_id=1, source_target_pairs={{0,4},{2,6},{4,0},{6,2},{8,12},{10,14},{12,8},{14,10},{1,5},{3,7},... | collective-permute-start | bytes 61448 | tf_op jit(solution)/shard_map/ppermute | solution.py:348
  68.4 10.4 %copy-start.4 = (bf16[512,512]{1,0:T(8,128)(2,1)S(1)}, bf16[512,512]{1,0:T(8,128)(2,1)}, u32[]{:S(2)}) copy-start(bf16[512,512]{1,0:T(8,128)(2,1)} %w_key.3) | copy-start | bytes 1572868
  68.4 30.0 %all-to-all-start.2 = ((bf16[16,16,1280]{2,1,0:T(8,128)(2,1)}), bf16[16,16,1280]{2,1,0:T(8,128)(2,1)S(1)}, u32[]{:S(2)}, u32[]{:S(2)}) async-start(bf16[16,16,1280]{2,1,0:T(8,128)(2,1)} %get-tuple-element.57), calls=%async_computation.2 | async-start | bytes 1310720 | tf_op jit(solution)/shard_map/all_to_all | solution.py:234

commit v3 on v2

--- a/solution.py
+++ b/solution.py
@@ -16,11 +16,12 @@
 LOCAL = 4
 ROWS = LOCAL * RESP
 EXT = 640
+KEY = DC + DR
 CHIPS = 16
 HALF = CHIPS * PAGE
 KEYS = 2 * HALF + RESP
 WIDE = 2 * LOCAL * DN + EXT
-OWNERS = [4 * (b & 1) + 2 * (b >> 1 & 1) + (b >> 2 & 1) for b in range(RESP // PAGE)]
+OWNERS = [1 * (b & 1) + 4 * (b >> 1 & 1) + 2 * (b >> 2 & 1) for b in range(RESP // PAGE)]
 SCALE = (DN + DR) ** (-0.5)
 F32 = jnp.float32
 BF16 = jnp.bfloat16
@@ -83,6 +84,20 @@
         )
 
 
+def first_scores_kernel(where, query, d_out, own, resp_keys, scores, d_attention):
+    length = where[0]
+    pages = own[...].reshape(HALF, EXT)
+    resp = resp_keys[...]
+    scores[0:HALF, :] = dot(pages, query[...], 1, 1) * SCALE
+    token = lax.broadcasted_iota(jnp.int32, (RESP, ROWS), 1) % RESP
+    key_at = lax.broadcasted_iota(jnp.int32, (RESP, ROWS), 0)
+    allowed = (key_at <= token) & (key_at < length)
+    own_scores = dot(resp, query[...], 1, 1) * SCALE
+    scores[HALF : HALF + RESP, :] = jnp.where(allowed, own_scores, -1e30)
+    d_attention[0:HALF, :] = dot(pages[:, 0:DC], d_out[...], 1, 1)
+    d_attention[HALF : HALF + RESP, :] = dot(resp[:, 0:DC], d_out[...], 1, 1)
+
+
 def attention_kernel(
     where,
     query,
@@ -90,29 +105,35 @@
     own,
     other,
     resp_keys,
+    first_scores,
+    first_d_attention,
     keep_resp,
     send_resp,
     attention_out,
     d_scores_out,
     keys,
 ):
-    length = where[0]
     keys[0:HALF, :] = own[...].reshape(HALF, EXT)
     keys[HALF : 2 * HALF, :] = other[...].reshape(HALF, EXT)
     keys[2 * HALF : KEYS, :] = resp_keys[...]
-    scores = dot(keys[...], query[...], 1, 1) * SCALE
-    token = lax.broadcasted_iota(jnp.int32, (RESP, ROWS), 1) % RESP
-    key_at = lax.broadcasted_iota(jnp.int32, (RESP, ROWS), 0)
-    allowed = (key_at <= token) & (key_at < length)
+    other_rows = other[...].reshape(HALF, EXT)
+    other_scores = dot(other_rows, query[...], 1, 1) * SCALE
     scores = jnp.concatenate(
-        [scores[0 : 2 * HALF], jnp.where(allowed, scores[2 * HALF : KEYS], -1e30)], axis=0
+        [first_scores[0:HALF], other_scores, first_scores[HALF : HALF + RESP]], axis=0
     )
     highest = jnp.max(scores, axis=0, keepdims=True)
     exponent = jnp.exp(scores - highest)
     attention = exponent * (1.0 / jnp.sum(exponent, axis=0, keepdims=True))
     attention_b = attention.astype(BF16)
     attention_out[...] = attention_b
-    d_attention = dot(keys[:, 0:DC], d_out[...], 1, 1)
+    d_attention = jnp.concatenate(
+        [
+            first_d_attention[0:HALF],
+            dot(other_rows[:, 0:DC], d_out[...], 1, 1),
+            first_d_attention[HALF : HALF + RESP],
+        ],
+        axis=0,
+    )
     row_delta = jnp.sum(attention * d_attention, axis=0, keepdims=True)
     d_scores = (SCALE * attention * (d_attention - row_delta)).astype(BF16)
     d_scores_out[...] = d_scores
@@ -127,7 +148,25 @@
         send_resp[g] = jnp.where(place == 0, high, low)
 
 
-def grads_kernel(
+def half_grads(parity, first_key, q_nope, masked, query, d_out, attention, d_scores, d_query, out_latent, out):
+    starts = [pl.multiple_of((2 * k + parity) * PAGE, PAGE) for k in range(CHIPS)]
+    d_q = jnp.concatenate([d_query[pl.ds(start, PAGE), :] for start in starts], axis=0)
+    values = jnp.concatenate([out_latent[pl.ds(start, PAGE), :] for start in starts], axis=0)
+    for h in range(LOCAL):
+        key_part = dot(d_q[:, columns(h, RESP)], q_nope[:, columns(h, DN)], 1, 0)
+        out[:, :, columns(h, DN)] = key_part.astype(BF16).reshape(CHIPS, PAGE, DN)
+        value_part = dot(values[:, columns(h, RESP)], masked[:, columns(h, DV)], 1, 0)
+        out[:, :, columns(LOCAL + h, DN)] = value_part.astype(BF16).reshape(CHIPS, PAGE, DN)
+    rows = slice(first_key, first_key + HALF)
+    key_grad = dot(d_scores[rows, :], query[...], 1, 0)
+    key_grad_v = dot(attention[rows, :], d_out[...], 1, 0)
+    width = 2 * LOCAL * DN
+    latent_part = (key_grad[:, 0:DC] + key_grad_v).astype(BF16)
+    out[:, :, width : width + DC] = latent_part.reshape(CHIPS, PAGE, DC)
+    out[:, :, width + DC : WIDE] = key_grad[:, DC:EXT].astype(BF16).reshape(CHIPS, PAGE, EXT - DC)
+
+
+def send_kernel(
     where,
     q_nope,
     masked,
@@ -136,35 +175,19 @@
     keys,
     attention,
     d_scores,
-    d_query_out,
-    keep,
+    d_query,
+    out_latent,
     send,
-    weight,
-    prompt,
 ):
-    core = where[1]
-    prompt_scores = d_scores[0 : 2 * HALF, :]
-    key_grad = dot(prompt_scores, query[...], 1, 0)
-    key_grad_v = dot(attention[0 : 2 * HALF, :], d_out[...], 1, 0)
-    prompt[:, 0:DC] = (key_grad[:, 0:DC] + key_grad_v).astype(BF16)
-    prompt[:, DC:EXT] = key_grad[:, DC:EXT].astype(BF16)
-    d_query = dot(keys[...], d_scores[...], 0, 0).astype(BF16)
-    d_query_out[...] = d_query
-    out_latent = dot(keys[:, 0:DC], attention[...], 0, 0).astype(BF16)
-    for h in range(LOCAL):
-        d_q = d_query[0:DC, columns(h, RESP)]
-        weight[:, columns(h, DN)] = dot(d_q, q_nope[:, columns(h, DN)], 1, 0).astype(BF16)
-        weight[:, columns(LOCAL + h, DN)] = dot(
-            out_latent[:, columns(h, RESP)], masked[:, columns(h, DV)], 1, 0
-        ).astype(BF16)
-    width = 2 * LOCAL * DN
-    for k in range(CHIPS):
-        mine = pl.ds(pl.multiple_of((2 * k + core) * PAGE, PAGE), PAGE)
-        theirs = pl.ds(pl.multiple_of((2 * k + 1 - core) * PAGE, PAGE), PAGE)
-        keep[k, :, 0:width] = weight[mine, :]
-        send[k, :, 0:width] = weight[theirs, :]
-        keep[k, :, width:WIDE] = prompt[k * PAGE : (k + 1) * PAGE, :]
-        send[k, :, width:WIDE] = prompt[HALF + k * PAGE : HALF + (k + 1) * PAGE, :]
+    d_query[...] = dot(keys[...], d_scores[...], 0, 0).astype(BF16)
+    out_latent[...] = dot(keys[:, 0:DC], attention[...], 0, 0).astype(BF16)
+    half_grads(1 - where[1], HALF, q_nope, masked, query, d_out, attention, d_scores, d_query, out_latent, send)
+
+
+def keep_kernel(
+    where, q_nope, masked, query, d_out, attention, d_scores, d_query, out_latent, keep
+):
+    half_grads(where[1], 0, q_nope, masked, query, d_out, attention, d_scores, d_query, out_latent, keep)
 
 
 def query_grad_kernel(d_query, w_key, d_q_nope, d_q_rope):
@@ -189,31 +212,38 @@
     send[...] = (kept[theirs].astype(F32) + received[theirs].astype(F32)).astype(BF16)
 
 
-def middle_kernel(sample_parts, kept, received, d_key_up, d_value_up, out):
-    total = sample_parts[0].astype(F32)
+def line_kernel(sample_parts, kept, received, out):
+    first = 2 * LOCAL * DN
+    page = sample_parts[0, :, first:WIDE].astype(F32)
     for k in range(1, CHIPS):
-        total = total + sample_parts[k].astype(F32)
-    d_key_up[...] = total[:, 0 : LOCAL * DN]
-    d_value_up[...] = total[:, LOCAL * DN : 2 * LOCAL * DN]
-    page = total[:, 2 * LOCAL * DN : WIDE]
+        page = page + sample_parts[k, :, first:WIDE].astype(F32)
     rows = kept[0].astype(F32) + received[0].astype(F32)
-    line = jnp.concatenate([rows, page], axis=1).astype(BF16)
+    line = jnp.concatenate([rows[:, 0:KEY], page[:, 0:KEY]], axis=1).astype(BF16)
     for g in range(CHIPS):
         out[g] = line
 
 
+def weights_kernel(sample_parts, d_key_up, d_value_up):
+    for out, first in ((d_key_up, 0), (d_value_up, LOCAL * DN)):
+        lanes = slice(first, first + LOCAL * DN)
+        total = sample_parts[0, :, lanes].astype(F32)
+        for k in range(1, CHIPS):
+            total = total + sample_parts[k, :, lanes].astype(F32)
+        out[...] = total
+
+
 def last_kernel(parts, d_prompt, d_prompt_rope, d_resp, d_resp_rope_t):
-    page = parts[0, :, EXT : 2 * EXT].astype(F32)
+    page = parts[0].astype(F32)
     for g in range(1, CHIPS):
-        page = page + parts[g, :, EXT : 2 * EXT].astype(F32)
-    d_prompt[...] = page[:, 0:DC]
-    d_prompt_rope[...] = page[:, DC : DC + DR]
+        page = page + parts[g].astype(F32)
+    d_prompt[...] = page[:, KEY : KEY + DC]
+    d_prompt_rope[...] = page[:, KEY + DC : 2 * KEY]
     rows = jnp.concatenate(
-        [parts[g, :, 0:EXT].astype(F32) + parts[g + 8, :, 0:EXT].astype(F32) for g in OWNERS],
+        [parts[g, :, 0:KEY].astype(F32) + parts[g + 8, :, 0:KEY].astype(F32) for g in OWNERS],
         axis=0,
     )
     d_resp[...] = rows[:, 0:DC]
-    d_resp_rope_t[...] = jnp.transpose(rows[:, DC:EXT])[0:DR]
+    d_resp_rope_t[...] = jnp.transpose(rows[:, DC:KEY])
 
 
 def call(kernel, outs, *args, scratch=(), scalars=0, flops=0, far=False):
@@ -222,7 +252,7 @@
     return pl.pallas_call(
         kernel,
         out_shape=[jax.ShapeDtypeStruct(shape, kind) for shape, kind in outs],
-        in_specs=[smem] * scalars + [pl.BlockSpec(memory_space=pl.ANY) if far else vmem] * (len(args) - scalars),
+        in_specs=[smem] * scalars + [pl.BlockSpec(memory_space=pltpu.HBM) if far else vmem] * (len(args) - scalars),
         out_specs=[vmem] * len(outs),
         scratch_shapes=list(scratch),
         compiler_params=PARAMS,
@@ -250,8 +280,8 @@
     (pages,) = call(
         pages_kernel,
         [((CHIPS, PAGE, EXT), BF16)],
-        prompt_latent,
-        jnp.transpose(prompt_rope_t),
+        pltpu.with_memory_space_constraint(prompt_latent, pltpu.HBM),
+        pltpu.with_memory_space_constraint(jnp.transpose(prompt_rope_t), pltpu.HBM),
         far=True,
         scratch=[
             pltpu.VMEM((PAGE, DC), BF16),
@@ -262,7 +292,7 @@
     own = spread(pages, ("xl", "y"))
     z = lax.axis_index("z")
     where = jnp.stack(
-        [lengths[0], lax.axis_index("c"), lax.axis_index("xh"), z & 1, z >> 1 & 1]
+        [lengths[0], lax.axis_index("c"), z & 1, z >> 1 & 1, lax.axis_index("xh")]
     )
     query, d_out, masked, resp_keys = call(
         query_kernel,
@@ -285,6 +315,17 @@
     )
     own, query = lax.optimization_barrier((own, query))
     other = lax.ppermute(own, "c", swap)
+    first_scores, first_d_attention = call(
+        first_scores_kernel,
+        [((HALF + RESP, ROWS), F32)] * 2,
+        where,
+        query,
+        d_out,
+        own,
+        resp_keys,
+        scalars=1,
+        flops=2_000_000_000,
+    )
     keep_resp, send_resp, attention, d_scores, keys = call(
         attention_kernel,
         [
@@ -300,15 +341,17 @@
         own,
         other,
         resp_keys,
+        first_scores,
+        first_d_attention,
         scalars=1,
         flops=4_000_000_000,
     )
-    got_resp = lax.ppermute(send_resp, "xh", swap)
-    d_query, keep, send = call(
-        grads_kernel,
+    got_resp = lax.ppermute(send_resp, "z", [(i, i ^ 1) for i in range(8)])
+    d_query, out_latent, send = call(
+        send_kernel,
         [
             ((EXT, ROWS), BF16),
-            ((CHIPS, PAGE, WIDE), BF16),
+            ((DC, ROWS), BF16),
             ((CHIPS, PAGE, WIDE), BF16),
         ],
         where,
@@ -321,10 +364,21 @@
         d_scores,
         scalars=1,
         flops=4_000_000_000,
-        scratch=[
-            pltpu.VMEM((DC, 2 * LOCAL * DN), BF16),
-            pltpu.VMEM((2 * HALF, EXT), BF16),
-        ],
+    )
+    (keep,) = call(
+        keep_kernel,
+        [((CHIPS, PAGE, WIDE), BF16)],
+        where,
+        q_nope,
+        masked,
+        query,
+        d_out,
+        attention,
+        d_scores,
+        d_query,
+        out_latent,
+        scalars=1,
+        flops=2_000_000_000,
     )
     chip_sum = keep + lax.ppermute(send, "c", swap)
     sample_parts = spread(chip_sum, ("xl", "y"))
@@ -335,27 +389,36 @@
         w_key_up,
         flops=1_000_000_000,
     )
-    for bit in range(2):
-        half = keep_resp.shape[0] // 2
-        keep_resp, send_resp = call(
-            functools.partial(halve_kernel, 3 + bit),
-            [((half, PAGE, EXT), BF16)] * 2,
-            where,
-            keep_resp,
-            got_resp,
-            scalars=1,
-        )
-        got_resp = lax.ppermute(send_resp, "z", [(i, i ^ (1 << bit)) for i in range(8)])
-    d_key_up, d_value_up, line = call(
-        middle_kernel,
-        [
-            ((PAGE, LOCAL * DN), F32),
-            ((PAGE, LOCAL * DV), F32),
-            ((CHIPS, PAGE, 2 * EXT), BF16),
-        ],
+    keep_resp, send_resp = call(
+        functools.partial(halve_kernel, 3),
+        [((2, PAGE, EXT), BF16)] * 2,
+        where,
+        keep_resp,
+        got_resp,
+        scalars=1,
+    )
+    got_resp = lax.ppermute(send_resp, "z", [(i, i ^ 2) for i in range(8)])
+    keep_resp, send_resp = call(
+        functools.partial(halve_kernel, 4),
+        [((1, PAGE, EXT), BF16)] * 2,
+        where,
+        keep_resp,
+        got_resp,
+        scalars=1,
+    )
+    got_resp = lax.ppermute(send_resp, "xh", swap)
+    (line,) = call(
+        line_kernel,
+        [((CHIPS, PAGE, 2 * KEY), BF16)],
         sample_parts,
         keep_resp,
         got_resp,
+    )
+    d_key_up, d_value_up = call(
+        weights_kernel,
+        [((PAGE, LOCAL * DN), F32), ((PAGE, LOCAL * DV), F32)],
+        sample_parts,
+        flops=1_000_000_000,
     )
     lines = spread(line, HEAD)
     d_prompt, d_prompt_rope, d_resp, d_resp_rope_t = call(

time: 99.9 us -> 96.5 us (0.966)
  waiting for transfers between devices: 38.8 us -> 32.3 us
  Pallas kernels: 10.9 us -> 14.1 us
  local copies, waits for them, and re-layouts: 2.55 us -> 1.16 us
  starting transfers between devices: 44.4 us -> 45.6 us
    ppermute x1, waiting for transfers between devices: 6.13 us -> 2.53 us  [body(): got_resp = lax.ppermute(send_resp, 'xh', swap)]
    pallas_call x9 -> x12, Pallas kernels: 10.9 us -> 14.1 us  [call(): pl.pallas_call(kernel, out_shape=[jax.ShapeDtypeStruct(shape, kind) for s...]
    ppermute x1, waiting for transfers between devices: 1.59 us -> 0.17 us  [body(): other = lax.ppermute(own, 'c', swap)]
    unnamed x20 -> x16, local copies, waits for them, and re-layouts: 2.47 us -> 1.07 us
    ppermute x1, waiting for transfers between devices: 2.22 us -> 0.83 us  [body(): chip_sum = keep + lax.ppermute(send, 'c', swap)]
  transfers between devices with their start and end apart: 8 -> 8, of which waited for: 7 -> 7; matrix products, arithmetic and copies ran while one was open for 0% -> 0% of each run, Pallas kernels for 3% -> 7%
where the time goes in v3:
time: 96.5 us; the launch traced here: 95.9 us
  starting transfers between devices  45.6 us (47%)
  waiting for transfers between devices  32.3 us (33%)
  Pallas kernels  14.1 us (15%)
  between operations  1.5 us (2%)
  local copies, waits for them, and re-layouts  1.16 us (1%)
  other arithmetic  1.13 us (1%)
    all_to_all x3, starting transfers between devices, spread(): return lax.all_to_all(parts, axes, 0, 0, tiled=True)  26.5 us
    all_to_all x3, waiting for transfers between devices, spread(): return lax.all_to_all(parts, axes, 0, 0, tiled=True)  24.3 us
    pallas_call x12, Pallas kernels, call(): pl.pallas_call(kernel, out_shape=[jax.ShapeDtypeStruct(shape, kind) for s...  14.1 us
    ppermute x1, starting transfers between devices, body(): got_resp = lax.ppermute(send_resp, 'z', [(i, i ^ 2) for i in range(8)])  6.1 us
    ppermute x1, starting transfers between devices, body(): got_resp = lax.ppermute(send_resp, 'xh', swap)  4.64 us
    ppermute x1, starting transfers between devices, body(): got_resp = lax.ppermute(send_resp, 'z', [(i, i ^ 1) for i in range(8)])  4.27 us
    ppermute x1, waiting for transfers between devices, body(): got_resp = lax.ppermute(send_resp, 'xh', swap)  2.53 us
    ppermute x1, waiting for transfers between devices, body(): got_resp = lax.ppermute(send_resp, 'z', [(i, i ^ 1) for i in range(8)])  2.4 us
  transfers between devices with their start and end apart: 8, of which 7 were waited for; matrix products, arithmetic and copies ran while one was open for 0% of the time, Pallas kernels for 7%

profile of v3, /device:TPU:24, one launch (start us, length us, event | category | flops | bytes accessed | tf_op | source)
XLA Modules:
  0.0 95.9 jit_solution(11796485641659685543)
XLA Ops:
  0.6 1.5 %shard_map.162 = bf16[16,16,640]{2,1,0:T(8,128)(2,1)} custom-call(bf16[16,512]{1,0:T(8,128)(2,1)} %latent_far.1, bf16[16,64]{1,0:T(8,128)(2,1)} %bitcast.6), custom_call_target="tpu_custom_call" | custom-call | tf_op jit(solution)/shard_map/pallas_call | solution.py:252
  2.2 9.1 %all-to-all-start = ((bf16[16,16,640]{2,1,0:T(8,128)(2,1)}), bf16[16,16,640]{2,1,0:T(8,128)(2,1)S(1)}, u32[]{:S(2)}, u32[]{:S(2)}) async-start(bf16[16,16,640]{2,1,0:T(8,128)(2,1)} %shard_map.162), calls=%async_computation | async-start | bytes 655360 | tf_op jit(solution)/shard_map/all_to_all | solution.py:264
  12.1 1.0 %copy-done.1 = bf16[512,512]{1,0:T(8,128)(2,1)S(1)} copy-done((bf16[512,512]{1,0:T(8,128)(2,1)S(1)}, bf16[512,512]{1,0:T(8,128)(2,1)}, u32[]{:S(2)}) %copy-start.1) | copy-done | bytes 524312
  13.2 1.0 %shard_map.161 = (bf16[512,640]{1,0:T(8,128)(2,1)S(1)}, bf16[512,512]{1,0:T(8,128)(2,1)S(1)}, bf16[128,512]{1,0:T(8,128)(2,1)S(1)}, bf16[128,640]{1,0:T(8,128)(2,1)S(1)}) custom-call(s32[5]{0:T(128)S(1)} %stack.19.where, bf16[128,512]{1,0:T(8,128)(2,1)S(1)} %copy-done.5, bf16[128,256]{1,0:T(8,128)(2,1)S(1)} %copy-done.6, bf16[128,512]{1,0:T(8,128)(2,1)S(1)} %copy-done.3, ...), custom_call_target="tpu_custom_call" | custom-call | flops 4000000000 | tf_op jit(solution)/shard_map/pallas_call | solution.py:252
  14.2 6.5 %all-to-all-done.own = bf16[16,16,640]{2,1,0:T(8,128)(2,1)S(1)} async-done(((bf16[16,16,640]{2,1,0:T(8,128)(2,1)}), bf16[16,16,640]{2,1,0:T(8,128)(2,1)S(1)}, u32[]{:S(2)}, u32[]{:S(2)}) %all-to-all-start) | async-done | bytes 327712 | tf_op jit(solution)/shard_map/all_to_all | solution.py:264
  20.7 1.9 %collective-permute-start = (bf16[16,16,640]{2,1,0:T(8,128)(2,1)S(1)}, bf16[16,16,640]{2,1,0:T(8,128)(2,1)S(1)}, u32[]{:S(2)}, u32[]{:S(2)}) collective-permute-start(bf16[16,16,640]{2,1,0:T(8,128)(2,1)S(1)} %all-to-all-done.own), channel_id=1, source_target_pairs={{0,16},{16,0},{1,17},{17,1},{2,18},{18,2},{3,19},{19,3},{4,20},{20... | collective-permute-start | bytes 983048 | tf_op jit(solution)/shard_map/ppermute | solution.py:317
  22.6 1.4 %shard_map.163 = (f32[384,512]{1,0:T(8,128)S(1)}, f32[384,512]{1,0:T(8,128)S(1)}) custom-call(s32[5]{0:T(128)S(1)} %stack.19.where, bf16[512,640]{1,0:T(8,128)(2,1)S(1)} %get-tuple-element.38.query, bf16[512,512]{1,0:T(8,128)(2,1)S(1)} %get-tuple-element.39.d_out, bf16[16,16,640]{2,1,0:T(8,128)(2,1)S(1)} %all-to-all-done.own, ...), custom_call_target="tpu_custom_call" | custom-call | flops 2000000000 | tf_op jit(solution)/shard_map/pallas_call | solution.py:252
  24.2 2.1 %shard_map.164 = (bf16[4,16,640]{2,1,0:T(8,128)(2,1)S(1)}, bf16[4,16,640]{2,1,0:T(8,128)(2,1)S(1)}, bf16[640,512]{1,0:T(8,128)(2,1)S(1)}, bf16[640,512]{1,0:T(8,128)(2,1)S(1)}, bf16[640,640]{1,0:T(8,128)(2,1)S(1)}) custom-call(s32[5]{0:T(128)S(1)} %stack.19.where, bf16[512,640]{1,0:T(8,128)(2,1)S(1)} %get-tuple-element.38.query, ...), custom_call_target="tpu_custom_call" | custom-call | flops 4000000000 | tf_op jit(solution)/shard_map/pallas_call | solution.py:252
  26.3 2.3 %shard_map.165 = (bf16[640,512]{1,0:T(8,128)(2,1)S(1)}, bf16[512,512]{1,0:T(8,128)(2,1)S(1)}, bf16[16,16,1664]{2,1,0:T(8,128)(2,1)S(1)}) custom-call(s32[5]{0:T(128)S(1)} %stack.19.where, bf16[128,512]{1,0:T(8,128)(2,1)S(1)} %copy-done.5, bf16[128,512]{1,0:T(8,128)(2,1)S(1)} %get-tuple-element.36.masked, bf16[512,640]{1,0:T(8,128)(2,1)S(1)} %get-tuple-element.38.query, ...), custom_call_target="tpu_custom_call" | custom-call | flops 4000000000 | tf_op jit(solution)/shard_map/pallas_call | solution.py:252
  28.6 2.2 %collective-permute-start.1 = (bf16[16,16,1664]{2,1,0:T(8,128)(2,1)S(1)}, bf16[16,16,1664]{2,1,0:T(8,128)(2,1)S(1)}, u32[]{:S(2)}, u32[]{:S(2)}) collective-permute-start(bf16[16,16,1664]{2,1,0:T(8,128)(2,1)S(1)} %get-tuple-element.51), channel_id=1, source_target_pairs={{0,16},{16,0},{1,17},{17,1},{2,18},{18,2},{3,19},{19,3},{4,20},{20... | collective-permute-start | bytes 2555912 | tf_op jit(solution)/shard_map/ppermute | solution.py:383
  30.8 1.2 %shard_map.167 = bf16[16,16,1664]{2,1,0:T(8,128)(2,1)S(1)} custom-call(s32[5]{0:T(128)S(1)} %stack.19.where, bf16[128,512]{1,0:T(8,128)(2,1)S(1)} %copy-done.5, bf16[128,512]{1,0:T(8,128)(2,1)S(1)} %get-tuple-element.36.masked, bf16[512,640]{1,0:T(8,128)(2,1)S(1)} %get-tuple-element.38.query, bf16[512,512]{1,0:T(8,128)(2,1)S(1)} %get-tuple-element.39.d_out, ...), custom_call_target="tpu_custom_call" | custom-call | flops 2000000000 | tf_op jit(solution)/shard_map/pallas_call | solution.py:252
  32.0 0.8 collective-permute-done.1
  32.9 1.1 %add.3 = bf16[16,16,1664]{2,1,0:T(8,128)(2,1)} add(bf16[16,16,1664]{2,1,0:T(8,128)(2,1)S(1)} %shard_map.167, bf16[16,16,1664]{2,1,0:T(8,128)(2,1)S(1)} %collective-permute-done.1) | non-fusion elementwise | flops 425984 | bytes 2555904 | tf_op jit(solution)/shard_map/add | solution.py:383
  34.0 6.0 %all-to-all-start.1 = ((bf16[16,16,1664]{2,1,0:T(8,128)(2,1)}), bf16[16,16,1664]{2,1,0:T(8,128)(2,1)S(1)}, u32[]{:S(2)}, u32[]{:S(2)}) async-start(bf16[16,16,1664]{2,1,0:T(8,128)(2,1)} %add.3), calls=%async_computation.1 | async-start | bytes 1703936 | tf_op jit(solution)/shard_map/all_to_all | solution.py:264
  40.0 4.3 %collective-permute-start.2 = (bf16[4,16,640]{2,1,0:T(8,128)(2,1)S(1)}, bf16[4,16,640]{2,1,0:T(8,128)(2,1)S(1)}, u32[]{:S(2)}, u32[]{:S(2)}) collective-permute-start(bf16[4,16,640]{2,1,0:T(8,128)(2,1)S(1)} %get-tuple-element.55), channel_id=1, source_target_pairs={{0,2},{2,0},{4,6},{6,4},{8,10},{10,8},{12,14},{14,12},{1,3},{3,1},... | collective-permute-start | bytes 245768 | tf_op jit(solution)/shard_map/ppermute | solution.py:349
  44.3 2.4 %collective-permute-done.2.received = bf16[4,16,640]{2,1,0:T(8,128)(2,1)S(1)} collective-permute-done((bf16[4,16,640]{2,1,0:T(8,128)(2,1)S(1)}, bf16[4,16,640]{2,1,0:T(8,128)(2,1)S(1)}, u32[]{:S(2)}, u32[]{:S(2)}) %collective-permute-start.2) | collective-permute-done | bytes 81952 | tf_op jit(solution)/shard_map/ppermute | solution.py:349
  47.2 6.1 %collective-permute-start.3 = (bf16[2,16,640]{2,1,0:T(8,128)(2,1)S(1)}, bf16[2,16,640]{2,1,0:T(8,128)(2,1)S(1)}, u32[]{:S(2)}, u32[]{:S(2)}) collective-permute-start(bf16[2,16,640]{2,1,0:T(8,128)(2,1)S(1)} %get-tuple-element.57), channel_id=1, source_target_pairs={{0,4},{2,6},{4,0},{6,2},{8,12},{10,14},{12,8},{14,10},{1,5},{3,7},... | collective-permute-start | bytes 122888 | tf_op jit(solution)/shard_map/ppermute | solution.py:400
  53.3 2.1 %collective-permute-done.3.received = bf16[2,16,640]{2,1,0:T(8,128)(2,1)S(1)} collective-permute-done((bf16[2,16,640]{2,1,0:T(8,128)(2,1)S(1)}, bf16[2,16,640]{2,1,0:T(8,128)(2,1)S(1)}, u32[]{:S(2)}, u32[]{:S(2)}) %collective-permute-start.3) | collective-permute-done | bytes 40992 | tf_op jit(solution)/shard_map/ppermute | solution.py:400
  56.0 4.6 %collective-permute-start.4 = (bf16[1,16,640]{2,1,0:T(8,128)(2,1)S(1)}, bf16[1,16,640]{2,1,0:T(8,128)(2,1)S(1)}, u32[]{:S(2)}, u32[]{:S(2)}) collective-permute-start(bf16[1,16,640]{2,1,0:T(8,128)(2,1)S(1)} %get-tuple-element.59), channel_id=1, source_target_pairs={{0,1},{1,0},{2,3},{3,2},{4,5},{5,4},{6,7},{7,6},{8,9},{9,8},{10,11... | collective-permute-start | bytes 61448 | tf_op jit(solution)/shard_map/ppermute | solution.py:409
  60.6 2.5 %collective-permute-done.4.received = bf16[1,16,640]{2,1,0:T(8,128)(2,1)S(1)} collective-permute-done((bf16[1,16,640]{2,1,0:T(8,128)(2,1)S(1)}, bf16[1,16,640]{2,1,0:T(8,128)(2,1)S(1)}, u32[]{:S(2)}, u32[]{:S(2)}) %collective-permute-start.4) | collective-permute-done | bytes 20512 | tf_op jit(solution)/shard_map/ppermute | solution.py:409
  63.2 1.0 %shard_map.171 = bf16[16,16,1152]{2,1,0:T(8,128)(2,1)} custom-call(bf16[16,16,1664]{2,1,0:T(8,128)(2,1)S(1)} %all-to-all-done.1.sample_parts, bf16[1,16,640]{2,1,0:T(8,128)(2,1)S(1)} %get-tuple-element.58.kept, bf16[1,16,640]{2,1,0:T(8,128)(2,1)S(1)} %collective-permute-done.4.received), custom_call_target="tpu_custom_call" | custom-call | tf_op jit(solution)/shard_map/pallas_call | solution.py:252
  64.2 11.4 %all-to-all-start.2 = ((bf16[16,16,1152]{2,1,0:T(8,128)(2,1)}), bf16[16,16,1152]{2,1,0:T(8,128)(2,1)S(1)}, u32[]{:S(2)}, u32[]{:S(2)}) async-start(bf16[16,16,1152]{2,1,0:T(8,128)(2,1)} %shard_map.171), calls=%async_computation.2 | async-start | bytes 1179648 | tf_op jit(solution)/shard_map/all_to_all | solution.py:264
  75.6 1.0 %shard_map.166 = (bf16[128,512]{1,0:T(8,128)(2,1)}, bf16[128,256]{1,0:T(8,128)(2,1)}) custom-call(bf16[640,512]{1,0:T(8,128)(2,1)S(1)} %get-tuple-element.47.d_query, bf16[512,512]{1,0:T(8,128)(2,1)S(1)} %copy-done.2), custom_call_target="tpu_custom_call" | custom-call | flops 1000000000 | tf_op jit(solution)/shard_map/pallas_call | solution.py:252
  77.3 17.7 %all-to-all-done.2.parts = bf16[16,16,1152]{2,1,0:T(8,128)(2,1)S(1)} async-done(((bf16[16,16,1152]{2,1,0:T(8,128)(2,1)}), bf16[16,16,1152]{2,1,0:T(8,128)(2,1)S(1)}, u32[]{:S(2)}, u32[]{:S(2)}) %all-to-all-start.2) | async-done | bytes 589856 | tf_op jit(solution)/shard_map/all_to_all | solution.py:264
  (22 shorter events, 2.9 us)
Async XLA Ops:
  0.6 11.4 %copy-start = (bf16[512,512]{1,0:T(8,128)(2,1)S(1)}, bf16[512,512]{1,0:T(8,128)(2,1)}, u32[]{:S(2)}) copy-start(bf16[512,512]{1,0:T(8,128)(2,1)} %w_value.1) | copy-start | bytes 1572868
  2.2 9.9 %copy-start.3 = (bf16[128,512]{1,0:T(8,128)(2,1)S(1)}, bf16[128,512]{1,0:T(8,128)(2,1)}, u32[]{:S(2)}) copy-start(bf16[128,512]{1,0:T(8,128)(2,1)} %grad.1) | copy-start | bytes 393220
  2.2 9.9 %copy-start.4 = (bf16[128,512]{1,0:T(8,128)(2,1)S(1)}, bf16[128,512]{1,0:T(8,128)(2,1)}, u32[]{:S(2)}) copy-start(bf16[128,512]{1,0:T(8,128)(2,1)} %resp_latent.1) | copy-start | bytes 393220
  2.2 9.9 %copy-start.5 = (bf16[128,512]{1,0:T(8,128)(2,1)S(1)}, bf16[128,512]{1,0:T(8,128)(2,1)}, u32[]{:S(2)}) copy-start(bf16[128,512]{1,0:T(8,128)(2,1)} %q_nope.5) | copy-start | bytes 393220
  2.2 9.9 %copy-start.6 = (bf16[128,256]{1,0:T(8,128)(2,1)S(1)}, bf16[128,256]{1,0:T(8,128)(2,1)}, u32[]{:S(2)}) copy-start(bf16[128,256]{1,0:T(8,128)(2,1)} %q_rope.1) | copy-start | bytes 196612
  2.2 18.5 %all-to-all-start = ((bf16[16,16,640]{2,1,0:T(8,128)(2,1)}), bf16[16,16,640]{2,1,0:T(8,128)(2,1)S(1)}, u32[]{:S(2)}, u32[]{:S(2)}) async-start(bf16[16,16,640]{2,1,0:T(8,128)(2,1)} %shard_map.162), calls=%async_computation | async-start | bytes 655360 | tf_op jit(solution)/shard_map/all_to_all | solution.py:264
  11.3 0.8 copy-start.7
  12.1 1.0 %copy-start.1 = (bf16[512,512]{1,0:T(8,128)(2,1)S(1)}, bf16[512,512]{1,0:T(8,128)(2,1)}, u32[]{:S(2)}) copy-start(bf16[512,512]{1,0:T(8,128)(2,1)} %w_key.3) | copy-start | bytes 1572868
  20.7 3.5 %collective-permute-start = (bf16[16,16,640]{2,1,0:T(8,128)(2,1)S(1)}, bf16[16,16,640]{2,1,0:T(8,128)(2,1)S(1)}, u32[]{:S(2)}, u32[]{:S(2)}) collective-permute-start(bf16[16,16,640]{2,1,0:T(8,128)(2,1)S(1)} %all-to-all-done.own), channel_id=1, source_target_pairs={{0,16},{16,0},{1,17},{17,1},{2,18},{18,2},{3,19},{19,3},{4,20},{20... | collective-permute-start | bytes 983048 | tf_op jit(solution)/shard_map/ppermute | solution.py:317
  28.6 4.3 %collective-permute-start.1 = (bf16[16,16,1664]{2,1,0:T(8,128)(2,1)S(1)}, bf16[16,16,1664]{2,1,0:T(8,128)(2,1)S(1)}, u32[]{:S(2)}, u32[]{:S(2)}) collective-permute-start(bf16[16,16,1664]{2,1,0:T(8,128)(2,1)S(1)} %get-tuple-element.51), channel_id=1, source_target_pairs={{0,16},{16,0},{1,17},{17,1},{2,18},{18,2},{3,19},{19,3},{4,20},{20... | collective-permute-start | bytes 2555912 | tf_op jit(solution)/shard_map/ppermute | solution.py:383
  34.0 29.2 %all-to-all-start.1 = ((bf16[16,16,1664]{2,1,0:T(8,128)(2,1)}), bf16[16,16,1664]{2,1,0:T(8,128)(2,1)S(1)}, u32[]{:S(2)}, u32[]{:S(2)}) async-start(bf16[16,16,1664]{2,1,0:T(8,128)(2,1)} %add.3), calls=%async_computation.1 | async-start | bytes 1703936 | tf_op jit(solution)/shard_map/all_to_all | solution.py:264
  40.0 6.7 %collective-permute-start.2 = (bf16[4,16,640]{2,1,0:T(8,128)(2,1)S(1)}, bf16[4,16,640]{2,1,0:T(8,128)(2,1)S(1)}, u32[]{:S(2)}, u32[]{:S(2)}) collective-permute-start(bf16[4,16,640]{2,1,0:T(8,128)(2,1)S(1)} %get-tuple-element.55), channel_id=1, source_target_pairs={{0,2},{2,0},{4,6},{6,4},{8,10},{10,8},{12,14},{14,12},{1,3},{3,1},... | collective-permute-start | bytes 245768 | tf_op jit(solution)/shard_map/ppermute | solution.py:349
  47.2 8.2 %collective-permute-start.3 = (bf16[2,16,640]{2,1,0:T(8,128)(2,1)S(1)}, bf16[2,16,640]{2,1,0:T(8,128)(2,1)S(1)}, u32[]{:S(2)}, u32[]{:S(2)}) collective-permute-start(bf16[2,16,640]{2,1,0:T(8,128)(2,1)S(1)} %get-tuple-element.57), channel_id=1, source_target_pairs={{0,4},{2,6},{4,0},{6,2},{8,12},{10,14},{12,8},{14,10},{1,5},{3,7},... | collective-permute-start | bytes 122888 | tf_op jit(solution)/shard_map/ppermute | solution.py:400
  56.0 7.2 %collective-permute-start.4 = (bf16[1,16,640]{2,1,0:T(8,128)(2,1)S(1)}, bf16[1,16,640]{2,1,0:T(8,128)(2,1)S(1)}, u32[]{:S(2)}, u32[]{:S(2)}) collective-permute-start(bf16[1,16,640]{2,1,0:T(8,128)(2,1)S(1)} %get-tuple-element.59), channel_id=1, source_target_pairs={{0,1},{1,0},{2,3},{3,2},{4,5},{5,4},{6,7},{7,6},{8,9},{9,8},{10,11... | collective-permute-start | bytes 61448 | tf_op jit(solution)/shard_map/ppermute | solution.py:409
  64.2 11.4 %copy-start.2 = (bf16[512,512]{1,0:T(8,128)(2,1)S(1)}, bf16[512,512]{1,0:T(8,128)(2,1)}, u32[]{:S(2)}) copy-start(bf16[512,512]{1,0:T(8,128)(2,1)} %w_key.3) | copy-start | bytes 1572868
  64.2 30.9 %all-to-all-start.2 = ((bf16[16,16,1152]{2,1,0:T(8,128)(2,1)}), bf16[16,16,1152]{2,1,0:T(8,128)(2,1)S(1)}, u32[]{:S(2)}, u32[]{:S(2)}) async-start(bf16[16,16,1152]{2,1,0:T(8,128)(2,1)} %shard_map.171), calls=%async_computation.2 | async-start | bytes 1179648 | tf_op jit(solution)/shard_map/all_to_all | solution.py:264

commit v4 on v3

--- a/solution.py
+++ b/solution.py
@@ -21,7 +21,7 @@
 HALF = CHIPS * PAGE
 KEYS = 2 * HALF + RESP
 WIDE = 2 * LOCAL * DN + EXT
-OWNERS = [1 * (b & 1) + 4 * (b >> 1 & 1) + 2 * (b >> 2 & 1) for b in range(RESP // PAGE)]
+OWNERS = [8 * (b & 1) + 2 * (b >> 1 & 1) + (b >> 2 & 1) for b in range(RESP // PAGE)]
 SCALE = (DN + DR) ** (-0.5)
 F32 = jnp.float32
 BF16 = jnp.bfloat16
@@ -239,7 +239,7 @@
     d_prompt[...] = page[:, KEY : KEY + DC]
     d_prompt_rope[...] = page[:, KEY + DC : 2 * KEY]
     rows = jnp.concatenate(
-        [parts[g, :, 0:KEY].astype(F32) + parts[g + 8, :, 0:KEY].astype(F32) for g in OWNERS],
+        [parts[g, :, 0:KEY].astype(F32) + parts[g + 4, :, 0:KEY].astype(F32) for g in OWNERS],
         axis=0,
     )
     d_resp[...] = rows[:, 0:DC]
@@ -420,7 +420,7 @@
         sample_parts,
         flops=1_000_000_000,
     )
-    lines = spread(line, HEAD)
+    lines = spread(line, ("xh", "z"))
     d_prompt, d_prompt_rope, d_resp, d_resp_rope_t = call(
         last_kernel,
         [

time: 96.5 us -> 94.4 us (0.978)
  the two profiles are of different devices: /device:TPU:24 before, /device:TPU:16 now
where the time goes in v4:
time: 94.4 us; the launch traced here: 93.8 us
  starting transfers between devices  45.2 us (48%)
  waiting for transfers between devices  30.7 us (33%)
  Pallas kernels  14.1 us (15%)
  between operations  1.5 us (2%)
  local copies, waits for them, and re-layouts  1.16 us (1%)
  other arithmetic  1.13 us (1%)
    all_to_all x3, starting transfers between devices, spread(): return lax.all_to_all(parts, axes, 0, 0, tiled=True)  26 us
    all_to_all x3, waiting for transfers between devices, spread(): return lax.all_to_all(parts, axes, 0, 0, tiled=True)  22.6 us
    pallas_call x12, Pallas kernels, call(): pl.pallas_call(kernel, out_shape=[jax.ShapeDtypeStruct(shape, kind) for s...  14.1 us
    ppermute x1, starting transfers between devices, body(): got_resp = lax.ppermute(send_resp, 'z', [(i, i ^ 2) for i in range(8)])  6.1 us
    ppermute x1, starting transfers between devices, body(): got_resp = lax.ppermute(send_resp, 'xh', swap)  4.64 us
    ppermute x1, starting transfers between devices, body(): got_resp = lax.ppermute(send_resp, 'z', [(i, i ^ 1) for i in range(8)])  4.27 us
    ppermute x1, waiting for transfers between devices, body(): got_resp = lax.ppermute(send_resp, 'xh', swap)  2.53 us
    ppermute x1, waiting for transfers between devices, body(): got_resp = lax.ppermute(send_resp, 'z', [(i, i ^ 1) for i in range(8)])  2.4 us
  transfers between devices with their start and end apart: 8, of which 7 were waited for; matrix products, arithmetic and copies ran while one was open for 0% of the time, Pallas kernels for 7%

profile of v4, /device:TPU:16, one launch (start us, length us, event | category | flops | bytes accessed | tf_op | source)
XLA Modules:
  0.0 93.8 jit_solution(8416235792857595963)
XLA Ops:
  0.6 1.5 %shard_map.162 = bf16[16,16,640]{2,1,0:T(8,128)(2,1)} custom-call(bf16[16,512]{1,0:T(8,128)(2,1)} %latent_far.1, bf16[16,64]{1,0:T(8,128)(2,1)} %bitcast.6), custom_call_target="tpu_custom_call" | custom-call | tf_op jit(solution)/shard_map/pallas_call | solution.py:252
  2.2 9.2 %all-to-all-start = ((bf16[16,16,640]{2,1,0:T(8,128)(2,1)}), bf16[16,16,640]{2,1,0:T(8,128)(2,1)S(1)}, u32[]{:S(2)}, u32[]{:S(2)}) async-start(bf16[16,16,640]{2,1,0:T(8,128)(2,1)} %shard_map.162), calls=%async_computation | async-start | bytes 655360 | tf_op jit(solution)/shard_map/all_to_all | solution.py:264
  12.2 1.0 %copy-done.1 = bf16[512,512]{1,0:T(8,128)(2,1)S(1)} copy-done((bf16[512,512]{1,0:T(8,128)(2,1)S(1)}, bf16[512,512]{1,0:T(8,128)(2,1)}, u32[]{:S(2)}) %copy-start.1) | copy-done | bytes 524312
  13.3 1.0 %shard_map.161 = (bf16[512,640]{1,0:T(8,128)(2,1)S(1)}, bf16[512,512]{1,0:T(8,128)(2,1)S(1)}, bf16[128,512]{1,0:T(8,128)(2,1)S(1)}, bf16[128,640]{1,0:T(8,128)(2,1)S(1)}) custom-call(s32[5]{0:T(128)S(1)} %stack.19.where, bf16[128,512]{1,0:T(8,128)(2,1)S(1)} %copy-done.5, bf16[128,256]{1,0:T(8,128)(2,1)S(1)} %copy-done.6, bf16[128,512]{1,0:T(8,128)(2,1)S(1)} %copy-done.3, ...), custom_call_target="tpu_custom_call" | custom-call | flops 4000000000 | tf_op jit(solution)/shard_map/pallas_call | solution.py:252
  14.3 7.1 %all-to-all-done.own = bf16[16,16,640]{2,1,0:T(8,128)(2,1)S(1)} async-done(((bf16[16,16,640]{2,1,0:T(8,128)(2,1)}), bf16[16,16,640]{2,1,0:T(8,128)(2,1)S(1)}, u32[]{:S(2)}, u32[]{:S(2)}) %all-to-all-start) | async-done | bytes 327712 | tf_op jit(solution)/shard_map/all_to_all | solution.py:264
  21.3 1.9 %collective-permute-start = (bf16[16,16,640]{2,1,0:T(8,128)(2,1)S(1)}, bf16[16,16,640]{2,1,0:T(8,128)(2,1)S(1)}, u32[]{:S(2)}, u32[]{:S(2)}) collective-permute-start(bf16[16,16,640]{2,1,0:T(8,128)(2,1)S(1)} %all-to-all-done.own), channel_id=1, source_target_pairs={{0,16},{16,0},{1,17},{17,1},{2,18},{18,2},{3,19},{19,3},{4,20},{20... | collective-permute-start | bytes 983048 | tf_op jit(solution)/shard_map/ppermute | solution.py:317
  23.3 1.4 %shard_map.163 = (f32[384,512]{1,0:T(8,128)S(1)}, f32[384,512]{1,0:T(8,128)S(1)}) custom-call(s32[5]{0:T(128)S(1)} %stack.19.where, bf16[512,640]{1,0:T(8,128)(2,1)S(1)} %get-tuple-element.38.query, bf16[512,512]{1,0:T(8,128)(2,1)S(1)} %get-tuple-element.39.d_out, bf16[16,16,640]{2,1,0:T(8,128)(2,1)S(1)} %all-to-all-done.own, ...), custom_call_target="tpu_custom_call" | custom-call | flops 2000000000 | tf_op jit(solution)/shard_map/pallas_call | solution.py:252
  24.8 2.1 %shard_map.164 = (bf16[4,16,640]{2,1,0:T(8,128)(2,1)S(1)}, bf16[4,16,640]{2,1,0:T(8,128)(2,1)S(1)}, bf16[640,512]{1,0:T(8,128)(2,1)S(1)}, bf16[640,512]{1,0:T(8,128)(2,1)S(1)}, bf16[640,640]{1,0:T(8,128)(2,1)S(1)}) custom-call(s32[5]{0:T(128)S(1)} %stack.19.where, bf16[512,640]{1,0:T(8,128)(2,1)S(1)} %get-tuple-element.38.query, ...), custom_call_target="tpu_custom_call" | custom-call | flops 4000000000 | tf_op jit(solution)/shard_map/pallas_call | solution.py:252
  27.0 2.3 %shard_map.165 = (bf16[640,512]{1,0:T(8,128)(2,1)S(1)}, bf16[512,512]{1,0:T(8,128)(2,1)S(1)}, bf16[16,16,1664]{2,1,0:T(8,128)(2,1)S(1)}) custom-call(s32[5]{0:T(128)S(1)} %stack.19.where, bf16[128,512]{1,0:T(8,128)(2,1)S(1)} %copy-done.5, bf16[128,512]{1,0:T(8,128)(2,1)S(1)} %get-tuple-element.36.masked, bf16[512,640]{1,0:T(8,128)(2,1)S(1)} %get-tuple-element.38.query, ...), custom_call_target="tpu_custom_call" | custom-call | flops 4000000000 | tf_op jit(solution)/shard_map/pallas_call | solution.py:252
  29.2 2.2 %collective-permute-start.1 = (bf16[16,16,1664]{2,1,0:T(8,128)(2,1)S(1)}, bf16[16,16,1664]{2,1,0:T(8,128)(2,1)S(1)}, u32[]{:S(2)}, u32[]{:S(2)}) collective-permute-start(bf16[16,16,1664]{2,1,0:T(8,128)(2,1)S(1)} %get-tuple-element.51), channel_id=1, source_target_pairs={{0,16},{16,0},{1,17},{17,1},{2,18},{18,2},{3,19},{19,3},{4,20},{20... | collective-permute-start | bytes 2555912 | tf_op jit(solution)/shard_map/ppermute | solution.py:383
  31.5 1.2 %shard_map.167 = bf16[16,16,1664]{2,1,0:T(8,128)(2,1)S(1)} custom-call(s32[5]{0:T(128)S(1)} %stack.19.where, bf16[128,512]{1,0:T(8,128)(2,1)S(1)} %copy-done.5, bf16[128,512]{1,0:T(8,128)(2,1)S(1)} %get-tuple-element.36.masked, bf16[512,640]{1,0:T(8,128)(2,1)S(1)} %get-tuple-element.38.query, bf16[512,512]{1,0:T(8,128)(2,1)S(1)} %get-tuple-element.39.d_out, ...), custom_call_target="tpu_custom_call" | custom-call | flops 2000000000 | tf_op jit(solution)/shard_map/pallas_call | solution.py:252
  32.7 0.8 collective-permute-done.1
  33.5 1.1 %add.3 = bf16[16,16,1664]{2,1,0:T(8,128)(2,1)} add(bf16[16,16,1664]{2,1,0:T(8,128)(2,1)S(1)} %shard_map.167, bf16[16,16,1664]{2,1,0:T(8,128)(2,1)S(1)} %collective-permute-done.1) | non-fusion elementwise | flops 425984 | bytes 2555904 | tf_op jit(solution)/shard_map/add | solution.py:383
  34.6 5.5 %all-to-all-start.1 = ((bf16[16,16,1664]{2,1,0:T(8,128)(2,1)}), bf16[16,16,1664]{2,1,0:T(8,128)(2,1)S(1)}, u32[]{:S(2)}, u32[]{:S(2)}) async-start(bf16[16,16,1664]{2,1,0:T(8,128)(2,1)} %add.3), calls=%async_computation.1 | async-start | bytes 1703936 | tf_op jit(solution)/shard_map/all_to_all | solution.py:264
  40.1 4.3 %collective-permute-start.2 = (bf16[4,16,640]{2,1,0:T(8,128)(2,1)S(1)}, bf16[4,16,640]{2,1,0:T(8,128)(2,1)S(1)}, u32[]{:S(2)}, u32[]{:S(2)}) collective-permute-start(bf16[4,16,640]{2,1,0:T(8,128)(2,1)S(1)} %get-tuple-element.55), channel_id=1, source_target_pairs={{0,2},{2,0},{4,6},{6,4},{8,10},{10,8},{12,14},{14,12},{1,3},{3,1},... | collective-permute-start | bytes 245768 | tf_op jit(solution)/shard_map/ppermute | solution.py:349
  44.4 2.4 %collective-permute-done.2.received = bf16[4,16,640]{2,1,0:T(8,128)(2,1)S(1)} collective-permute-done((bf16[4,16,640]{2,1,0:T(8,128)(2,1)S(1)}, bf16[4,16,640]{2,1,0:T(8,128)(2,1)S(1)}, u32[]{:S(2)}, u32[]{:S(2)}) %collective-permute-start.2) | collective-permute-done | bytes 81952 | tf_op jit(solution)/shard_map/ppermute | solution.py:349
  47.4 6.1 %collective-permute-start.3 = (bf16[2,16,640]{2,1,0:T(8,128)(2,1)S(1)}, bf16[2,16,640]{2,1,0:T(8,128)(2,1)S(1)}, u32[]{:S(2)}, u32[]{:S(2)}) collective-permute-start(bf16[2,16,640]{2,1,0:T(8,128)(2,1)S(1)} %get-tuple-element.57), channel_id=1, source_target_pairs={{0,4},{2,6},{4,0},{6,2},{8,12},{10,14},{12,8},{14,10},{1,5},{3,7},... | collective-permute-start | bytes 122888 | tf_op jit(solution)/shard_map/ppermute | solution.py:400
  53.5 2.1 %collective-permute-done.3.received = bf16[2,16,640]{2,1,0:T(8,128)(2,1)S(1)} collective-permute-done((bf16[2,16,640]{2,1,0:T(8,128)(2,1)S(1)}, bf16[2,16,640]{2,1,0:T(8,128)(2,1)S(1)}, u32[]{:S(2)}, u32[]{:S(2)}) %collective-permute-start.3) | collective-permute-done | bytes 40992 | tf_op jit(solution)/shard_map/ppermute | solution.py:400
  56.1 4.6 %collective-permute-start.4 = (bf16[1,16,640]{2,1,0:T(8,128)(2,1)S(1)}, bf16[1,16,640]{2,1,0:T(8,128)(2,1)S(1)}, u32[]{:S(2)}, u32[]{:S(2)}) collective-permute-start(bf16[1,16,640]{2,1,0:T(8,128)(2,1)S(1)} %get-tuple-element.59), channel_id=1, source_target_pairs={{0,1},{1,0},{2,3},{3,2},{4,5},{5,4},{6,7},{7,6},{8,9},{9,8},{10,11... | collective-permute-start | bytes 61448 | tf_op jit(solution)/shard_map/ppermute | solution.py:409
  60.8 2.5 %collective-permute-done.4.received = bf16[1,16,640]{2,1,0:T(8,128)(2,1)S(1)} collective-permute-done((bf16[1,16,640]{2,1,0:T(8,128)(2,1)S(1)}, bf16[1,16,640]{2,1,0:T(8,128)(2,1)S(1)}, u32[]{:S(2)}, u32[]{:S(2)}) %collective-permute-start.4) | collective-permute-done | bytes 20512 | tf_op jit(solution)/shard_map/ppermute | solution.py:409
  63.3 1.0 %shard_map.171 = bf16[16,16,1152]{2,1,0:T(8,128)(2,1)} custom-call(bf16[16,16,1664]{2,1,0:T(8,128)(2,1)S(1)} %all-to-all-done.1.sample_parts, bf16[1,16,640]{2,1,0:T(8,128)(2,1)S(1)} %get-tuple-element.58.kept, bf16[1,16,640]{2,1,0:T(8,128)(2,1)S(1)} %collective-permute-done.4.received), custom_call_target="tpu_custom_call" | custom-call | tf_op jit(solution)/shard_map/pallas_call | solution.py:252
  64.3 11.4 %all-to-all-start.2 = ((bf16[16,16,1152]{2,1,0:T(8,128)(2,1)}), bf16[16,16,1152]{2,1,0:T(8,128)(2,1)S(1)}, u32[]{:S(2)}, u32[]{:S(2)}) async-start(bf16[16,16,1152]{2,1,0:T(8,128)(2,1)} %shard_map.171), calls=%async_computation.2 | async-start | bytes 1179648 | tf_op jit(solution)/shard_map/all_to_all | solution.py:264
  75.7 1.0 %shard_map.166 = (bf16[128,512]{1,0:T(8,128)(2,1)}, bf16[128,256]{1,0:T(8,128)(2,1)}) custom-call(bf16[640,512]{1,0:T(8,128)(2,1)S(1)} %get-tuple-element.47.d_query, bf16[512,512]{1,0:T(8,128)(2,1)S(1)} %copy-done.2), custom_call_target="tpu_custom_call" | custom-call | flops 1000000000 | tf_op jit(solution)/shard_map/pallas_call | solution.py:252
  77.4 15.6 %all-to-all-done.2.parts = bf16[16,16,1152]{2,1,0:T(8,128)(2,1)S(1)} async-done(((bf16[16,16,1152]{2,1,0:T(8,128)(2,1)}), bf16[16,16,1152]{2,1,0:T(8,128)(2,1)S(1)}, u32[]{:S(2)}, u32[]{:S(2)}) %all-to-all-start.2) | async-done | bytes 589856 | tf_op jit(solution)/shard_map/all_to_all | solution.py:264
  (22 shorter events, 2.9 us)
Async XLA Ops:
  0.6 11.6 %copy-start = (bf16[512,512]{1,0:T(8,128)(2,1)S(1)}, bf16[512,512]{1,0:T(8,128)(2,1)}, u32[]{:S(2)}) copy-start(bf16[512,512]{1,0:T(8,128)(2,1)} %w_value.1) | copy-start | bytes 1572868
  2.2 10.0 %copy-start.3 = (bf16[128,512]{1,0:T(8,128)(2,1)S(1)}, bf16[128,512]{1,0:T(8,128)(2,1)}, u32[]{:S(2)}) copy-start(bf16[128,512]{1,0:T(8,128)(2,1)} %grad.1) | copy-start | bytes 393220
  2.2 10.0 %copy-start.4 = (bf16[128,512]{1,0:T(8,128)(2,1)S(1)}, bf16[128,512]{1,0:T(8,128)(2,1)}, u32[]{:S(2)}) copy-start(bf16[128,512]{1,0:T(8,128)(2,1)} %resp_latent.1) | copy-start | bytes 393220
  2.2 10.0 %copy-start.5 = (bf16[128,512]{1,0:T(8,128)(2,1)S(1)}, bf16[128,512]{1,0:T(8,128)(2,1)}, u32[]{:S(2)}) copy-start(bf16[128,512]{1,0:T(8,128)(2,1)} %q_nope.5) | copy-start | bytes 393220
  2.2 10.0 %copy-start.6 = (bf16[128,256]{1,0:T(8,128)(2,1)S(1)}, bf16[128,256]{1,0:T(8,128)(2,1)}, u32[]{:S(2)}) copy-start(bf16[128,256]{1,0:T(8,128)(2,1)} %q_rope.1) | copy-start | bytes 196612
  2.2 19.1 %all-to-all-start = ((bf16[16,16,640]{2,1,0:T(8,128)(2,1)}), bf16[16,16,640]{2,1,0:T(8,128)(2,1)S(1)}, u32[]{:S(2)}, u32[]{:S(2)}) async-start(bf16[16,16,640]{2,1,0:T(8,128)(2,1)} %shard_map.162), calls=%async_computation | async-start | bytes 655360 | tf_op jit(solution)/shard_map/all_to_all | solution.py:264
  11.4 0.8 copy-start.7
  12.2 1.0 %copy-start.1 = (bf16[512,512]{1,0:T(8,128)(2,1)S(1)}, bf16[512,512]{1,0:T(8,128)(2,1)}, u32[]{:S(2)}) copy-start(bf16[512,512]{1,0:T(8,128)(2,1)} %w_key.3) | copy-start | bytes 1572868
  21.3 3.5 %collective-permute-start = (bf16[16,16,640]{2,1,0:T(8,128)(2,1)S(1)}, bf16[16,16,640]{2,1,0:T(8,128)(2,1)S(1)}, u32[]{:S(2)}, u32[]{:S(2)}) collective-permute-start(bf16[16,16,640]{2,1,0:T(8,128)(2,1)S(1)} %all-to-all-done.own), channel_id=1, source_target_pairs={{0,16},{16,0},{1,17},{17,1},{2,18},{18,2},{3,19},{19,3},{4,20},{20... | collective-permute-start | bytes 983048 | tf_op jit(solution)/shard_map/ppermute | solution.py:317
  29.2 4.3 %collective-permute-start.1 = (bf16[16,16,1664]{2,1,0:T(8,128)(2,1)S(1)}, bf16[16,16,1664]{2,1,0:T(8,128)(2,1)S(1)}, u32[]{:S(2)}, u32[]{:S(2)}) collective-permute-start(bf16[16,16,1664]{2,1,0:T(8,128)(2,1)S(1)} %get-tuple-element.51), channel_id=1, source_target_pairs={{0,16},{16,0},{1,17},{17,1},{2,18},{18,2},{3,19},{19,3},{4,20},{20... | collective-permute-start | bytes 2555912 | tf_op jit(solution)/shard_map/ppermute | solution.py:383
  34.6 28.7 %all-to-all-start.1 = ((bf16[16,16,1664]{2,1,0:T(8,128)(2,1)}), bf16[16,16,1664]{2,1,0:T(8,128)(2,1)S(1)}, u32[]{:S(2)}, u32[]{:S(2)}) async-start(bf16[16,16,1664]{2,1,0:T(8,128)(2,1)} %add.3), calls=%async_computation.1 | async-start | bytes 1703936 | tf_op jit(solution)/shard_map/all_to_all | solution.py:264
  40.1 6.7 %collective-permute-start.2 = (bf16[4,16,640]{2,1,0:T(8,128)(2,1)S(1)}, bf16[4,16,640]{2,1,0:T(8,128)(2,1)S(1)}, u32[]{:S(2)}, u32[]{:S(2)}) collective-permute-start(bf16[4,16,640]{2,1,0:T(8,128)(2,1)S(1)} %get-tuple-element.55), channel_id=1, source_target_pairs={{0,2},{2,0},{4,6},{6,4},{8,10},{10,8},{12,14},{14,12},{1,3},{3,1},... | collective-permute-start | bytes 245768 | tf_op jit(solution)/shard_map/ppermute | solution.py:349
  47.4 8.2 %collective-permute-start.3 = (bf16[2,16,640]{2,1,0:T(8,128)(2,1)S(1)}, bf16[2,16,640]{2,1,0:T(8,128)(2,1)S(1)}, u32[]{:S(2)}, u32[]{:S(2)}) collective-permute-start(bf16[2,16,640]{2,1,0:T(8,128)(2,1)S(1)} %get-tuple-element.57), channel_id=1, source_target_pairs={{0,4},{2,6},{4,0},{6,2},{8,12},{10,14},{12,8},{14,10},{1,5},{3,7},... | collective-permute-start | bytes 122888 | tf_op jit(solution)/shard_map/ppermute | solution.py:400
  56.1 7.2 %collective-permute-start.4 = (bf16[1,16,640]{2,1,0:T(8,128)(2,1)S(1)}, bf16[1,16,640]{2,1,0:T(8,128)(2,1)S(1)}, u32[]{:S(2)}, u32[]{:S(2)}) collective-permute-start(bf16[1,16,640]{2,1,0:T(8,128)(2,1)S(1)} %get-tuple-element.59), channel_id=1, source_target_pairs={{0,1},{1,0},{2,3},{3,2},{4,5},{5,4},{6,7},{7,6},{8,9},{9,8},{10,11... | collective-permute-start | bytes 61448 | tf_op jit(solution)/shard_map/ppermute | solution.py:409
  64.3 11.4 %copy-start.2 = (bf16[512,512]{1,0:T(8,128)(2,1)S(1)}, bf16[512,512]{1,0:T(8,128)(2,1)}, u32[]{:S(2)}) copy-start(bf16[512,512]{1,0:T(8,128)(2,1)} %w_key.3) | copy-start | bytes 1572868
  64.3 28.7 %all-to-all-start.2 = ((bf16[16,16,1152]{2,1,0:T(8,128)(2,1)}), bf16[16,16,1152]{2,1,0:T(8,128)(2,1)S(1)}, u32[]{:S(2)}, u32[]{:S(2)}) async-start(bf16[16,16,1152]{2,1,0:T(8,128)(2,1)} %shard_map.171), calls=%async_computation.2 | async-start | bytes 1179648 | tf_op jit(solution)/shard_map/all_to_all | solution.py:264

commit v5 on v4

--- a/solution.py
+++ b/solution.py
@@ -107,8 +107,6 @@
     resp_keys,
     first_scores,
     first_d_attention,
-    keep_resp,
-    send_resp,
     attention_out,
     d_scores_out,
     keys,
@@ -137,15 +135,6 @@
     row_delta = jnp.sum(attention * d_attention, axis=0, keepdims=True)
     d_scores = (SCALE * attention * (d_attention - row_delta)).astype(BF16)
     d_scores_out[...] = d_scores
-    own_grad = dot(d_scores[2 * HALF : KEYS], query[...], 1, 0)
-    own_grad_v = dot(attention_b[2 * HALF : KEYS], d_out[...], 1, 0)
-    resp = jnp.concatenate([own_grad[:, 0:DC] + own_grad_v, own_grad[:, DC:EXT]], axis=1)
-    blocks = resp.astype(BF16).reshape(RESP // PAGE, PAGE, EXT)
-    place = where[2]
-    for g in range(RESP // PAGE // 2):
-        low, high = blocks[g], blocks[RESP // PAGE // 2 + g]
-        keep_resp[g] = jnp.where(place == 0, low, high)
-        send_resp[g] = jnp.where(place == 0, high, low)
 
 
 def half_grads(parity, first_key, q_nope, masked, query, d_out, attention, d_scores, d_query, out_latent, out):
@@ -185,9 +174,29 @@
 
 
 def keep_kernel(
-    where, q_nope, masked, query, d_out, attention, d_scores, d_query, out_latent, keep
+    where,
+    q_nope,
+    masked,
+    query,
+    d_out,
+    attention,
+    d_scores,
+    d_query,
+    out_latent,
+    keep,
+    keep_resp,
+    send_resp,
 ):
     half_grads(where[1], 0, q_nope, masked, query, d_out, attention, d_scores, d_query, out_latent, keep)
+    own_grad = dot(d_scores[2 * HALF : KEYS, :], query[...], 1, 0)
+    own_grad_v = dot(attention[2 * HALF : KEYS, :], d_out[...], 1, 0)
+    resp = jnp.concatenate([own_grad[:, 0:DC] + own_grad_v, own_grad[:, DC:EXT]], axis=1)
+    blocks = resp.astype(BF16).reshape(RESP // PAGE, PAGE, EXT)
+    place = where[2]
+    for g in range(RESP // PAGE // 2):
+        low, high = blocks[g], blocks[RESP // PAGE // 2 + g]
+        keep_resp[g] = jnp.where(place == 0, low, high)
+        send_resp[g] = jnp.where(place == 0, high, low)
 
 
 def query_grad_kernel(d_query, w_key, d_q_nope, d_q_rope):
@@ -326,11 +335,9 @@
         scalars=1,
         flops=2_000_000_000,
     )
-    keep_resp, send_resp, attention, d_scores, keys = call(
+    attention, d_scores, keys = call(
         attention_kernel,
         [
-            ((RESP // PAGE // 2, PAGE, EXT), BF16),
-            ((RESP // PAGE // 2, PAGE, EXT), BF16),
             ((KEYS, ROWS), BF16),
             ((KEYS, ROWS), BF16),
             ((KEYS, EXT), BF16),
@@ -346,7 +353,6 @@
         scalars=1,
         flops=4_000_000_000,
     )
-    got_resp = lax.ppermute(send_resp, "z", [(i, i ^ 1) for i in range(8)])
     d_query, out_latent, send = call(
         send_kernel,
         [
@@ -365,9 +371,13 @@
         scalars=1,
         flops=4_000_000_000,
     )
-    (keep,) = call(
+    keep, keep_resp, send_resp = call(
         keep_kernel,
-        [((CHIPS, PAGE, WIDE), BF16)],
+        [
+            ((CHIPS, PAGE, WIDE), BF16),
+            ((RESP // PAGE // 2, PAGE, EXT), BF16),
+            ((RESP // PAGE // 2, PAGE, EXT), BF16),
+        ],
         where,
         q_nope,
         masked,
@@ -380,6 +390,7 @@
         scalars=1,
         flops=2_000_000_000,
     )
+    got_resp = lax.ppermute(send_resp, "z", [(i, i ^ 1) for i in range(8)])
     chip_sum = keep + lax.ppermute(send, "c", swap)
     sample_parts = spread(chip_sum, ("xl", "y"))
     d_q_nope, d_q_rope = call(

time: 94.4 us -> 94.2 us (level)
  no operation moved by 1% of the time
where the time goes in v5:
time: 94.2 us; the launch traced here: 93.5 us
  starting transfers between devices  45.2 us (48%)
  waiting for transfers between devices  30.5 us (32%)
  Pallas kernels  14 us (15%)
  between operations  1.5 us (2%)
  local copies, waits for them, and re-layouts  1.16 us (1%)
  other arithmetic  1.13 us (1%)
    all_to_all x3, starting transfers between devices, spread(): return lax.all_to_all(parts, axes, 0, 0, tiled=True)  26 us
    all_to_all x3, waiting for transfers between devices, spread(): return lax.all_to_all(parts, axes, 0, 0, tiled=True)  22.6 us
    pallas_call x12, Pallas kernels, call(): pl.pallas_call(kernel, out_shape=[jax.ShapeDtypeStruct(shape, kind) for s...  14 us
    ppermute x1, starting transfers between devices, body(): got_resp = lax.ppermute(send_resp, 'z', [(i, i ^ 2) for i in range(8)])  6.1 us
    ppermute x1, starting transfers between devices, body(): got_resp = lax.ppermute(send_resp, 'xh', swap)  4.63 us
    ppermute x1, starting transfers between devices, body(): got_resp = lax.ppermute(send_resp, 'z', [(i, i ^ 1) for i in range(8)])  4.27 us
    ppermute x1, waiting for transfers between devices, body(): got_resp = lax.ppermute(send_resp, 'xh', swap)  2.54 us
    ppermute x1, waiting for transfers between devices, body(): got_resp = lax.ppermute(send_resp, 'z', [(i, i ^ 1) for i in range(8)])  2.4 us
  transfers between devices with their start and end apart: 8, of which 7 were waited for; matrix products, arithmetic and copies ran while one was open for 0% of the time, Pallas kernels for 7%

profile of v5, /device:TPU:16, one launch (start us, length us, event | category | flops | bytes accessed | tf_op | source)
XLA Modules:
  0.0 93.5 jit_solution(4497153911830398303)
XLA Ops:
  0.6 1.6 %shard_map.162 = bf16[16,16,640]{2,1,0:T(8,128)(2,1)} custom-call(bf16[16,512]{1,0:T(8,128)(2,1)} %latent_far.1, bf16[16,64]{1,0:T(8,128)(2,1)} %bitcast.6), custom_call_target="tpu_custom_call" | custom-call | tf_op jit(solution)/shard_map/pallas_call | solution.py:261
  2.2 9.2 %all-to-all-start = ((bf16[16,16,640]{2,1,0:T(8,128)(2,1)}), bf16[16,16,640]{2,1,0:T(8,128)(2,1)S(1)}, u32[]{:S(2)}, u32[]{:S(2)}) async-start(bf16[16,16,640]{2,1,0:T(8,128)(2,1)} %shard_map.162), calls=%async_computation | async-start | bytes 655360 | tf_op jit(solution)/shard_map/all_to_all | solution.py:273
  12.2 1.0 %copy-done.1 = bf16[512,512]{1,0:T(8,128)(2,1)S(1)} copy-done((bf16[512,512]{1,0:T(8,128)(2,1)S(1)}, bf16[512,512]{1,0:T(8,128)(2,1)}, u32[]{:S(2)}) %copy-start.1) | copy-done | bytes 524312
  13.3 1.0 %shard_map.161 = (bf16[512,640]{1,0:T(8,128)(2,1)S(1)}, bf16[512,512]{1,0:T(8,128)(2,1)S(1)}, bf16[128,512]{1,0:T(8,128)(2,1)S(1)}, bf16[128,640]{1,0:T(8,128)(2,1)S(1)}) custom-call(s32[5]{0:T(128)S(1)} %stack.19.where, bf16[128,512]{1,0:T(8,128)(2,1)S(1)} %copy-done.5, bf16[128,256]{1,0:T(8,128)(2,1)S(1)} %copy-done.6, bf16[128,512]{1,0:T(8,128)(2,1)S(1)} %copy-done.3, ...), custom_call_target="tpu_custom_call" | custom-call | flops 4000000000 | tf_op jit(solution)/shard_map/pallas_call | solution.py:261
  14.3 7.1 %all-to-all-done.own = bf16[16,16,640]{2,1,0:T(8,128)(2,1)S(1)} async-done(((bf16[16,16,640]{2,1,0:T(8,128)(2,1)}), bf16[16,16,640]{2,1,0:T(8,128)(2,1)S(1)}, u32[]{:S(2)}, u32[]{:S(2)}) %all-to-all-start) | async-done | bytes 327712 | tf_op jit(solution)/shard_map/all_to_all | solution.py:273
  21.3 1.9 %collective-permute-start = (bf16[16,16,640]{2,1,0:T(8,128)(2,1)S(1)}, bf16[16,16,640]{2,1,0:T(8,128)(2,1)S(1)}, u32[]{:S(2)}, u32[]{:S(2)}) collective-permute-start(bf16[16,16,640]{2,1,0:T(8,128)(2,1)S(1)} %all-to-all-done.own), channel_id=1, source_target_pairs={{0,16},{16,0},{1,17},{17,1},{2,18},{18,2},{3,19},{19,3},{4,20},{20... | collective-permute-start | bytes 983048 | tf_op jit(solution)/shard_map/ppermute | solution.py:326
  23.3 1.4 %shard_map.163 = (f32[384,512]{1,0:T(8,128)S(1)}, f32[384,512]{1,0:T(8,128)S(1)}) custom-call(s32[5]{0:T(128)S(1)} %stack.19.where, bf16[512,640]{1,0:T(8,128)(2,1)S(1)} %get-tuple-element.39.query, bf16[512,512]{1,0:T(8,128)(2,1)S(1)} %get-tuple-element.40.d_out, bf16[16,16,640]{2,1,0:T(8,128)(2,1)S(1)} %all-to-all-done.own, ...), custom_call_target="tpu_custom_call" | custom-call | flops 2000000000 | tf_op jit(solution)/shard_map/pallas_call | solution.py:261
  24.9 1.8 %shard_map.164 = (bf16[640,512]{1,0:T(8,128)(2,1)S(1)}, bf16[640,512]{1,0:T(8,128)(2,1)S(1)}, bf16[640,640]{1,0:T(8,128)(2,1)S(1)}) custom-call(s32[5]{0:T(128)S(1)} %stack.19.where, bf16[512,640]{1,0:T(8,128)(2,1)S(1)} %get-tuple-element.39.query, bf16[512,512]{1,0:T(8,128)(2,1)S(1)} %get-tuple-element.40.d_out, bf16[16,16,640]{2,1,0:T(8,128)(2,1)S(1)} %all-to-all-done.own, ...), custom_call_target="tpu_custom_call" | custom-call | flops 4000000000 | tf_op jit(solution)/shard_map/pallas_call | solution.py:261
  26.7 2.3 %shard_map.165 = (bf16[640,512]{1,0:T(8,128)(2,1)S(1)}, bf16[512,512]{1,0:T(8,128)(2,1)S(1)}, bf16[16,16,1664]{2,1,0:T(8,128)(2,1)S(1)}) custom-call(s32[5]{0:T(128)S(1)} %stack.19.where, bf16[128,512]{1,0:T(8,128)(2,1)S(1)} %copy-done.5, bf16[128,512]{1,0:T(8,128)(2,1)S(1)} %get-tuple-element.37.masked, bf16[512,640]{1,0:T(8,128)(2,1)S(1)} %get-tuple-element.39.query, ...), custom_call_target="tpu_custom_call" | custom-call | flops 4000000000 | tf_op jit(solution)/shard_map/pallas_call | solution.py:261
  28.9 2.3 %collective-permute-start.1 = (bf16[16,16,1664]{2,1,0:T(8,128)(2,1)S(1)}, bf16[16,16,1664]{2,1,0:T(8,128)(2,1)S(1)}, u32[]{:S(2)}, u32[]{:S(2)}) collective-permute-start(bf16[16,16,1664]{2,1,0:T(8,128)(2,1)S(1)} %get-tuple-element.53), channel_id=1, source_target_pairs={{0,16},{16,0},{1,17},{17,1},{2,18},{18,2},{3,19},{19,3},{4,20},{20... | collective-permute-start | bytes 2555912 | tf_op jit(solution)/shard_map/ppermute | solution.py:394
  31.2 1.4 %shard_map.167 = (bf16[16,16,1664]{2,1,0:T(8,128)(2,1)S(1)}, bf16[4,16,640]{2,1,0:T(8,128)(2,1)S(1)}, bf16[4,16,640]{2,1,0:T(8,128)(2,1)S(1)}) custom-call(s32[5]{0:T(128)S(1)} %stack.19.where, bf16[128,512]{1,0:T(8,128)(2,1)S(1)} %copy-done.5, bf16[128,512]{1,0:T(8,128)(2,1)S(1)} %get-tuple-element.37.masked, bf16[512,640]{1,0:T(8,128)(2,1)S(1)} %get-tuple-element.39.query, ...), custom_call_target="tpu_custom_call" | custom-call | flops 2000000000 | tf_op jit(solution)/shard_map/pallas_call | solution.py:261
  33.2 1.1 %add.3 = bf16[16,16,1664]{2,1,0:T(8,128)(2,1)} add(bf16[16,16,1664]{2,1,0:T(8,128)(2,1)S(1)} %get-tuple-element.52, bf16[16,16,1664]{2,1,0:T(8,128)(2,1)S(1)} %collective-permute-done.1) | non-fusion elementwise | flops 425984 | bytes 2555904 | tf_op jit(solution)/shard_map/add | solution.py:394
  34.4 5.5 %all-to-all-start.1 = ((bf16[16,16,1664]{2,1,0:T(8,128)(2,1)}), bf16[16,16,1664]{2,1,0:T(8,128)(2,1)S(1)}, u32[]{:S(2)}, u32[]{:S(2)}) async-start(bf16[16,16,1664]{2,1,0:T(8,128)(2,1)} %add.3), calls=%async_computation.1 | async-start | bytes 1703936 | tf_op jit(solution)/shard_map/all_to_all | solution.py:273
  39.8 4.3 %collective-permute-start.2 = (bf16[4,16,640]{2,1,0:T(8,128)(2,1)S(1)}, bf16[4,16,640]{2,1,0:T(8,128)(2,1)S(1)}, u32[]{:S(2)}, u32[]{:S(2)}) collective-permute-start(bf16[4,16,640]{2,1,0:T(8,128)(2,1)S(1)} %get-tuple-element.57), channel_id=1, source_target_pairs={{0,2},{2,0},{4,6},{6,4},{8,10},{10,8},{12,14},{14,12},{1,3},{3,1},... | collective-permute-start | bytes 245768 | tf_op jit(solution)/shard_map/ppermute | solution.py:393
  44.1 2.4 %collective-permute-done.2.received = bf16[4,16,640]{2,1,0:T(8,128)(2,1)S(1)} collective-permute-done((bf16[4,16,640]{2,1,0:T(8,128)(2,1)S(1)}, bf16[4,16,640]{2,1,0:T(8,128)(2,1)S(1)}, u32[]{:S(2)}, u32[]{:S(2)}) %collective-permute-start.2) | collective-permute-done | bytes 81952 | tf_op jit(solution)/shard_map/ppermute | solution.py:393
  47.1 6.1 %collective-permute-start.3 = (bf16[2,16,640]{2,1,0:T(8,128)(2,1)S(1)}, bf16[2,16,640]{2,1,0:T(8,128)(2,1)S(1)}, u32[]{:S(2)}, u32[]{:S(2)}) collective-permute-start(bf16[2,16,640]{2,1,0:T(8,128)(2,1)S(1)} %get-tuple-element.59), channel_id=1, source_target_pairs={{0,4},{2,6},{4,0},{6,2},{8,12},{10,14},{12,8},{14,10},{1,5},{3,7},... | collective-permute-start | bytes 122888 | tf_op jit(solution)/shard_map/ppermute | solution.py:411
  53.2 2.1 %collective-permute-done.3.received = bf16[2,16,640]{2,1,0:T(8,128)(2,1)S(1)} collective-permute-done((bf16[2,16,640]{2,1,0:T(8,128)(2,1)S(1)}, bf16[2,16,640]{2,1,0:T(8,128)(2,1)S(1)}, u32[]{:S(2)}, u32[]{:S(2)}) %collective-permute-start.3) | collective-permute-done | bytes 40992 | tf_op jit(solution)/shard_map/ppermute | solution.py:411
  55.8 4.6 %collective-permute-start.4 = (bf16[1,16,640]{2,1,0:T(8,128)(2,1)S(1)}, bf16[1,16,640]{2,1,0:T(8,128)(2,1)S(1)}, u32[]{:S(2)}, u32[]{:S(2)}) collective-permute-start(bf16[1,16,640]{2,1,0:T(8,128)(2,1)S(1)} %get-tuple-element.61), channel_id=1, source_target_pairs={{0,1},{1,0},{2,3},{3,2},{4,5},{5,4},{6,7},{7,6},{8,9},{9,8},{10,11... | collective-permute-start | bytes 61448 | tf_op jit(solution)/shard_map/ppermute | solution.py:420
  60.5 2.5 %collective-permute-done.4.received = bf16[1,16,640]{2,1,0:T(8,128)(2,1)S(1)} collective-permute-done((bf16[1,16,640]{2,1,0:T(8,128)(2,1)S(1)}, bf16[1,16,640]{2,1,0:T(8,128)(2,1)S(1)}, u32[]{:S(2)}, u32[]{:S(2)}) %collective-permute-start.4) | collective-permute-done | bytes 20512 | tf_op jit(solution)/shard_map/ppermute | solution.py:420
  63.0 1.0 %shard_map.171 = bf16[16,16,1152]{2,1,0:T(8,128)(2,1)} custom-call(bf16[16,16,1664]{2,1,0:T(8,128)(2,1)S(1)} %all-to-all-done.1.sample_parts, bf16[1,16,640]{2,1,0:T(8,128)(2,1)S(1)} %get-tuple-element.60.kept, bf16[1,16,640]{2,1,0:T(8,128)(2,1)S(1)} %collective-permute-done.4.received), custom_call_target="tpu_custom_call" | custom-call | tf_op jit(solution)/shard_map/pallas_call | solution.py:261
  64.0 11.4 %all-to-all-start.2 = ((bf16[16,16,1152]{2,1,0:T(8,128)(2,1)}), bf16[16,16,1152]{2,1,0:T(8,128)(2,1)S(1)}, u32[]{:S(2)}, u32[]{:S(2)}) async-start(bf16[16,16,1152]{2,1,0:T(8,128)(2,1)} %shard_map.171), calls=%async_computation.2 | async-start | bytes 1179648 | tf_op jit(solution)/shard_map/all_to_all | solution.py:273
  75.4 1.0 %shard_map.166 = (bf16[128,512]{1,0:T(8,128)(2,1)}, bf16[128,256]{1,0:T(8,128)(2,1)}) custom-call(bf16[640,512]{1,0:T(8,128)(2,1)S(1)} %get-tuple-element.48.d_query, bf16[512,512]{1,0:T(8,128)(2,1)S(1)} %copy-done.2), custom_call_target="tpu_custom_call" | custom-call | flops 1000000000 | tf_op jit(solution)/shard_map/pallas_call | solution.py:261
  77.1 15.6 %all-to-all-done.2.parts = bf16[16,16,1152]{2,1,0:T(8,128)(2,1)S(1)} async-done(((bf16[16,16,1152]{2,1,0:T(8,128)(2,1)}), bf16[16,16,1152]{2,1,0:T(8,128)(2,1)S(1)}, u32[]{:S(2)}, u32[]{:S(2)}) %all-to-all-start.2) | async-done | bytes 589856 | tf_op jit(solution)/shard_map/all_to_all | solution.py:273
  92.7 0.8 shard_map.172
  (22 shorter events, 2.8 us)
Async XLA Ops:
  0.6 11.6 %copy-start = (bf16[512,512]{1,0:T(8,128)(2,1)S(1)}, bf16[512,512]{1,0:T(8,128)(2,1)}, u32[]{:S(2)}) copy-start(bf16[512,512]{1,0:T(8,128)(2,1)} %w_value.1) | copy-start | bytes 1572868
  2.2 10.0 %copy-start.3 = (bf16[128,512]{1,0:T(8,128)(2,1)S(1)}, bf16[128,512]{1,0:T(8,128)(2,1)}, u32[]{:S(2)}) copy-start(bf16[128,512]{1,0:T(8,128)(2,1)} %grad.1) | copy-start | bytes 393220
  2.2 10.0 %copy-start.4 = (bf16[128,512]{1,0:T(8,128)(2,1)S(1)}, bf16[128,512]{1,0:T(8,128)(2,1)}, u32[]{:S(2)}) copy-start(bf16[128,512]{1,0:T(8,128)(2,1)} %resp_latent.1) | copy-start | bytes 393220
  2.2 10.0 %copy-start.5 = (bf16[128,512]{1,0:T(8,128)(2,1)S(1)}, bf16[128,512]{1,0:T(8,128)(2,1)}, u32[]{:S(2)}) copy-start(bf16[128,512]{1,0:T(8,128)(2,1)} %q_nope.5) | copy-start | bytes 393220
  2.2 10.0 %copy-start.6 = (bf16[128,256]{1,0:T(8,128)(2,1)S(1)}, bf16[128,256]{1,0:T(8,128)(2,1)}, u32[]{:S(2)}) copy-start(bf16[128,256]{1,0:T(8,128)(2,1)} %q_rope.1) | copy-start | bytes 196612
  2.2 19.1 %all-to-all-start = ((bf16[16,16,640]{2,1,0:T(8,128)(2,1)}), bf16[16,16,640]{2,1,0:T(8,128)(2,1)S(1)}, u32[]{:S(2)}, u32[]{:S(2)}) async-start(bf16[16,16,640]{2,1,0:T(8,128)(2,1)} %shard_map.162), calls=%async_computation | async-start | bytes 655360 | tf_op jit(solution)/shard_map/all_to_all | solution.py:273
  11.4 0.8 copy-start.7
  12.2 1.0 %copy-start.1 = (bf16[512,512]{1,0:T(8,128)(2,1)S(1)}, bf16[512,512]{1,0:T(8,128)(2,1)}, u32[]{:S(2)}) copy-start(bf16[512,512]{1,0:T(8,128)(2,1)} %w_key.3) | copy-start | bytes 1572868
  21.3 3.5 %collective-permute-start = (bf16[16,16,640]{2,1,0:T(8,128)(2,1)S(1)}, bf16[16,16,640]{2,1,0:T(8,128)(2,1)S(1)}, u32[]{:S(2)}, u32[]{:S(2)}) collective-permute-start(bf16[16,16,640]{2,1,0:T(8,128)(2,1)S(1)} %all-to-all-done.own), channel_id=1, source_target_pairs={{0,16},{16,0},{1,17},{17,1},{2,18},{18,2},{3,19},{19,3},{4,20},{20... | collective-permute-start | bytes 983048 | tf_op jit(solution)/shard_map/ppermute | solution.py:326
  28.9 4.3 %collective-permute-start.1 = (bf16[16,16,1664]{2,1,0:T(8,128)(2,1)S(1)}, bf16[16,16,1664]{2,1,0:T(8,128)(2,1)S(1)}, u32[]{:S(2)}, u32[]{:S(2)}) collective-permute-start(bf16[16,16,1664]{2,1,0:T(8,128)(2,1)S(1)} %get-tuple-element.53), channel_id=1, source_target_pairs={{0,16},{16,0},{1,17},{17,1},{2,18},{18,2},{3,19},{19,3},{4,20},{20... | collective-permute-start | bytes 2555912 | tf_op jit(solution)/shard_map/ppermute | solution.py:394
  34.4 28.7 %all-to-all-start.1 = ((bf16[16,16,1664]{2,1,0:T(8,128)(2,1)}), bf16[16,16,1664]{2,1,0:T(8,128)(2,1)S(1)}, u32[]{:S(2)}, u32[]{:S(2)}) async-start(bf16[16,16,1664]{2,1,0:T(8,128)(2,1)} %add.3), calls=%async_computation.1 | async-start | bytes 1703936 | tf_op jit(solution)/shard_map/all_to_all | solution.py:273
  39.8 6.7 %collective-permute-start.2 = (bf16[4,16,640]{2,1,0:T(8,128)(2,1)S(1)}, bf16[4,16,640]{2,1,0:T(8,128)(2,1)S(1)}, u32[]{:S(2)}, u32[]{:S(2)}) collective-permute-start(bf16[4,16,640]{2,1,0:T(8,128)(2,1)S(1)} %get-tuple-element.57), channel_id=1, source_target_pairs={{0,2},{2,0},{4,6},{6,4},{8,10},{10,8},{12,14},{14,12},{1,3},{3,1},... | collective-permute-start | bytes 245768 | tf_op jit(solution)/shard_map/ppermute | solution.py:393
  47.1 8.2 %collective-permute-start.3 = (bf16[2,16,640]{2,1,0:T(8,128)(2,1)S(1)}, bf16[2,16,640]{2,1,0:T(8,128)(2,1)S(1)}, u32[]{:S(2)}, u32[]{:S(2)}) collective-permute-start(bf16[2,16,640]{2,1,0:T(8,128)(2,1)S(1)} %get-tuple-element.59), channel_id=1, source_target_pairs={{0,4},{2,6},{4,0},{6,2},{8,12},{10,14},{12,8},{14,10},{1,5},{3,7},... | collective-permute-start | bytes 122888 | tf_op jit(solution)/shard_map/ppermute | solution.py:411
  55.8 7.2 %collective-permute-start.4 = (bf16[1,16,640]{2,1,0:T(8,128)(2,1)S(1)}, bf16[1,16,640]{2,1,0:T(8,128)(2,1)S(1)}, u32[]{:S(2)}, u32[]{:S(2)}) collective-permute-start(bf16[1,16,640]{2,1,0:T(8,128)(2,1)S(1)} %get-tuple-element.61), channel_id=1, source_target_pairs={{0,1},{1,0},{2,3},{3,2},{4,5},{5,4},{6,7},{7,6},{8,9},{9,8},{10,11... | collective-permute-start | bytes 61448 | tf_op jit(solution)/shard_map/ppermute | solution.py:420
  64.0 11.4 %copy-start.2 = (bf16[512,512]{1,0:T(8,128)(2,1)S(1)}, bf16[512,512]{1,0:T(8,128)(2,1)}, u32[]{:S(2)}) copy-start(bf16[512,512]{1,0:T(8,128)(2,1)} %w_key.3) | copy-start | bytes 1572868
  64.0 28.7 %all-to-all-start.2 = ((bf16[16,16,1152]{2,1,0:T(8,128)(2,1)}), bf16[16,16,1152]{2,1,0:T(8,128)(2,1)S(1)}, u32[]{:S(2)}, u32[]{:S(2)}) async-start(bf16[16,16,1152]{2,1,0:T(8,128)(2,1)} %shard_map.171), calls=%async_computation.2 | async-start | bytes 1179648 | tf_op jit(solution)/shard_map/all_to_all | solution.py:273

commit v6 on v5

--- a/solution.py
+++ b/solution.py
@@ -20,7 +20,8 @@
 CHIPS = 16
 HALF = CHIPS * PAGE
 KEYS = 2 * HALF + RESP
-WIDE = 2 * LOCAL * DN + EXT
+ROPE_AT = (2 * LOCAL + DC // 128) * PAGE
+WIDE = ROPE_AT + 8
 OWNERS = [8 * (b & 1) + 2 * (b >> 1 & 1) + (b >> 2 & 1) for b in range(RESP // PAGE)]
 SCALE = (DN + DR) ** (-0.5)
 F32 = jnp.float32
@@ -100,6 +101,8 @@
 
 def attention_kernel(
     where,
+    q_nope,
+    masked,
     query,
     d_out,
     own,
@@ -109,6 +112,9 @@
     first_d_attention,
     attention_out,
     d_scores_out,
+    d_query,
+    out_latent,
+    send,
     keys,
 ):
     keys[0:HALF, :] = own[...].reshape(HALF, EXT)
@@ -135,42 +141,41 @@
     row_delta = jnp.sum(attention * d_attention, axis=0, keepdims=True)
     d_scores = (SCALE * attention * (d_attention - row_delta)).astype(BF16)
     d_scores_out[...] = d_scores
+    d_query[...] = dot(keys[...], d_scores, 0, 0).astype(BF16)
+    out_latent[...] = dot(keys[:, 0:DC], attention_b, 0, 0).astype(BF16)
+    half_grads(
+        1 - where[1],
+        HALF,
+        q_nope,
+        masked,
+        query,
+        d_out,
+        attention_out,
+        d_scores_out,
+        d_query,
+        out_latent,
+        send,
+    )
 
 
 def half_grads(parity, first_key, q_nope, masked, query, d_out, attention, d_scores, d_query, out_latent, out):
     starts = [pl.multiple_of((2 * k + parity) * PAGE, PAGE) for k in range(CHIPS)]
     d_q = jnp.concatenate([d_query[pl.ds(start, PAGE), :] for start in starts], axis=0)
     values = jnp.concatenate([out_latent[pl.ds(start, PAGE), :] for start in starts], axis=0)
+    blocks = []
     for h in range(LOCAL):
-        key_part = dot(d_q[:, columns(h, RESP)], q_nope[:, columns(h, DN)], 1, 0)
-        out[:, :, columns(h, DN)] = key_part.astype(BF16).reshape(CHIPS, PAGE, DN)
-        value_part = dot(values[:, columns(h, RESP)], masked[:, columns(h, DV)], 1, 0)
-        out[:, :, columns(LOCAL + h, DN)] = value_part.astype(BF16).reshape(CHIPS, PAGE, DN)
+        blocks.append(dot(d_q[:, columns(h, RESP)], q_nope[:, columns(h, DN)], 1, 0))
+    for h in range(LOCAL):
+        blocks.append(dot(values[:, columns(h, RESP)], masked[:, columns(h, DV)], 1, 0))
     rows = slice(first_key, first_key + HALF)
     key_grad = dot(d_scores[rows, :], query[...], 1, 0)
-    key_grad_v = dot(attention[rows, :], d_out[...], 1, 0)
-    width = 2 * LOCAL * DN
-    latent_part = (key_grad[:, 0:DC] + key_grad_v).astype(BF16)
-    out[:, :, width : width + DC] = latent_part.reshape(CHIPS, PAGE, DC)
-    out[:, :, width + DC : WIDE] = key_grad[:, DC:EXT].astype(BF16).reshape(CHIPS, PAGE, EXT - DC)
-
-
-def send_kernel(
-    where,
-    q_nope,
-    masked,
-    query,
-    d_out,
-    keys,
-    attention,
-    d_scores,
-    d_query,
-    out_latent,
-    send,
-):
-    d_query[...] = dot(keys[...], d_scores[...], 0, 0).astype(BF16)
-    out_latent[...] = dot(keys[:, 0:DC], attention[...], 0, 0).astype(BF16)
-    half_grads(1 - where[1], HALF, q_nope, masked, query, d_out, attention, d_scores, d_query, out_latent, send)
+    latent_part = key_grad[:, 0:DC] + dot(attention[rows, :], d_out[...], 1, 0)
+    blocks += [latent_part[:, columns(part, 128)] for part in range(DC // 128)]
+    for at, block in enumerate(blocks):
+        out[:, columns(at, PAGE), :] = block.astype(BF16).reshape(CHIPS, PAGE, 128)
+    rope = key_grad[:, DC : DC + DR].reshape(CHIPS, PAGE, DR)
+    rope = jnp.concatenate([rope[:, 0:8], rope[:, 8:16]], axis=2)
+    out[:, ROPE_AT:WIDE, :] = rope.astype(BF16)
 
 
 def keep_kernel(
@@ -221,24 +226,31 @@
     send[...] = (kept[theirs].astype(F32) + received[theirs].astype(F32)).astype(BF16)
 
 
+def add_blocks(parts, rows):
+    total = parts[0, rows, :].astype(F32)
+    for k in range(1, CHIPS):
+        total = total + parts[k, rows, :].astype(F32)
+    return total
+
+
 def line_kernel(sample_parts, kept, received, out):
-    first = 2 * LOCAL * DN
-    page = sample_parts[0, :, first:WIDE].astype(F32)
-    for k in range(1, CHIPS):
-        page = page + sample_parts[k, :, first:WIDE].astype(F32)
+    latent = add_blocks(sample_parts, slice(2 * LOCAL * PAGE, ROPE_AT))
+    rope = add_blocks(sample_parts, slice(ROPE_AT, WIDE))
+    rope = jnp.concatenate([rope[:, 0:DR], rope[:, DR : 2 * DR]], axis=0)
     rows = kept[0].astype(F32) + received[0].astype(F32)
-    line = jnp.concatenate([rows[:, 0:KEY], page[:, 0:KEY]], axis=1).astype(BF16)
+    line = jnp.concatenate(
+        [rows[:, 0:KEY]] + [latent[columns(part, PAGE)] for part in range(DC // 128)] + [rope],
+        axis=1,
+    ).astype(BF16)
     for g in range(CHIPS):
         out[g] = line
 
 
 def weights_kernel(sample_parts, d_key_up, d_value_up):
-    for out, first in ((d_key_up, 0), (d_value_up, LOCAL * DN)):
-        lanes = slice(first, first + LOCAL * DN)
-        total = sample_parts[0, :, lanes].astype(F32)
-        for k in range(1, CHIPS):
-            total = total + sample_parts[k, :, lanes].astype(F32)
-        out[...] = total
+    total = add_blocks(sample_parts, slice(0, 2 * LOCAL * PAGE))
+    for h in range(LOCAL):
+        d_key_up[:, columns(h, DN)] = total[columns(h, PAGE)]
+        d_value_up[:, columns(h, DV)] = total[columns(LOCAL + h, PAGE)]
 
 
 def last_kernel(parts, d_prompt, d_prompt_rope, d_resp, d_resp_rope_t):
@@ -335,14 +347,18 @@
         scalars=1,
         flops=2_000_000_000,
     )
-    attention, d_scores, keys = call(
+    attention, d_scores, d_query, out_latent, send = call(
         attention_kernel,
         [
             ((KEYS, ROWS), BF16),
             ((KEYS, ROWS), BF16),
-            ((KEYS, EXT), BF16),
-        ],
-        where,
+            ((EXT, ROWS), BF16),
+            ((DC, ROWS), BF16),
+            ((CHIPS, WIDE, 128), BF16),
+        ],
+        where,
+        q_nope,
+        masked,
         query,
         d_out,
         own,
@@ -352,29 +368,12 @@
         first_d_attention,
         scalars=1,
         flops=4_000_000_000,
-    )
-    d_query, out_latent, send = call(
-        send_kernel,
-        [
-            ((EXT, ROWS), BF16),
-            ((DC, ROWS), BF16),
-            ((CHIPS, PAGE, WIDE), BF16),
-        ],
-        where,
-        q_nope,
-        masked,
-        query,
-        d_out,
-        keys,
-        attention,
-        d_scores,
-        scalars=1,
-        flops=4_000_000_000,
+        scratch=[pltpu.VMEM((KEYS, EXT), BF16)],
     )
     keep, keep_resp, send_resp = call(
         keep_kernel,
         [
-            ((CHIPS, PAGE, WIDE), BF16),
+            ((CHIPS, WIDE, 128), BF16),
             ((RESP // PAGE // 2, PAGE, EXT), BF16),
             ((RESP // PAGE // 2, PAGE, EXT), BF16),
         ],

time: 94.2 us -> 92.5 us (0.982)
    pallas_call x12 -> x11, Pallas kernels: 14 us -> 13.3 us  [call(): pl.pallas_call(kernel, out_shape=[jax.ShapeDtypeStruct(shape, kind) for s...]
where the time goes in v6:
time: 92.5 us; the launch traced here: 91.9 us
  starting transfers between devices  45.2 us (49%)
  waiting for transfers between devices  29.6 us (32%)
  Pallas kernels  13.3 us (14%)
  between operations  1.49 us (2%)
  local copies, waits for them, and re-layouts  1.16 us (1%)
  other arithmetic  1.12 us (1%)
    all_to_all x3, starting transfers between devices, spread(): return lax.all_to_all(parts, axes, 0, 0, tiled=True)  26.1 us
    all_to_all x3, waiting for transfers between devices, spread(): return lax.all_to_all(parts, axes, 0, 0, tiled=True)  21.8 us
    pallas_call x11, Pallas kernels, call(): pl.pallas_call(kernel, out_shape=[jax.ShapeDtypeStruct(shape, kind) for s...  13.3 us
    ppermute x1, starting transfers between devices, body(): got_resp = lax.ppermute(send_resp, 'z', [(i, i ^ 2) for i in range(8)])  6.09 us
    ppermute x1, starting transfers between devices, body(): got_resp = lax.ppermute(send_resp, 'xh', swap)  4.64 us
    ppermute x1, starting transfers between devices, body(): got_resp = lax.ppermute(send_resp, 'z', [(i, i ^ 1) for i in range(8)])  4.27 us
    ppermute x1, waiting for transfers between devices, body(): got_resp = lax.ppermute(send_resp, 'xh', swap)  2.53 us
    ppermute x1, waiting for transfers between devices, body(): got_resp = lax.ppermute(send_resp, 'z', [(i, i ^ 1) for i in range(8)])  2.4 us
  transfers between devices with their start and end apart: 8, of which 7 were waited for; matrix products, arithmetic and copies ran while one was open for 0% of the time, Pallas kernels for 7%

profile of v6, /device:TPU:16, one launch (start us, length us, event | category | flops | bytes accessed | tf_op | source)
XLA Modules:
  0.0 91.9 jit_solution(1317515861229696772)
XLA Ops:
  0.6 1.5 %shard_map.162 = bf16[16,16,640]{2,1,0:T(8,128)(2,1)} custom-call(bf16[16,512]{1,0:T(8,128)(2,1)} %latent_far.1, bf16[16,64]{1,0:T(8,128)(2,1)} %bitcast.6), custom_call_target="tpu_custom_call" | custom-call | tf_op jit(solution)/shard_map/pallas_call | solution.py:273
  2.2 9.2 %all-to-all-start = ((bf16[16,16,640]{2,1,0:T(8,128)(2,1)}), bf16[16,16,640]{2,1,0:T(8,128)(2,1)S(1)}, u32[]{:S(2)}, u32[]{:S(2)}) async-start(bf16[16,16,640]{2,1,0:T(8,128)(2,1)} %shard_map.162), calls=%async_computation | async-start | bytes 655360 | tf_op jit(solution)/shard_map/all_to_all | solution.py:285
  12.2 1.0 %copy-done.1 = bf16[512,512]{1,0:T(8,128)(2,1)S(1)} copy-done((bf16[512,512]{1,0:T(8,128)(2,1)S(1)}, bf16[512,512]{1,0:T(8,128)(2,1)}, u32[]{:S(2)}) %copy-start.1) | copy-done | bytes 524312
  13.3 1.0 %shard_map.161 = (bf16[512,640]{1,0:T(8,128)(2,1)S(1)}, bf16[512,512]{1,0:T(8,128)(2,1)S(1)}, bf16[128,512]{1,0:T(8,128)(2,1)S(1)}, bf16[128,640]{1,0:T(8,128)(2,1)S(1)}) custom-call(s32[5]{0:T(128)S(1)} %stack.19.where, bf16[128,512]{1,0:T(8,128)(2,1)S(1)} %copy-done.5, bf16[128,256]{1,0:T(8,128)(2,1)S(1)} %copy-done.6, bf16[128,512]{1,0:T(8,128)(2,1)S(1)} %copy-done.3, ...), custom_call_target="tpu_custom_call" | custom-call | flops 4000000000 | tf_op jit(solution)/shard_map/pallas_call | solution.py:273
  14.3 7.1 %all-to-all-done.own = bf16[16,16,640]{2,1,0:T(8,128)(2,1)S(1)} async-done(((bf16[16,16,640]{2,1,0:T(8,128)(2,1)}), bf16[16,16,640]{2,1,0:T(8,128)(2,1)S(1)}, u32[]{:S(2)}, u32[]{:S(2)}) %all-to-all-start) | async-done | bytes 327712 | tf_op jit(solution)/shard_map/all_to_all | solution.py:285
  21.3 1.9 %collective-permute-start = (bf16[16,16,640]{2,1,0:T(8,128)(2,1)S(1)}, bf16[16,16,640]{2,1,0:T(8,128)(2,1)S(1)}, u32[]{:S(2)}, u32[]{:S(2)}) collective-permute-start(bf16[16,16,640]{2,1,0:T(8,128)(2,1)S(1)} %all-to-all-done.own), channel_id=1, source_target_pairs={{0,16},{16,0},{1,17},{17,1},{2,18},{18,2},{3,19},{19,3},{4,20},{20... | collective-permute-start | bytes 983048 | tf_op jit(solution)/shard_map/ppermute | solution.py:338
  23.3 1.4 %shard_map.163 = (f32[384,512]{1,0:T(8,128)S(1)}, f32[384,512]{1,0:T(8,128)S(1)}) custom-call(s32[5]{0:T(128)S(1)} %stack.19.where, bf16[512,640]{1,0:T(8,128)(2,1)S(1)} %get-tuple-element.38.query, bf16[512,512]{1,0:T(8,128)(2,1)S(1)} %get-tuple-element.39.d_out, bf16[16,16,640]{2,1,0:T(8,128)(2,1)S(1)} %all-to-all-done.own, ...), custom_call_target="tpu_custom_call" | custom-call | flops 2000000000 | tf_op jit(solution)/shard_map/pallas_call | solution.py:273
  24.8 3.3 %shard_map.164 = (bf16[640,512]{1,0:T(8,128)(2,1)S(1)}, bf16[640,512]{1,0:T(8,128)(2,1)S(1)}, bf16[640,512]{1,0:T(8,128)(2,1)S(1)}, bf16[512,512]{1,0:T(8,128)(2,1)S(1)}, bf16[16,200,128]{2,1,0:T(8,128)(2,1)S(1)}) custom-call(s32[5]{0:T(128)S(1)} %stack.19.where, bf16[128,512]{1,0:T(8,128)(2,1)S(1)} %copy-done.5, ...), custom_call_target="tpu_custom_call" | custom-call | flops 4000000000 | tf_op jit(solution)/shard_map/pallas_call | solution.py:273
  28.2 2.2 %collective-permute-start.1 = (bf16[16,200,128]{2,1,0:T(8,128)(2,1)S(1)}, bf16[16,200,128]{2,1,0:T(8,128)(2,1)S(1)}, u32[]{:S(2)}, u32[]{:S(2)}) collective-permute-start(bf16[16,200,128]{2,1,0:T(8,128)(2,1)S(1)} %get-tuple-element.51), channel_id=1, source_target_pairs={{0,16},{16,0},{1,17},{17,1},{2,18},{18,2},{3,19},{19,3},{4,20},{20... | collective-permute-start | bytes 2457608 | tf_op jit(solution)/shard_map/ppermute | solution.py:393
  30.5 1.4 %shard_map.166 = (bf16[16,200,128]{2,1,0:T(8,128)(2,1)S(1)}, bf16[4,16,640]{2,1,0:T(8,128)(2,1)S(1)}, bf16[4,16,640]{2,1,0:T(8,128)(2,1)S(1)}) custom-call(s32[5]{0:T(128)S(1)} %stack.19.where, bf16[128,512]{1,0:T(8,128)(2,1)S(1)} %copy-done.5, bf16[128,512]{1,0:T(8,128)(2,1)S(1)} %get-tuple-element.36.masked, bf16[512,640]{1,0:T(8,128)(2,1)S(1)} %get-tuple-element.38.query, ...), custom_call_target="tpu_custom_call" | custom-call | flops 2000000000 | tf_op jit(solution)/shard_map/pallas_call | solution.py:273
  32.4 1.1 %add.3 = bf16[16,200,128]{2,1,0:T(8,128)(2,1)} add(bf16[16,200,128]{2,1,0:T(8,128)(2,1)S(1)} %get-tuple-element.50, bf16[16,200,128]{2,1,0:T(8,128)(2,1)S(1)} %collective-permute-done.1) | non-fusion elementwise | flops 409600 | bytes 2457600 | tf_op jit(solution)/shard_map/add | solution.py:393
  33.5 5.5 %all-to-all-start.1 = ((bf16[16,200,128]{2,1,0:T(8,128)(2,1)}), bf16[16,200,128]{2,1,0:T(8,128)(2,1)S(1)}, u32[]{:S(2)}, u32[]{:S(2)}) async-start(bf16[16,200,128]{2,1,0:T(8,128)(2,1)} %add.3), calls=%async_computation.1 | async-start | bytes 1638400 | tf_op jit(solution)/shard_map/all_to_all | solution.py:285
  39.0 4.3 %collective-permute-start.2 = (bf16[4,16,640]{2,1,0:T(8,128)(2,1)S(1)}, bf16[4,16,640]{2,1,0:T(8,128)(2,1)S(1)}, u32[]{:S(2)}, u32[]{:S(2)}) collective-permute-start(bf16[4,16,640]{2,1,0:T(8,128)(2,1)S(1)} %get-tuple-element.55), channel_id=1, source_target_pairs={{0,2},{2,0},{4,6},{6,4},{8,10},{10,8},{12,14},{14,12},{1,3},{3,1},... | collective-permute-start | bytes 245768 | tf_op jit(solution)/shard_map/ppermute | solution.py:392
  43.3 2.4 %collective-permute-done.2.received = bf16[4,16,640]{2,1,0:T(8,128)(2,1)S(1)} collective-permute-done((bf16[4,16,640]{2,1,0:T(8,128)(2,1)S(1)}, bf16[4,16,640]{2,1,0:T(8,128)(2,1)S(1)}, u32[]{:S(2)}, u32[]{:S(2)}) %collective-permute-start.2) | collective-permute-done | bytes 81952 | tf_op jit(solution)/shard_map/ppermute | solution.py:392
  46.3 6.1 %collective-permute-start.3 = (bf16[2,16,640]{2,1,0:T(8,128)(2,1)S(1)}, bf16[2,16,640]{2,1,0:T(8,128)(2,1)S(1)}, u32[]{:S(2)}, u32[]{:S(2)}) collective-permute-start(bf16[2,16,640]{2,1,0:T(8,128)(2,1)S(1)} %get-tuple-element.57), channel_id=1, source_target_pairs={{0,4},{2,6},{4,0},{6,2},{8,12},{10,14},{12,8},{14,10},{1,5},{3,7},... | collective-permute-start | bytes 122888 | tf_op jit(solution)/shard_map/ppermute | solution.py:410
  52.4 2.1 %collective-permute-done.3.received = bf16[2,16,640]{2,1,0:T(8,128)(2,1)S(1)} collective-permute-done((bf16[2,16,640]{2,1,0:T(8,128)(2,1)S(1)}, bf16[2,16,640]{2,1,0:T(8,128)(2,1)S(1)}, u32[]{:S(2)}, u32[]{:S(2)}) %collective-permute-start.3) | collective-permute-done | bytes 40992 | tf_op jit(solution)/shard_map/ppermute | solution.py:410
  55.0 4.6 %collective-permute-start.4 = (bf16[1,16,640]{2,1,0:T(8,128)(2,1)S(1)}, bf16[1,16,640]{2,1,0:T(8,128)(2,1)S(1)}, u32[]{:S(2)}, u32[]{:S(2)}) collective-permute-start(bf16[1,16,640]{2,1,0:T(8,128)(2,1)S(1)} %get-tuple-element.59), channel_id=1, source_target_pairs={{0,1},{1,0},{2,3},{3,2},{4,5},{5,4},{6,7},{7,6},{8,9},{9,8},{10,11... | collective-permute-start | bytes 61448 | tf_op jit(solution)/shard_map/ppermute | solution.py:419
  59.7 2.5 %collective-permute-done.4.received = bf16[1,16,640]{2,1,0:T(8,128)(2,1)S(1)} collective-permute-done((bf16[1,16,640]{2,1,0:T(8,128)(2,1)S(1)}, bf16[1,16,640]{2,1,0:T(8,128)(2,1)S(1)}, u32[]{:S(2)}, u32[]{:S(2)}) %collective-permute-start.4) | collective-permute-done | bytes 20512 | tf_op jit(solution)/shard_map/ppermute | solution.py:419
  62.2 1.0 %shard_map.170 = bf16[16,16,1152]{2,1,0:T(8,128)(2,1)} custom-call(bf16[16,200,128]{2,1,0:T(8,128)(2,1)S(1)} %all-to-all-done.1.sample_parts, bf16[1,16,640]{2,1,0:T(8,128)(2,1)S(1)} %get-tuple-element.58.kept, bf16[1,16,640]{2,1,0:T(8,128)(2,1)S(1)} %collective-permute-done.4.received), custom_call_target="tpu_custom_call" | custom-call | tf_op jit(solution)/shard_map/pallas_call | solution.py:273
  63.2 11.4 %all-to-all-start.2 = ((bf16[16,16,1152]{2,1,0:T(8,128)(2,1)}), bf16[16,16,1152]{2,1,0:T(8,128)(2,1)S(1)}, u32[]{:S(2)}, u32[]{:S(2)}) async-start(bf16[16,16,1152]{2,1,0:T(8,128)(2,1)} %shard_map.170), calls=%async_computation.2 | async-start | bytes 1179648 | tf_op jit(solution)/shard_map/all_to_all | solution.py:285
  74.6 1.0 %shard_map.165 = (bf16[128,512]{1,0:T(8,128)(2,1)}, bf16[128,256]{1,0:T(8,128)(2,1)}) custom-call(bf16[640,512]{1,0:T(8,128)(2,1)S(1)} %get-tuple-element.44.d_query, bf16[512,512]{1,0:T(8,128)(2,1)S(1)} %copy-done.2), custom_call_target="tpu_custom_call" | custom-call | flops 1000000000 | tf_op jit(solution)/shard_map/pallas_call | solution.py:273
  75.7 0.7 shard_map.167
  76.4 14.7 %all-to-all-done.2.parts = bf16[16,16,1152]{2,1,0:T(8,128)(2,1)S(1)} async-done(((bf16[16,16,1152]{2,1,0:T(8,128)(2,1)}), bf16[16,16,1152]{2,1,0:T(8,128)(2,1)S(1)}, u32[]{:S(2)}, u32[]{:S(2)}) %all-to-all-start.2) | async-done | bytes 589856 | tf_op jit(solution)/shard_map/all_to_all | solution.py:285
  91.1 0.8 shard_map.171
  (21 shorter events, 2.0 us)
Async XLA Ops:
  0.6 11.6 %copy-start = (bf16[512,512]{1,0:T(8,128)(2,1)S(1)}, bf16[512,512]{1,0:T(8,128)(2,1)}, u32[]{:S(2)}) copy-start(bf16[512,512]{1,0:T(8,128)(2,1)} %w_value.1) | copy-start | bytes 1572868
  2.2 10.0 %copy-start.3 = (bf16[128,512]{1,0:T(8,128)(2,1)S(1)}, bf16[128,512]{1,0:T(8,128)(2,1)}, u32[]{:S(2)}) copy-start(bf16[128,512]{1,0:T(8,128)(2,1)} %grad.1) | copy-start | bytes 393220
  2.2 10.0 %copy-start.4 = (bf16[128,512]{1,0:T(8,128)(2,1)S(1)}, bf16[128,512]{1,0:T(8,128)(2,1)}, u32[]{:S(2)}) copy-start(bf16[128,512]{1,0:T(8,128)(2,1)} %resp_latent.1) | copy-start | bytes 393220
  2.2 10.0 %copy-start.5 = (bf16[128,512]{1,0:T(8,128)(2,1)S(1)}, bf16[128,512]{1,0:T(8,128)(2,1)}, u32[]{:S(2)}) copy-start(bf16[128,512]{1,0:T(8,128)(2,1)} %q_nope.5) | copy-start | bytes 393220
  2.2 10.0 %copy-start.6 = (bf16[128,256]{1,0:T(8,128)(2,1)S(1)}, bf16[128,256]{1,0:T(8,128)(2,1)}, u32[]{:S(2)}) copy-start(bf16[128,256]{1,0:T(8,128)(2,1)} %q_rope.1) | copy-start | bytes 196612
  2.2 19.1 %all-to-all-start = ((bf16[16,16,640]{2,1,0:T(8,128)(2,1)}), bf16[16,16,640]{2,1,0:T(8,128)(2,1)S(1)}, u32[]{:S(2)}, u32[]{:S(2)}) async-start(bf16[16,16,640]{2,1,0:T(8,128)(2,1)} %shard_map.162), calls=%async_computation | async-start | bytes 655360 | tf_op jit(solution)/shard_map/all_to_all | solution.py:285
  11.4 0.8 copy-start.7
  12.2 1.0 %copy-start.1 = (bf16[512,512]{1,0:T(8,128)(2,1)S(1)}, bf16[512,512]{1,0:T(8,128)(2,1)}, u32[]{:S(2)}) copy-start(bf16[512,512]{1,0:T(8,128)(2,1)} %w_key.3) | copy-start | bytes 1572868
  21.3 3.5 %collective-permute-start = (bf16[16,16,640]{2,1,0:T(8,128)(2,1)S(1)}, bf16[16,16,640]{2,1,0:T(8,128)(2,1)S(1)}, u32[]{:S(2)}, u32[]{:S(2)}) collective-permute-start(bf16[16,16,640]{2,1,0:T(8,128)(2,1)S(1)} %all-to-all-done.own), channel_id=1, source_target_pairs={{0,16},{16,0},{1,17},{17,1},{2,18},{18,2},{3,19},{19,3},{4,20},{20... | collective-permute-start | bytes 983048 | tf_op jit(solution)/shard_map/ppermute | solution.py:338
  28.2 4.2 %collective-permute-start.1 = (bf16[16,200,128]{2,1,0:T(8,128)(2,1)S(1)}, bf16[16,200,128]{2,1,0:T(8,128)(2,1)S(1)}, u32[]{:S(2)}, u32[]{:S(2)}) collective-permute-start(bf16[16,200,128]{2,1,0:T(8,128)(2,1)S(1)} %get-tuple-element.51), channel_id=1, source_target_pairs={{0,16},{16,0},{1,17},{17,1},{2,18},{18,2},{3,19},{19,3},{4,20},{20... | collective-permute-start | bytes 2457608 | tf_op jit(solution)/shard_map/ppermute | solution.py:393
  33.5 28.7 %all-to-all-start.1 = ((bf16[16,200,128]{2,1,0:T(8,128)(2,1)}), bf16[16,200,128]{2,1,0:T(8,128)(2,1)S(1)}, u32[]{:S(2)}, u32[]{:S(2)}) async-start(bf16[16,200,128]{2,1,0:T(8,128)(2,1)} %add.3), calls=%async_computation.1 | async-start | bytes 1638400 | tf_op jit(solution)/shard_map/all_to_all | solution.py:285
  39.0 6.7 %collective-permute-start.2 = (bf16[4,16,640]{2,1,0:T(8,128)(2,1)S(1)}, bf16[4,16,640]{2,1,0:T(8,128)(2,1)S(1)}, u32[]{:S(2)}, u32[]{:S(2)}) collective-permute-start(bf16[4,16,640]{2,1,0:T(8,128)(2,1)S(1)} %get-tuple-element.55), channel_id=1, source_target_pairs={{0,2},{2,0},{4,6},{6,4},{8,10},{10,8},{12,14},{14,12},{1,3},{3,1},... | collective-permute-start | bytes 245768 | tf_op jit(solution)/shard_map/ppermute | solution.py:392
  46.3 8.2 %collective-permute-start.3 = (bf16[2,16,640]{2,1,0:T(8,128)(2,1)S(1)}, bf16[2,16,640]{2,1,0:T(8,128)(2,1)S(1)}, u32[]{:S(2)}, u32[]{:S(2)}) collective-permute-start(bf16[2,16,640]{2,1,0:T(8,128)(2,1)S(1)} %get-tuple-element.57), channel_id=1, source_target_pairs={{0,4},{2,6},{4,0},{6,2},{8,12},{10,14},{12,8},{14,10},{1,5},{3,7},... | collective-permute-start | bytes 122888 | tf_op jit(solution)/shard_map/ppermute | solution.py:410
  55.0 7.2 %collective-permute-start.4 = (bf16[1,16,640]{2,1,0:T(8,128)(2,1)S(1)}, bf16[1,16,640]{2,1,0:T(8,128)(2,1)S(1)}, u32[]{:S(2)}, u32[]{:S(2)}) collective-permute-start(bf16[1,16,640]{2,1,0:T(8,128)(2,1)S(1)} %get-tuple-element.59), channel_id=1, source_target_pairs={{0,1},{1,0},{2,3},{3,2},{4,5},{5,4},{6,7},{7,6},{8,9},{9,8},{10,11... | collective-permute-start | bytes 61448 | tf_op jit(solution)/shard_map/ppermute | solution.py:419
  63.2 11.4 %copy-start.2 = (bf16[512,512]{1,0:T(8,128)(2,1)S(1)}, bf16[512,512]{1,0:T(8,128)(2,1)}, u32[]{:S(2)}) copy-start(bf16[512,512]{1,0:T(8,128)(2,1)} %w_key.3) | copy-start | bytes 1572868
  63.2 27.9 %all-to-all-start.2 = ((bf16[16,16,1152]{2,1,0:T(8,128)(2,1)}), bf16[16,16,1152]{2,1,0:T(8,128)(2,1)S(1)}, u32[]{:S(2)}, u32[]{:S(2)}) async-start(bf16[16,16,1152]{2,1,0:T(8,128)(2,1)} %shard_map.170), calls=%async_computation.2 | async-start | bytes 1179648 | tf_op jit(solution)/shard_map/all_to_all | solution.py:285

commit v7 on v6

--- a/solution.py
+++ b/solution.py
@@ -22,7 +22,8 @@
 KEYS = 2 * HALF + RESP
 ROPE_AT = (2 * LOCAL + DC // 128) * PAGE
 WIDE = ROPE_AT + 8
-OWNERS = [8 * (b & 1) + 2 * (b >> 1 & 1) + (b >> 2 & 1) for b in range(RESP // PAGE)]
+PACKED = DC // 128 * PAGE + 8
+OWNERS = [8 * (b & 1) + (3, 0, 1, 2)[b >> 1] for b in range(RESP // PAGE)]
 SCALE = (DN + DR) ** (-0.5)
 F32 = jnp.float32
 BF16 = jnp.bfloat16
@@ -51,9 +52,22 @@
     second.start()
     first.wait()
     second.wait()
-    page = with_rope(latent[...], rope[...])
+    rows = rope[...].astype(F32)
+    rows = jnp.concatenate([rows[0:8], rows[8:16]], axis=1).astype(BF16)
     for k in range(CHIPS):
-        out[k] = page
+        for part in range(DC // 128):
+            out[k, columns(part, PAGE), :] = latent[:, columns(part, 128)]
+        out[k, DC // 128 * PAGE : PACKED, :] = rows
+
+
+def unpack(pages, keys):
+    for part in range(DC // 128):
+        block = pages[:, columns(part, PAGE), :]
+        keys[:, columns(part, 128)] = block.reshape(HALF, 128)
+    rope = pages[:, DC // 128 * PAGE : PACKED, :].astype(F32)
+    rope = jnp.concatenate([rope[:, :, 0:DR], rope[:, :, DR : 2 * DR]], axis=1)
+    rope = jnp.concatenate([rope, jnp.zeros_like(rope)], axis=2)
+    keys[:, DC:EXT] = rope.reshape(HALF, EXT - DC).astype(BF16)
 
 
 def query_kernel(
@@ -85,9 +99,10 @@
         )
 
 
-def first_scores_kernel(where, query, d_out, own, resp_keys, scores, d_attention):
+def first_scores_kernel(where, query, d_out, own, resp_keys, scores, d_attention, own_keys):
     length = where[0]
-    pages = own[...].reshape(HALF, EXT)
+    unpack(own, own_keys)
+    pages = own_keys[...]
     resp = resp_keys[...]
     scores[0:HALF, :] = dot(pages, query[...], 1, 1) * SCALE
     token = lax.broadcasted_iota(jnp.int32, (RESP, ROWS), 1) % RESP
@@ -117,10 +132,10 @@
     send,
     keys,
 ):
-    keys[0:HALF, :] = own[...].reshape(HALF, EXT)
-    keys[HALF : 2 * HALF, :] = other[...].reshape(HALF, EXT)
+    keys[0:HALF, :] = own[...]
+    unpack(other, keys.at[HALF : 2 * HALF])
     keys[2 * HALF : KEYS, :] = resp_keys[...]
-    other_rows = other[...].reshape(HALF, EXT)
+    other_rows = keys[HALF : 2 * HALF, :]
     other_scores = dot(other_rows, query[...], 1, 1) * SCALE
     scores = jnp.concatenate(
         [first_scores[0:HALF], other_scores, first_scores[HALF : HALF + RESP]], axis=0
@@ -195,11 +210,16 @@
     half_grads(where[1], 0, q_nope, masked, query, d_out, attention, d_scores, d_query, out_latent, keep)
     own_grad = dot(d_scores[2 * HALF : KEYS, :], query[...], 1, 0)
     own_grad_v = dot(attention[2 * HALF : KEYS, :], d_out[...], 1, 0)
-    resp = jnp.concatenate([own_grad[:, 0:DC] + own_grad_v, own_grad[:, DC:EXT]], axis=1)
-    blocks = resp.astype(BF16).reshape(RESP // PAGE, PAGE, EXT)
+    latent = (own_grad[:, 0:DC] + own_grad_v).reshape(RESP // PAGE, PAGE, DC)
+    rope = own_grad[:, DC:KEY].reshape(RESP // PAGE, PAGE, DR)
+    packed = jnp.concatenate(
+        [latent[:, :, columns(part, 128)] for part in range(DC // 128)]
+        + [jnp.concatenate([rope[:, 0:8], rope[:, 8:16]], axis=2)],
+        axis=1,
+    ).astype(BF16)
     place = where[2]
     for g in range(RESP // PAGE // 2):
-        low, high = blocks[g], blocks[RESP // PAGE // 2 + g]
+        low, high = packed[g], packed[RESP // PAGE // 2 + g]
         keep_resp[g] = jnp.where(place == 0, low, high)
         send_resp[g] = jnp.where(place == 0, high, low)
 
@@ -234,14 +254,9 @@
 
 
 def line_kernel(sample_parts, kept, received, out):
-    latent = add_blocks(sample_parts, slice(2 * LOCAL * PAGE, ROPE_AT))
-    rope = add_blocks(sample_parts, slice(ROPE_AT, WIDE))
-    rope = jnp.concatenate([rope[:, 0:DR], rope[:, DR : 2 * DR]], axis=0)
+    page = add_blocks(sample_parts, slice(2 * LOCAL * PAGE, WIDE))
     rows = kept[0].astype(F32) + received[0].astype(F32)
-    line = jnp.concatenate(
-        [rows[:, 0:KEY]] + [latent[columns(part, PAGE)] for part in range(DC // 128)] + [rope],
-        axis=1,
-    ).astype(BF16)
+    line = jnp.concatenate([rows, page], axis=0).astype(BF16)
     for g in range(CHIPS):
         out[g] = line
 
@@ -253,18 +268,26 @@
         d_value_up[:, columns(h, DV)] = total[columns(LOCAL + h, PAGE)]
 
 
+def unpacked(block):
+    latent = [block[columns(part, PAGE)] for part in range(DC // 128)]
+    rope = block[DC // 128 * PAGE : PACKED]
+    return (
+        jnp.concatenate(latent, axis=1),
+        jnp.concatenate([rope[:, 0:DR], rope[:, DR : 2 * DR]], axis=0),
+    )
+
+
 def last_kernel(parts, d_prompt, d_prompt_rope, d_resp, d_resp_rope_t):
-    page = parts[0].astype(F32)
-    for g in range(1, CHIPS):
-        page = page + parts[g].astype(F32)
-    d_prompt[...] = page[:, KEY : KEY + DC]
-    d_prompt_rope[...] = page[:, KEY + DC : 2 * KEY]
-    rows = jnp.concatenate(
-        [parts[g, :, 0:KEY].astype(F32) + parts[g + 4, :, 0:KEY].astype(F32) for g in OWNERS],
-        axis=0,
-    )
-    d_resp[...] = rows[:, 0:DC]
-    d_resp_rope_t[...] = jnp.transpose(rows[:, DC:KEY])
+    latent, rope = unpacked(add_blocks(parts, slice(PACKED, 2 * PACKED)))
+    d_prompt[...] = latent
+    d_prompt_rope[...] = rope
+    ropes = []
+    for at, g in enumerate(OWNERS):
+        block = parts[g, 0:PACKED, :].astype(F32) + parts[g + 4, 0:PACKED, :].astype(F32)
+        latent, rope = unpacked(block)
+        d_resp[columns(at, PAGE), :] = latent
+        ropes.append(rope)
+    d_resp_rope_t[...] = jnp.transpose(jnp.concatenate(ropes, axis=0))
 
 
 def call(kernel, outs, *args, scratch=(), scalars=0, flops=0, far=False):
@@ -300,7 +323,7 @@
     swap = [(0, 1), (1, 0)]
     (pages,) = call(
         pages_kernel,
-        [((CHIPS, PAGE, EXT), BF16)],
+        [((CHIPS, PACKED, 128), BF16)],
         pltpu.with_memory_space_constraint(prompt_latent, pltpu.HBM),
         pltpu.with_memory_space_constraint(jnp.transpose(prompt_rope_t), pltpu.HBM),
         far=True,
@@ -313,7 +336,7 @@
     own = spread(pages, ("xl", "y"))
     z = lax.axis_index("z")
     where = jnp.stack(
-        [lengths[0], lax.axis_index("c"), z & 1, z >> 1 & 1, lax.axis_index("xh")]
+        [lengths[0], lax.axis_index("c"), (z + 1) >> 1 & 1, 1 - (z & 1), lax.axis_index("xh")]
     )
     query, d_out, masked, resp_keys = call(
         query_kernel,
@@ -336,9 +359,9 @@
     )
     own, query = lax.optimization_barrier((own, query))
     other = lax.ppermute(own, "c", swap)
-    first_scores, first_d_attention = call(
+    first_scores, first_d_attention, own_keys = call(
         first_scores_kernel,
-        [((HALF + RESP, ROWS), F32)] * 2,
+        [((HALF + RESP, ROWS), F32)] * 2 + [((HALF, EXT), BF16)],
         where,
         query,
         d_out,
@@ -361,7 +384,7 @@
         masked,
         query,
         d_out,
-        own,
+        own_keys,
         other,
         resp_keys,
         first_scores,
@@ -374,8 +397,8 @@
         keep_kernel,
         [
             ((CHIPS, WIDE, 128), BF16),
-            ((RESP // PAGE // 2, PAGE, EXT), BF16),
-            ((RESP // PAGE // 2, PAGE, EXT), BF16),
+            ((RESP // PAGE // 2, PACKED, 128), BF16),
+            ((RESP // PAGE // 2, PACKED, 128), BF16),
         ],
         where,
         q_nope,
@@ -401,16 +424,16 @@
     )
     keep_resp, send_resp = call(
         functools.partial(halve_kernel, 3),
-        [((2, PAGE, EXT), BF16)] * 2,
+        [((2, PACKED, 128), BF16)] * 2,
         where,
         keep_resp,
         got_resp,
         scalars=1,
     )
-    got_resp = lax.ppermute(send_resp, "z", [(i, i ^ 2) for i in range(8)])
+    got_resp = lax.ppermute(send_resp, "z", [(i, (i + 2 * (i & 1) - 1) % 8) for i in range(8)])
     keep_resp, send_resp = call(
         functools.partial(halve_kernel, 4),
-        [((1, PAGE, EXT), BF16)] * 2,
+        [((1, PACKED, 128), BF16)] * 2,
         where,
         keep_resp,
         got_resp,
@@ -419,7 +442,7 @@
     got_resp = lax.ppermute(send_resp, "xh", swap)
     (line,) = call(
         line_kernel,
-        [((CHIPS, PAGE, 2 * KEY), BF16)],
+        [((CHIPS, 2 * PACKED, 128), BF16)],
         sample_parts,
         keep_resp,
         got_resp,

time: 92.5 us -> 91.8 us (level)
  waiting for transfers between devices: 29.6 us -> 28.1 us
    all_to_all x3, starting transfers between devices: 26.1 us -> 21.4 us  [spread(): return lax.all_to_all(parts, axes, 0, 0, tiled=True)]
    ppermute x1, starting transfers between devices: 6.09 us -> 10.6 us  [body(): lax.ppermute(send_resp, 'z', [(i, (i + 2 * (i & 1) - 1) % 8) for i in ran...]
    all_to_all x3, waiting for transfers between devices: 21.8 us -> 20.7 us  [spread(): return lax.all_to_all(parts, axes, 0, 0, tiled=True)]
where the time goes in v7:
time: 91.8 us; the launch traced here: 91.1 us
  starting transfers between devices  45.1 us (49%)
  waiting for transfers between devices  28.1 us (31%)
  Pallas kernels  13.2 us (14%)
  local copies, waits for them, and re-layouts  1.99 us (2%)
  between operations  1.48 us (2%)
  other arithmetic  1.12 us (1%)
    all_to_all x3, starting transfers between devices, spread(): return lax.all_to_all(parts, axes, 0, 0, tiled=True)  21.4 us
    all_to_all x3, waiting for transfers between devices, spread(): return lax.all_to_all(parts, axes, 0, 0, tiled=True)  20.7 us
    pallas_call x11, Pallas kernels, call(): pl.pallas_call(kernel, out_shape=[jax.ShapeDtypeStruct(shape, kind) for s...  13.2 us
    ppermute x1, starting transfers between devices, body(): lax.ppermute(send_resp, 'z', [(i, (i + 2 * (i & 1) - 1) % 8) for i in ran...  10.6 us
    ppermute x1, starting transfers between devices, body(): got_resp = lax.ppermute(send_resp, 'xh', swap)  4.63 us
    ppermute x1, starting transfers between devices, body(): got_resp = lax.ppermute(send_resp, 'z', [(i, i ^ 1) for i in range(8)])  4.26 us
    ppermute x1, waiting for transfers between devices, body(): got_resp = lax.ppermute(send_resp, 'xh', swap)  2.52 us
    ppermute x1, waiting for transfers between devices, body(): got_resp = lax.ppermute(send_resp, 'z', [(i, i ^ 1) for i in range(8)])  2.32 us
  transfers between devices with their start and end apart: 8, of which 7 were waited for; matrix products, arithmetic and copies ran while one was open for 0% of the time, Pallas kernels for 7%

profile of v7, /device:TPU:16, one launch (start us, length us, event | category | flops | bytes accessed | tf_op | source)
XLA Modules:
  0.0 91.1 jit_solution(11513830309917945074)
XLA Ops:
  0.6 1.6 %shard_map.162 = bf16[16,72,128]{2,1,0:T(8,128)(2,1)} custom-call(bf16[16,512]{1,0:T(8,128)(2,1)} %latent_far.1, bf16[16,64]{1,0:T(8,128)(2,1)} %bitcast.6), custom_call_target="tpu_custom_call" | custom-call | tf_op jit(solution)/shard_map/pallas_call | solution.py:296
  2.3 9.2 %all-to-all-start = ((bf16[16,72,128]{2,1,0:T(8,128)(2,1)}), bf16[16,72,128]{2,1,0:T(8,128)(2,1)S(1)}, u32[]{:S(2)}, u32[]{:S(2)}) async-start(bf16[16,72,128]{2,1,0:T(8,128)(2,1)} %shard_map.162), calls=%async_computation | async-start | bytes 589824 | tf_op jit(solution)/shard_map/all_to_all | solution.py:308
  12.2 1.0 %copy-done.1 = bf16[512,512]{1,0:T(8,128)(2,1)S(1)} copy-done((bf16[512,512]{1,0:T(8,128)(2,1)S(1)}, bf16[512,512]{1,0:T(8,128)(2,1)}, u32[]{:S(2)}) %copy-start.1) | copy-done | bytes 524312
  13.3 0.8 copy-done.6
  14.1 1.0 %shard_map.161 = (bf16[512,640]{1,0:T(8,128)(2,1)S(1)}, bf16[512,512]{1,0:T(8,128)(2,1)S(1)}, bf16[128,512]{1,0:T(8,128)(2,1)S(1)}, bf16[128,640]{1,0:T(8,128)(2,1)S(1)}) custom-call(s32[5]{0:T(128)S(1)} %stack.19.where, bf16[128,512]{1,0:T(8,128)(2,1)S(1)} %copy-done.5, bf16[128,256]{1,0:T(8,128)(2,1)S(1)} %copy-done.6, bf16[128,512]{1,0:T(8,128)(2,1)S(1)} %copy-done.3, ...), custom_call_target="tpu_custom_call" | custom-call | flops 4000000000 | tf_op jit(solution)/shard_map/pallas_call | solution.py:296
  15.1 5.7 %all-to-all-done.own = bf16[16,72,128]{2,1,0:T(8,128)(2,1)S(1)} async-done(((bf16[16,72,128]{2,1,0:T(8,128)(2,1)}), bf16[16,72,128]{2,1,0:T(8,128)(2,1)S(1)}, u32[]{:S(2)}, u32[]{:S(2)}) %all-to-all-start) | async-done | bytes 294944 | tf_op jit(solution)/shard_map/all_to_all | solution.py:308
  20.8 1.9 %collective-permute-start = (bf16[16,72,128]{2,1,0:T(8,128)(2,1)S(1)}, bf16[16,72,128]{2,1,0:T(8,128)(2,1)S(1)}, u32[]{:S(2)}, u32[]{:S(2)}) collective-permute-start(bf16[16,72,128]{2,1,0:T(8,128)(2,1)S(1)} %all-to-all-done.own), channel_id=1, source_target_pairs={{0,16},{16,0},{1,17},{17,1},{2,18},{18,2},{3,19},{19,3},{4,20},{20... | collective-permute-start | bytes 884744 | tf_op jit(solution)/shard_map/ppermute | solution.py:361
  22.7 1.4 %shard_map.163 = (f32[384,512]{1,0:T(8,128)S(1)}, f32[384,512]{1,0:T(8,128)S(1)}, bf16[256,640]{1,0:T(8,128)(2,1)S(1)}) custom-call(s32[5]{0:T(128)S(1)} %stack.19.where, bf16[512,640]{1,0:T(8,128)(2,1)S(1)} %get-tuple-element.39.query, bf16[512,512]{1,0:T(8,128)(2,1)S(1)} %get-tuple-element.40.d_out, bf16[16,72,128]{2,1,0:T(8,128)(2,1)S(1)} %all-to-all-done.own, ...), custom_call_target="tpu_custom_call" | custom-call | flops 2000000000 | tf_op jit(solution)/shard_map/pallas_call | solution.py:296
  24.2 3.3 %shard_map.164 = (bf16[640,512]{1,0:T(8,128)(2,1)S(1)}, bf16[640,512]{1,0:T(8,128)(2,1)S(1)}, bf16[640,512]{1,0:T(8,128)(2,1)S(1)}, bf16[512,512]{1,0:T(8,128)(2,1)S(1)}, bf16[16,200,128]{2,1,0:T(8,128)(2,1)S(1)}) custom-call(s32[5]{0:T(128)S(1)} %stack.19.where, bf16[128,512]{1,0:T(8,128)(2,1)S(1)} %copy-done.5, ...), custom_call_target="tpu_custom_call" | custom-call | flops 4000000000 | tf_op jit(solution)/shard_map/pallas_call | solution.py:296
  27.5 2.3 %collective-permute-start.1 = (bf16[16,200,128]{2,1,0:T(8,128)(2,1)S(1)}, bf16[16,200,128]{2,1,0:T(8,128)(2,1)S(1)}, u32[]{:S(2)}, u32[]{:S(2)}) collective-permute-start(bf16[16,200,128]{2,1,0:T(8,128)(2,1)S(1)} %get-tuple-element.53), channel_id=1, source_target_pairs={{0,16},{16,0},{1,17},{17,1},{2,18},{18,2},{3,19},{19,3},{4,20},{20... | collective-permute-start | bytes 2457608 | tf_op jit(solution)/shard_map/ppermute | solution.py:416
  29.8 1.4 %shard_map.166 = (bf16[16,200,128]{2,1,0:T(8,128)(2,1)S(1)}, bf16[4,72,128]{2,1,0:T(8,128)(2,1)S(1)}, bf16[4,72,128]{2,1,0:T(8,128)(2,1)S(1)}) custom-call(s32[5]{0:T(128)S(1)} %stack.19.where, bf16[128,512]{1,0:T(8,128)(2,1)S(1)} %copy-done.5, bf16[128,512]{1,0:T(8,128)(2,1)S(1)} %get-tuple-element.37.masked, bf16[512,640]{1,0:T(8,128)(2,1)S(1)} %get-tuple-element.39.query, ...), custom_call_target="tpu_custom_call" | custom-call | flops 2000000000 | tf_op jit(solution)/shard_map/pallas_call | solution.py:296
  31.8 1.1 %add.7 = bf16[16,200,128]{2,1,0:T(8,128)(2,1)} add(bf16[16,200,128]{2,1,0:T(8,128)(2,1)S(1)} %get-tuple-element.52, bf16[16,200,128]{2,1,0:T(8,128)(2,1)S(1)} %collective-permute-done.1) | non-fusion elementwise | flops 409600 | bytes 2457600 | tf_op jit(solution)/shard_map/add | solution.py:416
  32.9 5.4 %all-to-all-start.1 = ((bf16[16,200,128]{2,1,0:T(8,128)(2,1)}), bf16[16,200,128]{2,1,0:T(8,128)(2,1)S(1)}, u32[]{:S(2)}, u32[]{:S(2)}) async-start(bf16[16,200,128]{2,1,0:T(8,128)(2,1)} %add.7), calls=%async_computation.1 | async-start | bytes 1638400 | tf_op jit(solution)/shard_map/all_to_all | solution.py:308
  38.3 4.3 %collective-permute-start.2 = (bf16[4,72,128]{2,1,0:T(8,128)(2,1)S(1)}, bf16[4,72,128]{2,1,0:T(8,128)(2,1)S(1)}, u32[]{:S(2)}, u32[]{:S(2)}) collective-permute-start(bf16[4,72,128]{2,1,0:T(8,128)(2,1)S(1)} %get-tuple-element.57), channel_id=1, source_target_pairs={{0,2},{2,0},{4,6},{6,4},{8,10},{10,8},{12,14},{14,12},{1,3},{3,1},... | collective-permute-start | bytes 221192 | tf_op jit(solution)/shard_map/ppermute | solution.py:415
  42.5 2.3 %collective-permute-done.2.received = bf16[4,72,128]{2,1,0:T(8,128)(2,1)S(1)} collective-permute-done((bf16[4,72,128]{2,1,0:T(8,128)(2,1)S(1)}, bf16[4,72,128]{2,1,0:T(8,128)(2,1)S(1)}, u32[]{:S(2)}, u32[]{:S(2)}) %collective-permute-start.2) | collective-permute-done | bytes 73760 | tf_op jit(solution)/shard_map/ppermute | solution.py:415
  45.4 10.6 %collective-permute-start.3 = (bf16[2,72,128]{2,1,0:T(8,128)(2,1)S(1)}, bf16[2,72,128]{2,1,0:T(8,128)(2,1)S(1)}, u32[]{:S(2)}, u32[]{:S(2)}) collective-permute-start(bf16[2,72,128]{2,1,0:T(8,128)(2,1)S(1)} %get-tuple-element.59), channel_id=1, source_target_pairs={{0,14},{2,4},{4,2},{6,8},{8,6},{10,12},{12,10},{14,0},{1,15},{3,5}... | collective-permute-start | bytes 110600 | tf_op jit(solution)/shard_map/ppermute | solution.py:433
  56.0 1.9 %collective-permute-done.3.received = bf16[2,72,128]{2,1,0:T(8,128)(2,1)S(1)} collective-permute-done((bf16[2,72,128]{2,1,0:T(8,128)(2,1)S(1)}, bf16[2,72,128]{2,1,0:T(8,128)(2,1)S(1)}, u32[]{:S(2)}, u32[]{:S(2)}) %collective-permute-start.3) | collective-permute-done | bytes 36896 | tf_op jit(solution)/shard_map/ppermute | solution.py:433
  58.5 4.6 %collective-permute-start.4 = (bf16[1,72,128]{2,1,0:T(8,128)(2,1)S(1)}, bf16[1,72,128]{2,1,0:T(8,128)(2,1)S(1)}, u32[]{:S(2)}, u32[]{:S(2)}) collective-permute-start(bf16[1,72,128]{2,1,0:T(8,128)(2,1)S(1)} %get-tuple-element.61), channel_id=1, source_target_pairs={{0,1},{1,0},{2,3},{3,2},{4,5},{5,4},{6,7},{7,6},{8,9},{9,8},{10,11... | collective-permute-start | bytes 55304 | tf_op jit(solution)/shard_map/ppermute | solution.py:442
  63.2 2.5 %collective-permute-done.4.received = bf16[1,72,128]{2,1,0:T(8,128)(2,1)S(1)} collective-permute-done((bf16[1,72,128]{2,1,0:T(8,128)(2,1)S(1)}, bf16[1,72,128]{2,1,0:T(8,128)(2,1)S(1)}, u32[]{:S(2)}, u32[]{:S(2)}) %collective-permute-start.4) | collective-permute-done | bytes 18464 | tf_op jit(solution)/shard_map/ppermute | solution.py:442
  65.7 0.9 %shard_map.170 = bf16[16,144,128]{2,1,0:T(8,128)(2,1)} custom-call(bf16[16,200,128]{2,1,0:T(8,128)(2,1)S(1)} %all-to-all-done.1.sample_parts, bf16[1,72,128]{2,1,0:T(8,128)(2,1)S(1)} %get-tuple-element.60.kept, bf16[1,72,128]{2,1,0:T(8,128)(2,1)S(1)} %collective-permute-done.4.received), custom_call_target="tpu_custom_call" | custom-call | tf_op jit(solution)/shard_map/pallas_call | solution.py:296
  66.6 6.9 %all-to-all-start.2 = ((bf16[16,144,128]{2,1,0:T(8,128)(2,1)}), bf16[16,144,128]{2,1,0:T(8,128)(2,1)S(1)}, u32[]{:S(2)}, u32[]{:S(2)}) async-start(bf16[16,144,128]{2,1,0:T(8,128)(2,1)} %shard_map.170), calls=%async_computation.2 | async-start | bytes 1179648 | tf_op jit(solution)/shard_map/all_to_all | solution.py:308
  73.5 1.0 %shard_map.165 = (bf16[128,512]{1,0:T(8,128)(2,1)}, bf16[128,256]{1,0:T(8,128)(2,1)}) custom-call(bf16[640,512]{1,0:T(8,128)(2,1)S(1)} %get-tuple-element.46.d_query, bf16[512,512]{1,0:T(8,128)(2,1)S(1)} %copy-done.2), custom_call_target="tpu_custom_call" | custom-call | flops 1000000000 | tf_op jit(solution)/shard_map/pallas_call | solution.py:296
  75.2 15.0 %all-to-all-done.2.parts = bf16[16,144,128]{2,1,0:T(8,128)(2,1)S(1)} async-done(((bf16[16,144,128]{2,1,0:T(8,128)(2,1)}), bf16[16,144,128]{2,1,0:T(8,128)(2,1)S(1)}, u32[]{:S(2)}, u32[]{:S(2)}) %all-to-all-start.2) | async-done | bytes 589856 | tf_op jit(solution)/shard_map/all_to_all | solution.py:308
  90.2 0.8 shard_map.171
  (21 shorter events, 2.6 us)
Async XLA Ops:
  0.6 11.6 %copy-start = (bf16[512,512]{1,0:T(8,128)(2,1)S(1)}, bf16[512,512]{1,0:T(8,128)(2,1)}, u32[]{:S(2)}) copy-start(bf16[512,512]{1,0:T(8,128)(2,1)} %w_value.1) | copy-start | bytes 1572868
  2.2 10.0 %copy-start.3 = (bf16[128,512]{1,0:T(8,128)(2,1)S(1)}, bf16[128,512]{1,0:T(8,128)(2,1)}, u32[]{:S(2)}) copy-start(bf16[128,512]{1,0:T(8,128)(2,1)} %grad.1) | copy-start | bytes 393220
  2.2 10.0 %copy-start.4 = (bf16[128,512]{1,0:T(8,128)(2,1)S(1)}, bf16[128,512]{1,0:T(8,128)(2,1)}, u32[]{:S(2)}) copy-start(bf16[128,512]{1,0:T(8,128)(2,1)} %resp_latent.1) | copy-start | bytes 393220
  2.3 10.0 %copy-start.5 = (bf16[128,512]{1,0:T(8,128)(2,1)S(1)}, bf16[128,512]{1,0:T(8,128)(2,1)}, u32[]{:S(2)}) copy-start(bf16[128,512]{1,0:T(8,128)(2,1)} %q_nope.5) | copy-start | bytes 393220
  2.3 18.5 %all-to-all-start = ((bf16[16,72,128]{2,1,0:T(8,128)(2,1)}), bf16[16,72,128]{2,1,0:T(8,128)(2,1)S(1)}, u32[]{:S(2)}, u32[]{:S(2)}) async-start(bf16[16,72,128]{2,1,0:T(8,128)(2,1)} %shard_map.162), calls=%async_computation | async-start | bytes 589824 | tf_op jit(solution)/shard_map/all_to_all | solution.py:308
  11.4 0.8 copy-start.7
  12.2 1.0 %copy-start.1 = (bf16[512,512]{1,0:T(8,128)(2,1)S(1)}, bf16[512,512]{1,0:T(8,128)(2,1)}, u32[]{:S(2)}) copy-start(bf16[512,512]{1,0:T(8,128)(2,1)} %w_key.3) | copy-start | bytes 1572868
  13.3 0.8 copy-start.6
  20.8 3.5 %collective-permute-start = (bf16[16,72,128]{2,1,0:T(8,128)(2,1)S(1)}, bf16[16,72,128]{2,1,0:T(8,128)(2,1)S(1)}, u32[]{:S(2)}, u32[]{:S(2)}) collective-permute-start(bf16[16,72,128]{2,1,0:T(8,128)(2,1)S(1)} %all-to-all-done.own), channel_id=1, source_target_pairs={{0,16},{16,0},{1,17},{17,1},{2,18},{18,2},{3,19},{19,3},{4,20},{20... | collective-permute-start | bytes 884744 | tf_op jit(solution)/shard_map/ppermute | solution.py:361
  27.5 4.2 %collective-permute-start.1 = (bf16[16,200,128]{2,1,0:T(8,128)(2,1)S(1)}, bf16[16,200,128]{2,1,0:T(8,128)(2,1)S(1)}, u32[]{:S(2)}, u32[]{:S(2)}) collective-permute-start(bf16[16,200,128]{2,1,0:T(8,128)(2,1)S(1)} %get-tuple-element.53), channel_id=1, source_target_pairs={{0,16},{16,0},{1,17},{17,1},{2,18},{18,2},{3,19},{19,3},{4,20},{20... | collective-permute-start | bytes 2457608 | tf_op jit(solution)/shard_map/ppermute | solution.py:416
  32.9 32.8 %all-to-all-start.1 = ((bf16[16,200,128]{2,1,0:T(8,128)(2,1)}), bf16[16,200,128]{2,1,0:T(8,128)(2,1)S(1)}, u32[]{:S(2)}, u32[]{:S(2)}) async-start(bf16[16,200,128]{2,1,0:T(8,128)(2,1)} %add.7), calls=%async_computation.1 | async-start | bytes 1638400 | tf_op jit(solution)/shard_map/all_to_all | solution.py:308
  38.3 6.6 %collective-permute-start.2 = (bf16[4,72,128]{2,1,0:T(8,128)(2,1)S(1)}, bf16[4,72,128]{2,1,0:T(8,128)(2,1)S(1)}, u32[]{:S(2)}, u32[]{:S(2)}) collective-permute-start(bf16[4,72,128]{2,1,0:T(8,128)(2,1)S(1)} %get-tuple-element.57), channel_id=1, source_target_pairs={{0,2},{2,0},{4,6},{6,4},{8,10},{10,8},{12,14},{14,12},{1,3},{3,1},... | collective-permute-start | bytes 221192 | tf_op jit(solution)/shard_map/ppermute | solution.py:415
  45.4 12.5 %collective-permute-start.3 = (bf16[2,72,128]{2,1,0:T(8,128)(2,1)S(1)}, bf16[2,72,128]{2,1,0:T(8,128)(2,1)S(1)}, u32[]{:S(2)}, u32[]{:S(2)}) collective-permute-start(bf16[2,72,128]{2,1,0:T(8,128)(2,1)S(1)} %get-tuple-element.59), channel_id=1, source_target_pairs={{0,14},{2,4},{4,2},{6,8},{8,6},{10,12},{12,10},{14,0},{1,15},{3,5}... | collective-permute-start | bytes 110600 | tf_op jit(solution)/shard_map/ppermute | solution.py:433
  58.5 7.2 %collective-permute-start.4 = (bf16[1,72,128]{2,1,0:T(8,128)(2,1)S(1)}, bf16[1,72,128]{2,1,0:T(8,128)(2,1)S(1)}, u32[]{:S(2)}, u32[]{:S(2)}) collective-permute-start(bf16[1,72,128]{2,1,0:T(8,128)(2,1)S(1)} %get-tuple-element.61), channel_id=1, source_target_pairs={{0,1},{1,0},{2,3},{3,2},{4,5},{5,4},{6,7},{7,6},{8,9},{9,8},{10,11... | collective-permute-start | bytes 55304 | tf_op jit(solution)/shard_map/ppermute | solution.py:442
  66.6 6.9 %copy-start.2 = (bf16[512,512]{1,0:T(8,128)(2,1)S(1)}, bf16[512,512]{1,0:T(8,128)(2,1)}, u32[]{:S(2)}) copy-start(bf16[512,512]{1,0:T(8,128)(2,1)} %w_key.3) | copy-start | bytes 1572868
  66.6 23.6 %all-to-all-start.2 = ((bf16[16,144,128]{2,1,0:T(8,128)(2,1)}), bf16[16,144,128]{2,1,0:T(8,128)(2,1)S(1)}, u32[]{:S(2)}, u32[]{:S(2)}) async-start(bf16[16,144,128]{2,1,0:T(8,128)(2,1)} %shard_map.170), calls=%async_computation.2 | async-start | bytes 1179648 | tf_op jit(solution)/shard_map/all_to_all | solution.py:308

commit v8 on v7

--- a/solution.py
+++ b/solution.py
@@ -23,7 +23,8 @@
 ROPE_AT = (2 * LOCAL + DC // 128) * PAGE
 WIDE = ROPE_AT + 8
 PACKED = DC // 128 * PAGE + 8
-OWNERS = [8 * (b & 1) + (3, 0, 1, 2)[b >> 1] for b in range(RESP // PAGE)]
+OWNERS = [(b & 1) + 2 * (3, 0, 1, 2)[b >> 1] for b in range(RESP // PAGE)]
+ORDER = [2 * (3 * k % 8) + xh for xh in range(2) for k in range(8)]
 SCALE = (DN + DR) ** (-0.5)
 F32 = jnp.float32
 BF16 = jnp.bfloat16
@@ -283,7 +284,8 @@
     d_prompt_rope[...] = rope
     ropes = []
     for at, g in enumerate(OWNERS):
-        block = parts[g, 0:PACKED, :].astype(F32) + parts[g + 4, 0:PACKED, :].astype(F32)
+        low, high = ORDER.index(g), ORDER.index(g + 8)
+        block = parts[low, 0:PACKED, :].astype(F32) + parts[high, 0:PACKED, :].astype(F32)
         latent, rope = unpacked(block)
         d_resp[columns(at, PAGE), :] = latent
         ropes.append(rope)
@@ -453,7 +455,9 @@
         sample_parts,
         flops=1_000_000_000,
     )
-    lines = spread(line, ("xh", "z"))
+    lines = lax.all_to_all(
+        line, HEAD, 0, 0, axis_index_groups=[ORDER], tiled=True
+    )
     d_prompt, d_prompt_rope, d_resp, d_resp_rope_t = call(
         last_kernel,
         [

time: 91.8 us -> 91.2 us (level)
    all_to_all x3 -> x2, waiting for transfers between devices: 20.7 us -> 5.67 us  [spread(): return lax.all_to_all(parts, axes, 0, 0, tiled=True)]
    all_to_all x0 -> x1, waiting for transfers between devices: none -> 14.5 us  [body(): lax.all_to_all(line, HEAD, 0, 0, axis_index_groups=[ORDER], tiled=True)]
    all_to_all x0 -> x1, starting transfers between devices: none -> 6.9 us  [body(): lax.all_to_all(line, HEAD, 0, 0, axis_index_groups=[ORDER], tiled=True)]
    all_to_all x3 -> x2, starting transfers between devices: 21.4 us -> 14.6 us  [spread(): return lax.all_to_all(parts, axes, 0, 0, tiled=True)]
where the time goes in v8:
time: 91.2 us; the launch traced here: 90.5 us
  starting transfers between devices  45.1 us (49%)
  waiting for transfers between devices  27.6 us (30%)
  Pallas kernels  13.2 us (14%)
  local copies, waits for them, and re-layouts  1.99 us (2%)
  between operations  1.48 us (2%)
  other arithmetic  1.12 us (1%)
    all_to_all x2, starting transfers between devices, spread(): return lax.all_to_all(parts, axes, 0, 0, tiled=True)  14.6 us
    all_to_all x1, waiting for transfers between devices, body(): lax.all_to_all(line, HEAD, 0, 0, axis_index_groups=[ORDER], tiled=True)  14.5 us
    pallas_call x11, Pallas kernels, call(): pl.pallas_call(kernel, out_shape=[jax.ShapeDtypeStruct(shape, kind) for s...  13.2 us
    ppermute x1, starting transfers between devices, body(): lax.ppermute(send_resp, 'z', [(i, (i + 2 * (i & 1) - 1) % 8) for i in ran...  10.6 us
    all_to_all x1, starting transfers between devices, body(): lax.all_to_all(line, HEAD, 0, 0, axis_index_groups=[ORDER], tiled=True)  6.9 us
    all_to_all x2, waiting for transfers between devices, spread(): return lax.all_to_all(parts, axes, 0, 0, tiled=True)  5.67 us
    ppermute x1, starting transfers between devices, body(): got_resp = lax.ppermute(send_resp, 'xh', swap)  4.63 us
    ppermute x1, starting transfers between devices, body(): got_resp = lax.ppermute(send_resp, 'z', [(i, i ^ 1) for i in range(8)])  4.26 us
  transfers between devices with their start and end apart: 8, of which 7 were waited for; matrix products, arithmetic and copies ran while one was open for 0% of the time, Pallas kernels for 7%

profile of v8, /device:TPU:16, one launch (start us, length us, event | category | flops | bytes accessed | tf_op | source)
XLA Modules:
  0.0 90.5 jit_solution(13618805185576216532)
XLA Ops:
  0.6 1.6 %shard_map.162 = bf16[16,72,128]{2,1,0:T(8,128)(2,1)} custom-call(bf16[16,512]{1,0:T(8,128)(2,1)} %latent_far.1, bf16[16,64]{1,0:T(8,128)(2,1)} %bitcast.6), custom_call_target="tpu_custom_call" | custom-call | tf_op jit(solution)/shard_map/pallas_call | solution.py:298
  2.3 9.2 %all-to-all-start = ((bf16[16,72,128]{2,1,0:T(8,128)(2,1)}), bf16[16,72,128]{2,1,0:T(8,128)(2,1)S(1)}, u32[]{:S(2)}, u32[]{:S(2)}) async-start(bf16[16,72,128]{2,1,0:T(8,128)(2,1)} %shard_map.162), calls=%async_computation | async-start | bytes 589824 | tf_op jit(solution)/shard_map/all_to_all | solution.py:310
  12.2 1.0 %copy-done.1 = bf16[512,512]{1,0:T(8,128)(2,1)S(1)} copy-done((bf16[512,512]{1,0:T(8,128)(2,1)S(1)}, bf16[512,512]{1,0:T(8,128)(2,1)}, u32[]{:S(2)}) %copy-start.1) | copy-done | bytes 524312
  13.3 0.8 copy-done.6
  14.1 1.0 %shard_map.161 = (bf16[512,640]{1,0:T(8,128)(2,1)S(1)}, bf16[512,512]{1,0:T(8,128)(2,1)S(1)}, bf16[128,512]{1,0:T(8,128)(2,1)S(1)}, bf16[128,640]{1,0:T(8,128)(2,1)S(1)}) custom-call(s32[5]{0:T(128)S(1)} %stack.19.where, bf16[128,512]{1,0:T(8,128)(2,1)S(1)} %copy-done.5, bf16[128,256]{1,0:T(8,128)(2,1)S(1)} %copy-done.6, bf16[128,512]{1,0:T(8,128)(2,1)S(1)} %copy-done.3, ...), custom_call_target="tpu_custom_call" | custom-call | flops 4000000000 | tf_op jit(solution)/shard_map/pallas_call | solution.py:298
  15.1 5.7 %all-to-all-done.own = bf16[16,72,128]{2,1,0:T(8,128)(2,1)S(1)} async-done(((bf16[16,72,128]{2,1,0:T(8,128)(2,1)}), bf16[16,72,128]{2,1,0:T(8,128)(2,1)S(1)}, u32[]{:S(2)}, u32[]{:S(2)}) %all-to-all-start) | async-done | bytes 294944 | tf_op jit(solution)/shard_map/all_to_all | solution.py:310
  20.8 1.9 %collective-permute-start = (bf16[16,72,128]{2,1,0:T(8,128)(2,1)S(1)}, bf16[16,72,128]{2,1,0:T(8,128)(2,1)S(1)}, u32[]{:S(2)}, u32[]{:S(2)}) collective-permute-start(bf16[16,72,128]{2,1,0:T(8,128)(2,1)S(1)} %all-to-all-done.own), channel_id=1, source_target_pairs={{0,16},{16,0},{1,17},{17,1},{2,18},{18,2},{3,19},{19,3},{4,20},{20... | collective-permute-start | bytes 884744 | tf_op jit(solution)/shard_map/ppermute | solution.py:363
  22.7 1.4 %shard_map.163 = (f32[384,512]{1,0:T(8,128)S(1)}, f32[384,512]{1,0:T(8,128)S(1)}, bf16[256,640]{1,0:T(8,128)(2,1)S(1)}) custom-call(s32[5]{0:T(128)S(1)} %stack.19.where, bf16[512,640]{1,0:T(8,128)(2,1)S(1)} %get-tuple-element.39.query, bf16[512,512]{1,0:T(8,128)(2,1)S(1)} %get-tuple-element.40.d_out, bf16[16,72,128]{2,1,0:T(8,128)(2,1)S(1)} %all-to-all-done.own, ...), custom_call_target="tpu_custom_call" | custom-call | flops 2000000000 | tf_op jit(solution)/shard_map/pallas_call | solution.py:298
  24.2 3.3 %shard_map.164 = (bf16[640,512]{1,0:T(8,128)(2,1)S(1)}, bf16[640,512]{1,0:T(8,128)(2,1)S(1)}, bf16[640,512]{1,0:T(8,128)(2,1)S(1)}, bf16[512,512]{1,0:T(8,128)(2,1)S(1)}, bf16[16,200,128]{2,1,0:T(8,128)(2,1)S(1)}) custom-call(s32[5]{0:T(128)S(1)} %stack.19.where, bf16[128,512]{1,0:T(8,128)(2,1)S(1)} %copy-done.5, ...), custom_call_target="tpu_custom_call" | custom-call | flops 4000000000 | tf_op jit(solution)/shard_map/pallas_call | solution.py:298
  27.5 2.3 %collective-permute-start.1 = (bf16[16,200,128]{2,1,0:T(8,128)(2,1)S(1)}, bf16[16,200,128]{2,1,0:T(8,128)(2,1)S(1)}, u32[]{:S(2)}, u32[]{:S(2)}) collective-permute-start(bf16[16,200,128]{2,1,0:T(8,128)(2,1)S(1)} %get-tuple-element.53), channel_id=1, source_target_pairs={{0,16},{16,0},{1,17},{17,1},{2,18},{18,2},{3,19},{19,3},{4,20},{20... | collective-permute-start | bytes 2457608 | tf_op jit(solution)/shard_map/ppermute | solution.py:418
  29.8 1.4 %shard_map.166 = (bf16[16,200,128]{2,1,0:T(8,128)(2,1)S(1)}, bf16[4,72,128]{2,1,0:T(8,128)(2,1)S(1)}, bf16[4,72,128]{2,1,0:T(8,128)(2,1)S(1)}) custom-call(s32[5]{0:T(128)S(1)} %stack.19.where, bf16[128,512]{1,0:T(8,128)(2,1)S(1)} %copy-done.5, bf16[128,512]{1,0:T(8,128)(2,1)S(1)} %get-tuple-element.37.masked, bf16[512,640]{1,0:T(8,128)(2,1)S(1)} %get-tuple-element.39.query, ...), custom_call_target="tpu_custom_call" | custom-call | flops 2000000000 | tf_op jit(solution)/shard_map/pallas_call | solution.py:298
  31.8 1.1 %add.7 = bf16[16,200,128]{2,1,0:T(8,128)(2,1)} add(bf16[16,200,128]{2,1,0:T(8,128)(2,1)S(1)} %get-tuple-element.52, bf16[16,200,128]{2,1,0:T(8,128)(2,1)S(1)} %collective-permute-done.1) | non-fusion elementwise | flops 409600 | bytes 2457600 | tf_op jit(solution)/shard_map/add | solution.py:418
  32.9 5.4 %all-to-all-start.1 = ((bf16[16,200,128]{2,1,0:T(8,128)(2,1)}), bf16[16,200,128]{2,1,0:T(8,128)(2,1)S(1)}, u32[]{:S(2)}, u32[]{:S(2)}) async-start(bf16[16,200,128]{2,1,0:T(8,128)(2,1)} %add.7), calls=%async_computation.1 | async-start | bytes 1638400 | tf_op jit(solution)/shard_map/all_to_all | solution.py:310
  38.3 4.3 %collective-permute-start.2 = (bf16[4,72,128]{2,1,0:T(8,128)(2,1)S(1)}, bf16[4,72,128]{2,1,0:T(8,128)(2,1)S(1)}, u32[]{:S(2)}, u32[]{:S(2)}) collective-permute-start(bf16[4,72,128]{2,1,0:T(8,128)(2,1)S(1)} %get-tuple-element.57), channel_id=1, source_target_pairs={{0,2},{2,0},{4,6},{6,4},{8,10},{10,8},{12,14},{14,12},{1,3},{3,1},... | collective-permute-start | bytes 221192 | tf_op jit(solution)/shard_map/ppermute | solution.py:417
  42.5 2.3 %collective-permute-done.2.received = bf16[4,72,128]{2,1,0:T(8,128)(2,1)S(1)} collective-permute-done((bf16[4,72,128]{2,1,0:T(8,128)(2,1)S(1)}, bf16[4,72,128]{2,1,0:T(8,128)(2,1)S(1)}, u32[]{:S(2)}, u32[]{:S(2)}) %collective-permute-start.2) | collective-permute-done | bytes 73760 | tf_op jit(solution)/shard_map/ppermute | solution.py:417
  45.4 10.6 %collective-permute-start.3 = (bf16[2,72,128]{2,1,0:T(8,128)(2,1)S(1)}, bf16[2,72,128]{2,1,0:T(8,128)(2,1)S(1)}, u32[]{:S(2)}, u32[]{:S(2)}) collective-permute-start(bf16[2,72,128]{2,1,0:T(8,128)(2,1)S(1)} %get-tuple-element.59), channel_id=1, source_target_pairs={{0,14},{2,4},{4,2},{6,8},{8,6},{10,12},{12,10},{14,0},{1,15},{3,5}... | collective-permute-start | bytes 110600 | tf_op jit(solution)/shard_map/ppermute | solution.py:435
  56.0 1.9 %collective-permute-done.3.received = bf16[2,72,128]{2,1,0:T(8,128)(2,1)S(1)} collective-permute-done((bf16[2,72,128]{2,1,0:T(8,128)(2,1)S(1)}, bf16[2,72,128]{2,1,0:T(8,128)(2,1)S(1)}, u32[]{:S(2)}, u32[]{:S(2)}) %collective-permute-start.3) | collective-permute-done | bytes 36896 | tf_op jit(solution)/shard_map/ppermute | solution.py:435
  58.5 4.6 %collective-permute-start.4 = (bf16[1,72,128]{2,1,0:T(8,128)(2,1)S(1)}, bf16[1,72,128]{2,1,0:T(8,128)(2,1)S(1)}, u32[]{:S(2)}, u32[]{:S(2)}) collective-permute-start(bf16[1,72,128]{2,1,0:T(8,128)(2,1)S(1)} %get-tuple-element.61), channel_id=1, source_target_pairs={{0,1},{1,0},{2,3},{3,2},{4,5},{5,4},{6,7},{7,6},{8,9},{9,8},{10,11... | collective-permute-start | bytes 55304 | tf_op jit(solution)/shard_map/ppermute | solution.py:444
  63.2 2.5 %collective-permute-done.4.received = bf16[1,72,128]{2,1,0:T(8,128)(2,1)S(1)} collective-permute-done((bf16[1,72,128]{2,1,0:T(8,128)(2,1)S(1)}, bf16[1,72,128]{2,1,0:T(8,128)(2,1)S(1)}, u32[]{:S(2)}, u32[]{:S(2)}) %collective-permute-start.4) | collective-permute-done | bytes 18464 | tf_op jit(solution)/shard_map/ppermute | solution.py:444
  65.7 0.9 %shard_map.170 = bf16[16,144,128]{2,1,0:T(8,128)(2,1)} custom-call(bf16[16,200,128]{2,1,0:T(8,128)(2,1)S(1)} %all-to-all-done.1.sample_parts, bf16[1,72,128]{2,1,0:T(8,128)(2,1)S(1)} %get-tuple-element.60.kept, bf16[1,72,128]{2,1,0:T(8,128)(2,1)S(1)} %collective-permute-done.4.received), custom_call_target="tpu_custom_call" | custom-call | tf_op jit(solution)/shard_map/pallas_call | solution.py:298
  66.6 6.9 %all-to-all-start.2 = ((bf16[16,144,128]{2,1,0:T(8,128)(2,1)}), bf16[16,144,128]{2,1,0:T(8,128)(2,1)S(1)}, u32[]{:S(2)}, u32[]{:S(2)}) async-start(bf16[16,144,128]{2,1,0:T(8,128)(2,1)} %shard_map.170), calls=%async_computation.2 | async-start | bytes 1179648 | tf_op jit(solution)/shard_map/all_to_all | solution.py:458
  73.5 1.0 %shard_map.165 = (bf16[128,512]{1,0:T(8,128)(2,1)}, bf16[128,256]{1,0:T(8,128)(2,1)}) custom-call(bf16[640,512]{1,0:T(8,128)(2,1)S(1)} %get-tuple-element.46.d_query, bf16[512,512]{1,0:T(8,128)(2,1)S(1)} %copy-done.2), custom_call_target="tpu_custom_call" | custom-call | flops 1000000000 | tf_op jit(solution)/shard_map/pallas_call | solution.py:298
  75.2 14.5 %all-to-all-done.2.parts = bf16[16,144,128]{2,1,0:T(8,128)(2,1)S(1)} async-done(((bf16[16,144,128]{2,1,0:T(8,128)(2,1)}), bf16[16,144,128]{2,1,0:T(8,128)(2,1)S(1)}, u32[]{:S(2)}, u32[]{:S(2)}) %all-to-all-start.2) | async-done | bytes 589856 | tf_op jit(solution)/shard_map/all_to_all | solution.py:458
  89.7 0.8 shard_map.171
  (21 shorter events, 2.6 us)
Async XLA Ops:
  0.6 11.6 %copy-start = (bf16[512,512]{1,0:T(8,128)(2,1)S(1)}, bf16[512,512]{1,0:T(8,128)(2,1)}, u32[]{:S(2)}) copy-start(bf16[512,512]{1,0:T(8,128)(2,1)} %w_value.1) | copy-start | bytes 1572868
  2.2 10.0 %copy-start.3 = (bf16[128,512]{1,0:T(8,128)(2,1)S(1)}, bf16[128,512]{1,0:T(8,128)(2,1)}, u32[]{:S(2)}) copy-start(bf16[128,512]{1,0:T(8,128)(2,1)} %grad.1) | copy-start | bytes 393220
  2.2 10.0 %copy-start.4 = (bf16[128,512]{1,0:T(8,128)(2,1)S(1)}, bf16[128,512]{1,0:T(8,128)(2,1)}, u32[]{:S(2)}) copy-start(bf16[128,512]{1,0:T(8,128)(2,1)} %resp_latent.1) | copy-start | bytes 393220
  2.3 10.0 %copy-start.5 = (bf16[128,512]{1,0:T(8,128)(2,1)S(1)}, bf16[128,512]{1,0:T(8,128)(2,1)}, u32[]{:S(2)}) copy-start(bf16[128,512]{1,0:T(8,128)(2,1)} %q_nope.5) | copy-start | bytes 393220
  2.3 18.5 %all-to-all-start = ((bf16[16,72,128]{2,1,0:T(8,128)(2,1)}), bf16[16,72,128]{2,1,0:T(8,128)(2,1)S(1)}, u32[]{:S(2)}, u32[]{:S(2)}) async-start(bf16[16,72,128]{2,1,0:T(8,128)(2,1)} %shard_map.162), calls=%async_computation | async-start | bytes 589824 | tf_op jit(solution)/shard_map/all_to_all | solution.py:310
  11.4 0.8 copy-start.7
  12.2 1.0 %copy-start.1 = (bf16[512,512]{1,0:T(8,128)(2,1)S(1)}, bf16[512,512]{1,0:T(8,128)(2,1)}, u32[]{:S(2)}) copy-start(bf16[512,512]{1,0:T(8,128)(2,1)} %w_key.3) | copy-start | bytes 1572868
  13.3 0.8 copy-start.6
  20.8 3.5 %collective-permute-start = (bf16[16,72,128]{2,1,0:T(8,128)(2,1)S(1)}, bf16[16,72,128]{2,1,0:T(8,128)(2,1)S(1)}, u32[]{:S(2)}, u32[]{:S(2)}) collective-permute-start(bf16[16,72,128]{2,1,0:T(8,128)(2,1)S(1)} %all-to-all-done.own), channel_id=1, source_target_pairs={{0,16},{16,0},{1,17},{17,1},{2,18},{18,2},{3,19},{19,3},{4,20},{20... | collective-permute-start | bytes 884744 | tf_op jit(solution)/shard_map/ppermute | solution.py:363
  27.5 4.2 %collective-permute-start.1 = (bf16[16,200,128]{2,1,0:T(8,128)(2,1)S(1)}, bf16[16,200,128]{2,1,0:T(8,128)(2,1)S(1)}, u32[]{:S(2)}, u32[]{:S(2)}) collective-permute-start(bf16[16,200,128]{2,1,0:T(8,128)(2,1)S(1)} %get-tuple-element.53), channel_id=1, source_target_pairs={{0,16},{16,0},{1,17},{17,1},{2,18},{18,2},{3,19},{19,3},{4,20},{20... | collective-permute-start | bytes 2457608 | tf_op jit(solution)/shard_map/ppermute | solution.py:418
  32.9 32.8 %all-to-all-start.1 = ((bf16[16,200,128]{2,1,0:T(8,128)(2,1)}), bf16[16,200,128]{2,1,0:T(8,128)(2,1)S(1)}, u32[]{:S(2)}, u32[]{:S(2)}) async-start(bf16[16,200,128]{2,1,0:T(8,128)(2,1)} %add.7), calls=%async_computation.1 | async-start | bytes 1638400 | tf_op jit(solution)/shard_map/all_to_all | solution.py:310
  38.3 6.6 %collective-permute-start.2 = (bf16[4,72,128]{2,1,0:T(8,128)(2,1)S(1)}, bf16[4,72,128]{2,1,0:T(8,128)(2,1)S(1)}, u32[]{:S(2)}, u32[]{:S(2)}) collective-permute-start(bf16[4,72,128]{2,1,0:T(8,128)(2,1)S(1)} %get-tuple-element.57), channel_id=1, source_target_pairs={{0,2},{2,0},{4,6},{6,4},{8,10},{10,8},{12,14},{14,12},{1,3},{3,1},... | collective-permute-start | bytes 221192 | tf_op jit(solution)/shard_map/ppermute | solution.py:417
  45.4 12.5 %collective-permute-start.3 = (bf16[2,72,128]{2,1,0:T(8,128)(2,1)S(1)}, bf16[2,72,128]{2,1,0:T(8,128)(2,1)S(1)}, u32[]{:S(2)}, u32[]{:S(2)}) collective-permute-start(bf16[2,72,128]{2,1,0:T(8,128)(2,1)S(1)} %get-tuple-element.59), channel_id=1, source_target_pairs={{0,14},{2,4},{4,2},{6,8},{8,6},{10,12},{12,10},{14,0},{1,15},{3,5}... | collective-permute-start | bytes 110600 | tf_op jit(solution)/shard_map/ppermute | solution.py:435
  58.5 7.2 %collective-permute-start.4 = (bf16[1,72,128]{2,1,0:T(8,128)(2,1)S(1)}, bf16[1,72,128]{2,1,0:T(8,128)(2,1)S(1)}, u32[]{:S(2)}, u32[]{:S(2)}) collective-permute-start(bf16[1,72,128]{2,1,0:T(8,128)(2,1)S(1)} %get-tuple-element.61), channel_id=1, source_target_pairs={{0,1},{1,0},{2,3},{3,2},{4,5},{5,4},{6,7},{7,6},{8,9},{9,8},{10,11... | collective-permute-start | bytes 55304 | tf_op jit(solution)/shard_map/ppermute | solution.py:444
  66.6 6.9 %copy-start.2 = (bf16[512,512]{1,0:T(8,128)(2,1)S(1)}, bf16[512,512]{1,0:T(8,128)(2,1)}, u32[]{:S(2)}) copy-start(bf16[512,512]{1,0:T(8,128)(2,1)} %w_key.3) | copy-start | bytes 1572868
  66.6 23.1 %all-to-all-start.2 = ((bf16[16,144,128]{2,1,0:T(8,128)(2,1)}), bf16[16,144,128]{2,1,0:T(8,128)(2,1)S(1)}, u32[]{:S(2)}, u32[]{:S(2)}) async-start(bf16[16,144,128]{2,1,0:T(8,128)(2,1)} %shard_map.170), calls=%async_computation.2 | async-start | bytes 1179648 | tf_op jit(solution)/shard_map/all_to_all | solution.py:458

commit v9 on v8

--- a/solution.py
+++ b/solution.py
@@ -116,7 +116,6 @@
 
 
 def attention_kernel(
-    where,
     q_nope,
     masked,
     query,
@@ -160,7 +159,7 @@
     d_query[...] = dot(keys[...], d_scores, 0, 0).astype(BF16)
     out_latent[...] = dot(keys[:, 0:DC], attention_b, 0, 0).astype(BF16)
     half_grads(
-        1 - where[1],
+        1 - lax.axis_index("c"),
         HALF,
         q_nope,
         masked,
@@ -238,9 +237,9 @@
     d_q_rope[...] = d_rope.astype(BF16)
 
 
-def halve_kernel(bit, where, kept, received, keep, send):
+def halve_kernel(bit, kept, received, keep, send):
     half = keep.shape[0]
-    place = where[bit]
+    place = lax.axis_index("xh") if bit else 1 - (lax.axis_index("z") & 1)
     mine = pl.ds(place * half, half)
     theirs = pl.ds((1 - place) * half, half)
     keep[...] = (kept[mine].astype(F32) + received[mine].astype(F32)).astype(BF16)
@@ -381,7 +380,6 @@
             ((DC, ROWS), BF16),
             ((CHIPS, WIDE, 128), BF16),
         ],
-        where,
         q_nope,
         masked,
         query,
@@ -391,7 +389,6 @@
         resp_keys,
         first_scores,
         first_d_attention,
-        scalars=1,
         flops=4_000_000_000,
         scratch=[pltpu.VMEM((KEYS, EXT), BF16)],
     )
@@ -425,21 +422,17 @@
         flops=1_000_000_000,
     )
     keep_resp, send_resp = call(
-        functools.partial(halve_kernel, 3),
+        functools.partial(halve_kernel, 0),
         [((2, PACKED, 128), BF16)] * 2,
-        where,
         keep_resp,
         got_resp,
-        scalars=1,
     )
     got_resp = lax.ppermute(send_resp, "z", [(i, (i + 2 * (i & 1) - 1) % 8) for i in range(8)])
     keep_resp, send_resp = call(
-        functools.partial(halve_kernel, 4),
+        functools.partial(halve_kernel, 1),
         [((1, PACKED, 128), BF16)] * 2,
-        where,
         keep_resp,
         got_resp,
-        scalars=1,
     )
     got_resp = lax.ppermute(send_resp, "xh", swap)
     (line,) = call(

time: 91.2 us -> 91 us (level)
  Pallas kernels: 13.2 us -> 11.5 us
  waiting for transfers between devices: 27.6 us -> 29.1 us
    pallas_call x11, Pallas kernels: 13.2 us -> 11.5 us  [call(): pl.pallas_call(kernel, out_shape=[jax.ShapeDtypeStruct(shape, kind) for s...]
    all_to_all x1, waiting for transfers between devices: 14.5 us -> 16 us  [body(): lax.all_to_all(line, HEAD, 0, 0, axis_index_groups=[ORDER], tiled=True)]
  transfers between devices with their start and end apart: 8 -> 8, of which waited for: 7 -> 7; matrix products, arithmetic and copies ran while one was open for 0% -> 0% of each run, Pallas kernels for 7% -> 6%
where the time goes in v9:
time: 91 us; the launch traced here: 90.3 us
  starting transfers between devices  45.1 us (50%)
  waiting for transfers between devices  29.1 us (32%)
  Pallas kernels  11.5 us (13%)
  local copies, waits for them, and re-layouts  1.99 us (2%)
  between operations  1.47 us (2%)
  other arithmetic  1.12 us (1%)
    all_to_all x1, waiting for transfers between devices, body(): lax.all_to_all(line, HEAD, 0, 0, axis_index_groups=[ORDER], tiled=True)  16 us
    all_to_all x2, starting transfers between devices, spread(): return lax.all_to_all(parts, axes, 0, 0, tiled=True)  14.5 us
    pallas_call x11, Pallas kernels, call(): pl.pallas_call(kernel, out_shape=[jax.ShapeDtypeStruct(shape, kind) for s...  11.5 us
    ppermute x1, starting transfers between devices, body(): lax.ppermute(send_resp, 'z', [(i, (i + 2 * (i & 1) - 1) % 8) for i in ran...  10.6 us
    all_to_all x1, starting transfers between devices, body(): lax.all_to_all(line, HEAD, 0, 0, axis_index_groups=[ORDER], tiled=True)  6.9 us
    all_to_all x2, waiting for transfers between devices, spread(): return lax.all_to_all(parts, axes, 0, 0, tiled=True)  5.67 us
    ppermute x1, starting transfers between devices, body(): got_resp = lax.ppermute(send_resp, 'xh', swap)  4.64 us
    ppermute x1, starting transfers between devices, body(): got_resp = lax.ppermute(send_resp, 'z', [(i, i ^ 1) for i in range(8)])  4.27 us
  transfers between devices with their start and end apart: 8, of which 7 were waited for; matrix products, arithmetic and copies ran while one was open for 0% of the time, Pallas kernels for 6%

profile of v9, /device:TPU:16, one launch (start us, length us, event | category | flops | bytes accessed | tf_op | source)
XLA Modules:
  0.0 90.3 jit_solution(10808417382498029066)
XLA Ops:
  0.6 1.6 %shard_map.162 = bf16[16,72,128]{2,1,0:T(8,128)(2,1)} custom-call(bf16[16,512]{1,0:T(8,128)(2,1)} %latent_far.1, bf16[16,64]{1,0:T(8,128)(2,1)} %bitcast.6), custom_call_target="tpu_custom_call" | custom-call | tf_op jit(solution)/shard_map/pallas_call | solution.py:297
  2.3 9.2 %all-to-all-start = ((bf16[16,72,128]{2,1,0:T(8,128)(2,1)}), bf16[16,72,128]{2,1,0:T(8,128)(2,1)S(1)}, u32[]{:S(2)}, u32[]{:S(2)}) async-start(bf16[16,72,128]{2,1,0:T(8,128)(2,1)} %shard_map.162), calls=%async_computation | async-start | bytes 589824 | tf_op jit(solution)/shard_map/all_to_all | solution.py:309
  12.2 1.0 %copy-done.1 = bf16[512,512]{1,0:T(8,128)(2,1)S(1)} copy-done((bf16[512,512]{1,0:T(8,128)(2,1)S(1)}, bf16[512,512]{1,0:T(8,128)(2,1)}, u32[]{:S(2)}) %copy-start.1) | copy-done | bytes 524312
  13.3 0.8 copy-done.6
  14.1 1.0 %shard_map.161 = (bf16[512,640]{1,0:T(8,128)(2,1)S(1)}, bf16[512,512]{1,0:T(8,128)(2,1)S(1)}, bf16[128,512]{1,0:T(8,128)(2,1)S(1)}, bf16[128,640]{1,0:T(8,128)(2,1)S(1)}) custom-call(s32[5]{0:T(128)S(1)} %stack.19.where, bf16[128,512]{1,0:T(8,128)(2,1)S(1)} %copy-done.5, bf16[128,256]{1,0:T(8,128)(2,1)S(1)} %copy-done.6, bf16[128,512]{1,0:T(8,128)(2,1)S(1)} %copy-done.3, ...), custom_call_target="tpu_custom_call" | custom-call | flops 4000000000 | tf_op jit(solution)/shard_map/pallas_call | solution.py:297
  15.1 5.7 %all-to-all-done.own = bf16[16,72,128]{2,1,0:T(8,128)(2,1)S(1)} async-done(((bf16[16,72,128]{2,1,0:T(8,128)(2,1)}), bf16[16,72,128]{2,1,0:T(8,128)(2,1)S(1)}, u32[]{:S(2)}, u32[]{:S(2)}) %all-to-all-start) | async-done | bytes 294944 | tf_op jit(solution)/shard_map/all_to_all | solution.py:309
  20.8 1.9 %collective-permute-start = (bf16[16,72,128]{2,1,0:T(8,128)(2,1)S(1)}, bf16[16,72,128]{2,1,0:T(8,128)(2,1)S(1)}, u32[]{:S(2)}, u32[]{:S(2)}) collective-permute-start(bf16[16,72,128]{2,1,0:T(8,128)(2,1)S(1)} %all-to-all-done.own), channel_id=1, source_target_pairs={{0,16},{16,0},{1,17},{17,1},{2,18},{18,2},{3,19},{19,3},{4,20},{20... | collective-permute-start | bytes 884744 | tf_op jit(solution)/shard_map/ppermute | solution.py:362
  22.7 1.4 %shard_map.163 = (f32[384,512]{1,0:T(8,128)S(1)}, f32[384,512]{1,0:T(8,128)S(1)}, bf16[256,640]{1,0:T(8,128)(2,1)S(1)}) custom-call(s32[5]{0:T(128)S(1)} %stack.19.where, bf16[512,640]{1,0:T(8,128)(2,1)S(1)} %get-tuple-element.39.query, bf16[512,512]{1,0:T(8,128)(2,1)S(1)} %get-tuple-element.40.d_out, bf16[16,72,128]{2,1,0:T(8,128)(2,1)S(1)} %all-to-all-done.own, ...), custom_call_target="tpu_custom_call" | custom-call | flops 2000000000 | tf_op jit(solution)/shard_map/pallas_call | solution.py:297
  24.2 2.7 %shard_map.164 = (bf16[640,512]{1,0:T(8,128)(2,1)S(1)}, bf16[640,512]{1,0:T(8,128)(2,1)S(1)}, bf16[640,512]{1,0:T(8,128)(2,1)S(1)}, bf16[512,512]{1,0:T(8,128)(2,1)S(1)}, bf16[16,200,128]{2,1,0:T(8,128)(2,1)S(1)}) custom-call(bf16[128,512]{1,0:T(8,128)(2,1)S(1)} %copy-done.5, bf16[128,512]{1,0:T(8,128)(2,1)S(1)} %get-tuple-element.37.masked, ...), custom_call_target="tpu_custom_call" | custom-call | flops 4000000000 | tf_op jit(solution)/shard_map/pallas_call | solution.py:297
  26.9 2.3 %collective-permute-start.1 = (bf16[16,200,128]{2,1,0:T(8,128)(2,1)S(1)}, bf16[16,200,128]{2,1,0:T(8,128)(2,1)S(1)}, u32[]{:S(2)}, u32[]{:S(2)}) collective-permute-start(bf16[16,200,128]{2,1,0:T(8,128)(2,1)S(1)} %get-tuple-element.53), channel_id=1, source_target_pairs={{0,16},{16,0},{1,17},{17,1},{2,18},{18,2},{3,19},{19,3},{4,20},{20... | collective-permute-start | bytes 2457608 | tf_op jit(solution)/shard_map/ppermute | solution.py:415
  29.2 1.4 %shard_map.166 = (bf16[16,200,128]{2,1,0:T(8,128)(2,1)S(1)}, bf16[4,72,128]{2,1,0:T(8,128)(2,1)S(1)}, bf16[4,72,128]{2,1,0:T(8,128)(2,1)S(1)}) custom-call(s32[5]{0:T(128)S(1)} %stack.19.where, bf16[128,512]{1,0:T(8,128)(2,1)S(1)} %copy-done.5, bf16[128,512]{1,0:T(8,128)(2,1)S(1)} %get-tuple-element.37.masked, bf16[512,640]{1,0:T(8,128)(2,1)S(1)} %get-tuple-element.39.query, ...), custom_call_target="tpu_custom_call" | custom-call | flops 2000000000 | tf_op jit(solution)/shard_map/pallas_call | solution.py:297
  31.2 1.1 %add.7 = bf16[16,200,128]{2,1,0:T(8,128)(2,1)} add(bf16[16,200,128]{2,1,0:T(8,128)(2,1)S(1)} %get-tuple-element.52, bf16[16,200,128]{2,1,0:T(8,128)(2,1)S(1)} %collective-permute-done.1) | non-fusion elementwise | flops 409600 | bytes 2457600 | tf_op jit(solution)/shard_map/add | solution.py:415
  32.3 5.4 %all-to-all-start.1 = ((bf16[16,200,128]{2,1,0:T(8,128)(2,1)}), bf16[16,200,128]{2,1,0:T(8,128)(2,1)S(1)}, u32[]{:S(2)}, u32[]{:S(2)}) async-start(bf16[16,200,128]{2,1,0:T(8,128)(2,1)} %add.7), calls=%async_computation.1 | async-start | bytes 1638400 | tf_op jit(solution)/shard_map/all_to_all | solution.py:309
  37.7 4.3 %collective-permute-start.2 = (bf16[4,72,128]{2,1,0:T(8,128)(2,1)S(1)}, bf16[4,72,128]{2,1,0:T(8,128)(2,1)S(1)}, u32[]{:S(2)}, u32[]{:S(2)}) collective-permute-start(bf16[4,72,128]{2,1,0:T(8,128)(2,1)S(1)} %get-tuple-element.57), channel_id=1, source_target_pairs={{0,2},{2,0},{4,6},{6,4},{8,10},{10,8},{12,14},{14,12},{1,3},{3,1},... | collective-permute-start | bytes 221192 | tf_op jit(solution)/shard_map/ppermute | solution.py:414
  41.9 2.3 %collective-permute-done.2.received = bf16[4,72,128]{2,1,0:T(8,128)(2,1)S(1)} collective-permute-done((bf16[4,72,128]{2,1,0:T(8,128)(2,1)S(1)}, bf16[4,72,128]{2,1,0:T(8,128)(2,1)S(1)}, u32[]{:S(2)}, u32[]{:S(2)}) %collective-permute-start.2) | collective-permute-done | bytes 73760 | tf_op jit(solution)/shard_map/ppermute | solution.py:414
  44.3 10.6 %collective-permute-start.3 = (bf16[2,72,128]{2,1,0:T(8,128)(2,1)S(1)}, bf16[2,72,128]{2,1,0:T(8,128)(2,1)S(1)}, u32[]{:S(2)}, u32[]{:S(2)}) collective-permute-start(bf16[2,72,128]{2,1,0:T(8,128)(2,1)S(1)} %get-tuple-element.59), channel_id=1, source_target_pairs={{0,14},{2,4},{4,2},{6,8},{8,6},{10,12},{12,10},{14,0},{1,15},{3,5}... | collective-permute-start | bytes 110600 | tf_op jit(solution)/shard_map/ppermute | solution.py:430
  54.9 1.9 %collective-permute-done.3.received = bf16[2,72,128]{2,1,0:T(8,128)(2,1)S(1)} collective-permute-done((bf16[2,72,128]{2,1,0:T(8,128)(2,1)S(1)}, bf16[2,72,128]{2,1,0:T(8,128)(2,1)S(1)}, u32[]{:S(2)}, u32[]{:S(2)}) %collective-permute-start.3) | collective-permute-done | bytes 36896 | tf_op jit(solution)/shard_map/ppermute | solution.py:430
  56.8 4.6 %collective-permute-start.4 = (bf16[1,72,128]{2,1,0:T(8,128)(2,1)S(1)}, bf16[1,72,128]{2,1,0:T(8,128)(2,1)S(1)}, u32[]{:S(2)}, u32[]{:S(2)}) collective-permute-start(bf16[1,72,128]{2,1,0:T(8,128)(2,1)S(1)} %get-tuple-element.61), channel_id=1, source_target_pairs={{0,1},{1,0},{2,3},{3,2},{4,5},{5,4},{6,7},{7,6},{8,9},{9,8},{10,11... | collective-permute-start | bytes 55304 | tf_op jit(solution)/shard_map/ppermute | solution.py:437
  61.5 2.5 %collective-permute-done.4.received = bf16[1,72,128]{2,1,0:T(8,128)(2,1)S(1)} collective-permute-done((bf16[1,72,128]{2,1,0:T(8,128)(2,1)S(1)}, bf16[1,72,128]{2,1,0:T(8,128)(2,1)S(1)}, u32[]{:S(2)}, u32[]{:S(2)}) %collective-permute-start.4) | collective-permute-done | bytes 18464 | tf_op jit(solution)/shard_map/ppermute | solution.py:437
  64.0 0.9 %shard_map.170 = bf16[16,144,128]{2,1,0:T(8,128)(2,1)} custom-call(bf16[16,200,128]{2,1,0:T(8,128)(2,1)S(1)} %all-to-all-done.1.sample_parts, bf16[1,72,128]{2,1,0:T(8,128)(2,1)S(1)} %get-tuple-element.60.kept, bf16[1,72,128]{2,1,0:T(8,128)(2,1)S(1)} %collective-permute-done.4.received), custom_call_target="tpu_custom_call" | custom-call | tf_op jit(solution)/shard_map/pallas_call | solution.py:297
  64.9 6.9 %all-to-all-start.2 = ((bf16[16,144,128]{2,1,0:T(8,128)(2,1)}), bf16[16,144,128]{2,1,0:T(8,128)(2,1)S(1)}, u32[]{:S(2)}, u32[]{:S(2)}) async-start(bf16[16,144,128]{2,1,0:T(8,128)(2,1)} %shard_map.170), calls=%async_computation.2 | async-start | bytes 1179648 | tf_op jit(solution)/shard_map/all_to_all | solution.py:451
  71.8 1.0 %shard_map.165 = (bf16[128,512]{1,0:T(8,128)(2,1)}, bf16[128,256]{1,0:T(8,128)(2,1)}) custom-call(bf16[640,512]{1,0:T(8,128)(2,1)S(1)} %get-tuple-element.46.d_query, bf16[512,512]{1,0:T(8,128)(2,1)S(1)} %copy-done.2), custom_call_target="tpu_custom_call" | custom-call | flops 1000000000 | tf_op jit(solution)/shard_map/pallas_call | solution.py:297
  73.5 16.0 %all-to-all-done.2.parts = bf16[16,144,128]{2,1,0:T(8,128)(2,1)S(1)} async-done(((bf16[16,144,128]{2,1,0:T(8,128)(2,1)}), bf16[16,144,128]{2,1,0:T(8,128)(2,1)S(1)}, u32[]{:S(2)}, u32[]{:S(2)}) %all-to-all-start.2) | async-done | bytes 589856 | tf_op jit(solution)/shard_map/all_to_all | solution.py:451
  89.5 0.8 shard_map.171
  (21 shorter events, 1.5 us)
Async XLA Ops:
  0.6 11.6 %copy-start = (bf16[512,512]{1,0:T(8,128)(2,1)S(1)}, bf16[512,512]{1,0:T(8,128)(2,1)}, u32[]{:S(2)}) copy-start(bf16[512,512]{1,0:T(8,128)(2,1)} %w_value.1) | copy-start | bytes 1572868
  2.2 10.0 %copy-start.3 = (bf16[128,512]{1,0:T(8,128)(2,1)S(1)}, bf16[128,512]{1,0:T(8,128)(2,1)}, u32[]{:S(2)}) copy-start(bf16[128,512]{1,0:T(8,128)(2,1)} %grad.1) | copy-start | bytes 393220
  2.2 10.0 %copy-start.4 = (bf16[128,512]{1,0:T(8,128)(2,1)S(1)}, bf16[128,512]{1,0:T(8,128)(2,1)}, u32[]{:S(2)}) copy-start(bf16[128,512]{1,0:T(8,128)(2,1)} %resp_latent.1) | copy-start | bytes 393220
  2.3 10.0 %copy-start.5 = (bf16[128,512]{1,0:T(8,128)(2,1)S(1)}, bf16[128,512]{1,0:T(8,128)(2,1)}, u32[]{:S(2)}) copy-start(bf16[128,512]{1,0:T(8,128)(2,1)} %q_nope.5) | copy-start | bytes 393220
  2.3 18.5 %all-to-all-start = ((bf16[16,72,128]{2,1,0:T(8,128)(2,1)}), bf16[16,72,128]{2,1,0:T(8,128)(2,1)S(1)}, u32[]{:S(2)}, u32[]{:S(2)}) async-start(bf16[16,72,128]{2,1,0:T(8,128)(2,1)} %shard_map.162), calls=%async_computation | async-start | bytes 589824 | tf_op jit(solution)/shard_map/all_to_all | solution.py:309
  11.4 0.8 copy-start.7
  12.2 1.0 %copy-start.1 = (bf16[512,512]{1,0:T(8,128)(2,1)S(1)}, bf16[512,512]{1,0:T(8,128)(2,1)}, u32[]{:S(2)}) copy-start(bf16[512,512]{1,0:T(8,128)(2,1)} %w_key.3) | copy-start | bytes 1572868
  13.3 0.8 copy-start.6
  20.8 3.5 %collective-permute-start = (bf16[16,72,128]{2,1,0:T(8,128)(2,1)S(1)}, bf16[16,72,128]{2,1,0:T(8,128)(2,1)S(1)}, u32[]{:S(2)}, u32[]{:S(2)}) collective-permute-start(bf16[16,72,128]{2,1,0:T(8,128)(2,1)S(1)} %all-to-all-done.own), channel_id=1, source_target_pairs={{0,16},{16,0},{1,17},{17,1},{2,18},{18,2},{3,19},{19,3},{4,20},{20... | collective-permute-start | bytes 884744 | tf_op jit(solution)/shard_map/ppermute | solution.py:362
  26.9 4.2 %collective-permute-start.1 = (bf16[16,200,128]{2,1,0:T(8,128)(2,1)S(1)}, bf16[16,200,128]{2,1,0:T(8,128)(2,1)S(1)}, u32[]{:S(2)}, u32[]{:S(2)}) collective-permute-start(bf16[16,200,128]{2,1,0:T(8,128)(2,1)S(1)} %get-tuple-element.53), channel_id=1, source_target_pairs={{0,16},{16,0},{1,17},{17,1},{2,18},{18,2},{3,19},{19,3},{4,20},{20... | collective-permute-start | bytes 2457608 | tf_op jit(solution)/shard_map/ppermute | solution.py:415
  32.3 31.7 %all-to-all-start.1 = ((bf16[16,200,128]{2,1,0:T(8,128)(2,1)}), bf16[16,200,128]{2,1,0:T(8,128)(2,1)S(1)}, u32[]{:S(2)}, u32[]{:S(2)}) async-start(bf16[16,200,128]{2,1,0:T(8,128)(2,1)} %add.7), calls=%async_computation.1 | async-start | bytes 1638400 | tf_op jit(solution)/shard_map/all_to_all | solution.py:309
  37.7 6.6 %collective-permute-start.2 = (bf16[4,72,128]{2,1,0:T(8,128)(2,1)S(1)}, bf16[4,72,128]{2,1,0:T(8,128)(2,1)S(1)}, u32[]{:S(2)}, u32[]{:S(2)}) collective-permute-start(bf16[4,72,128]{2,1,0:T(8,128)(2,1)S(1)} %get-tuple-element.57), channel_id=1, source_target_pairs={{0,2},{2,0},{4,6},{6,4},{8,10},{10,8},{12,14},{14,12},{1,3},{3,1},... | collective-permute-start | bytes 221192 | tf_op jit(solution)/shard_map/ppermute | solution.py:414
  44.3 12.5 %collective-permute-start.3 = (bf16[2,72,128]{2,1,0:T(8,128)(2,1)S(1)}, bf16[2,72,128]{2,1,0:T(8,128)(2,1)S(1)}, u32[]{:S(2)}, u32[]{:S(2)}) collective-permute-start(bf16[2,72,128]{2,1,0:T(8,128)(2,1)S(1)} %get-tuple-element.59), channel_id=1, source_target_pairs={{0,14},{2,4},{4,2},{6,8},{8,6},{10,12},{12,10},{14,0},{1,15},{3,5}... | collective-permute-start | bytes 110600 | tf_op jit(solution)/shard_map/ppermute | solution.py:430
  56.8 7.2 %collective-permute-start.4 = (bf16[1,72,128]{2,1,0:T(8,128)(2,1)S(1)}, bf16[1,72,128]{2,1,0:T(8,128)(2,1)S(1)}, u32[]{:S(2)}, u32[]{:S(2)}) collective-permute-start(bf16[1,72,128]{2,1,0:T(8,128)(2,1)S(1)} %get-tuple-element.61), channel_id=1, source_target_pairs={{0,1},{1,0},{2,3},{3,2},{4,5},{5,4},{6,7},{7,6},{8,9},{9,8},{10,11... | collective-permute-start | bytes 55304 | tf_op jit(solution)/shard_map/ppermute | solution.py:437
  64.9 6.9 %copy-start.2 = (bf16[512,512]{1,0:T(8,128)(2,1)S(1)}, bf16[512,512]{1,0:T(8,128)(2,1)}, u32[]{:S(2)}) copy-start(bf16[512,512]{1,0:T(8,128)(2,1)} %w_key.3) | copy-start | bytes 1572868
  64.9 24.6 %all-to-all-start.2 = ((bf16[16,144,128]{2,1,0:T(8,128)(2,1)}), bf16[16,144,128]{2,1,0:T(8,128)(2,1)S(1)}, u32[]{:S(2)}, u32[]{:S(2)}) async-start(bf16[16,144,128]{2,1,0:T(8,128)(2,1)} %shard_map.170), calls=%async_computation.2 | async-start | bytes 1179648 | tf_op jit(solution)/shard_map/all_to_all | solution.py:451
